TPU v7x, 512 devices: a whole 4x4x16 slice. The times are simulated.
512 devices in a mesh: dp: 16 (over z), expert: 32 (over x, y, core).
Axes of the slice: x: 4, y: 4, z: 16, core: 2. Of those that a mesh axis runs over, the one named last changes fastest.
Arguments:
- tokens: bfloat16 [65536, 1024], P(('dp', 'expert')), may hold values from -6 to 6
- routes: int32 [65536, 8], P(('dp', 'expert')), may hold values from 0 to 63, all different within a row; in each aligned block of 128 rows (0 to 127, 128 to 255, ...) at most 24 rows name the same one
- route_gates: float32 [65536, 8], P(('dp', 'expert')), may hold values from 0.1 to 9
- route_cotangent: bfloat16 [65536, 8, 384], P(('dp', 'expert')), may hold values from -4 to 4
- gate_up: bfloat16 [1024, 64, 768], P('dp', 'expert'), may hold values from -0.1875 to 0.1875
Outputs:
- grad_tokens: bfloat16 [65536, 1024], P(('dp', 'expert'))
- grad_gate_up: bfloat16 [1024, 64, 768], P('dp', 'expert')
- load: float32 [64], P('expert')
Inputs may be any that keep to these rules, and one draw needn't show every extreme that they name: `routes`: each token names 8 different experts. Among the 128 rows of one device, no expert is named by more than 24 rows, a bound that some block reaches.
All inputs are finite; a program needn't handle non-finite values.
Results may differ from a plain program's by a relative error of at most 0.023.
Values may be sent and summed in bfloat16 or wider, within the bound.
No kernel may reach another device: no remote copies, remote signals or barrier semaphores. Data moves between devices by JAX's collectives and lax.ppermute only.
A program may use at most 64 MiB of HBM per device.

v0:
```python
import jax
import jax.numpy as jnp
from jax import lax
from jax.sharding import PartitionSpec as P


def route_slots(routes, per_device, devices, capacity):
    experts = per_device * devices
    flat_routes = routes.reshape(-1)
    table = (flat_routes[:, None] == jnp.arange(experts, dtype=jnp.int32)[None, :]).astype(
        jnp.int32
    )
    earlier = jnp.sum((jnp.cumsum(table, axis=0) - table) * table, axis=1)
    owner_device = flat_routes // per_device
    local_slot = flat_routes % per_device
    slot_index = (local_slot * devices + owner_device) * capacity + earlier
    return (slot_index, table)


def swiglu_grads(pre, cotangent, width):
    gate = pre[..., :width]
    upper = pre[..., width:]
    sigma = jax.nn.sigmoid(gate)
    scaled = cotangent.astype(jnp.float32)
    d_gate = scaled * upper * sigma * (1.0 + gate * (1.0 - sigma))
    d_upper = scaled * gate * sigma
    return jnp.concatenate([d_gate, d_upper], axis=-1).astype(jnp.bfloat16)


def body(tokens, routes, route_gates, route_cotangent, gate_up):
    tok_count, topk = routes.shape
    width = route_cotangent.shape[2]
    model = tokens.shape[1]
    per_device = gate_up.shape[1]
    devices = lax.axis_size("expert")
    data_ways = lax.axis_size("dp")
    capacity = 3 * tok_count * topk // (2 * per_device * devices)
    total_slots = per_device * devices * capacity
    slot_index, table = route_slots(routes, per_device, devices, capacity)
    gate_mark = route_gates.astype(jnp.bfloat16).reshape(-1)
    scaled = (route_gates[:, :, None] * route_cotangent.astype(jnp.float32)).astype(jnp.bfloat16)
    scaled = scaled.reshape(tok_count * topk, width)
    repeated = jnp.repeat(tokens, topk, axis=0)
    send_rows = jnp.zeros((total_slots, model), jnp.bfloat16).at[slot_index].set(repeated)
    send_rows = send_rows.reshape(per_device, devices, capacity, model)
    send_cot = jnp.zeros((total_slots, width), jnp.bfloat16).at[slot_index].set(scaled)
    send_cot = send_cot.reshape(per_device, devices, capacity, width)
    got_rows, got_cot = (
        lax.all_to_all(send_rows, "expert", split_axis=1, concat_axis=1, tiled=True),
        lax.all_to_all(send_cot, "expert", split_axis=1, concat_axis=1, tiled=True),
    )
    own_sums = jnp.sum(table.astype(jnp.float32) * gate_mark.astype(jnp.float32)[:, None], axis=0)
    everyone = lax.psum(own_sums, ("dp", "expert"))
    mine = lax.dynamic_slice_in_dim(everyone, lax.axis_index("expert") * per_device, per_device, 0)
    rows_in = got_rows.reshape(per_device, devices * capacity, model)
    cot_in = got_cot.reshape(per_device, devices * capacity, width)
    gathered = lax.all_gather(gate_up, "dp", axis=0, tiled=True)
    pre = jnp.einsum("jrd,dje->jre", rows_in, gathered, preferred_element_type=jnp.float32)
    grad_pre = swiglu_grads(pre, cot_in, width)
    route_grad = jnp.einsum(
        "jre,dje->jrd", grad_pre, gathered, preferred_element_type=jnp.float32
    ).astype(jnp.bfloat16)
    grad_weights = lax.psum_scatter(
        jnp.einsum("jrd,jre->dje", rows_in, grad_pre, preferred_element_type=jnp.float32).astype(
            jnp.bfloat16
        ),
        "dp",
        scatter_dimension=0,
        tiled=True,
    )
    returned = lax.all_to_all(
        route_grad.reshape(per_device, devices, capacity, model),
        "expert",
        split_axis=1,
        concat_axis=1,
        tiled=True,
    )
    picked = returned.reshape(total_slots, model)[slot_index].astype(jnp.float32)
    grad_tokens = jnp.sum(picked.reshape(tok_count, topk, model), axis=1).astype(jnp.bfloat16)
    load = mine * (per_device / (tok_count * topk * data_ways))
    return (grad_tokens, grad_weights, load)


def solution(mesh):
    in_specs = (
        P(("dp", "expert"), None),
        P(("dp", "expert"), None),
        P(("dp", "expert"), None),
        P(("dp", "expert"), None, None),
        P("dp", "expert", None),
    )
    out_specs = (P(("dp", "expert"), None), P("dp", "expert", None), P("expert"))
    return jax.shard_map(body, mesh=mesh, in_specs=in_specs, out_specs=out_specs, check_vma=False)
```

profile of v0, /device:TPU:6, one launch (start us, length us, event | category | flops | bytes accessed | tf_op | source)
XLA Modules:
  0.0 305.5 jit_solution(13680527470962333950)
XLA Ops:
  7.2 1.7 copy.51
  9.0 0.8 copy.41
  10.0 0.8 copy.46
  10.8 18.0 %reduce-window.6 = s32[64,8,128]{2,1,0:T(8,128)S(1)} reduce-window(s32[64,8,128]{2,1,0:T(8,128)S(1)} %fusion.16, s32[]{:T(128)} %constant.42.clone.1), window={size=1x1x128 pad=0_0x0_0x127_0}, to_apply=%region_0.0 | reduce-window | flops 8323072 | bytes 524292 | tf_op jit(solution)/shard_map/reduce-window
  29.5 5.5 %scatter_custom_fusion = bf16[1536,384]{1,0:T(8,128)(2,1)S(1)} fusion(s32[1024]{0:T(1024)S(1)} %bitcast.46, bf16[128,8,384]{2,1,0:T(8,128)(2,1)S(1)} %copy-done.5, f32[128,8]{1,0:T(8,128)S(1)} %copy.46, bf16[]{:T(256)} %constant.41.clone.1), kind=kCustom, calls=%fused_computation.20 | custom fusion | flops 1179648 | bytes 2031618 | tf_op jit(solution)/shard_map/scatter | solution.py:46
  35.1 1.2 copy.47
  36.2 10.3 %all-to-all-start = ((bf16[2,32,24,384]{3,2,0,1:T(8,128)(2,1)}), bf16[2,32,24,384]{3,2,0,1:T(8,128)(2,1)}, u32[]{:S(2)}, u32[]{:S(2)}) async-start(bf16[2,32,24,384]{3,2,0,1:T(8,128)(2,1)} %copy.47), calls=%async_computation | async-start | bytes 2359296 | tf_op jit(solution)/shard_map/all_to_all | solution.py:50
  46.5 6.3 %scatter_custom_fusion.1 = bf16[1536,1024]{1,0:T(8,128)(2,1)S(1)} fusion(s32[1024]{0:T(1024)S(1)} %bitcast.47, bf16[]{:T(256)} %constant.41.clone.1, bf16[128,1024]{1,0:T(8,128)(2,1)S(1)} %copy-done), kind=kCustom, calls=%fused_computation.13 | custom fusion | bytes 3407874 | tf_op jit(solution)/shard_map/scatter | solution.py:44
  52.9 2.1 copy.49
  55.0 8.2 %all-to-all-done = bf16[2,32,24,384]{3,2,0,1:T(8,128)(2,1)} async-done(((bf16[2,32,24,384]{3,2,0,1:T(8,128)(2,1)}), bf16[2,32,24,384]{3,2,0,1:T(8,128)(2,1)}, u32[]{:S(2)}, u32[]{:S(2)}) %all-to-all-start) | async-done | bytes 1179680 | tf_op jit(solution)/shard_map/all_to_all | solution.py:50
  63.2 5.8 %all-to-all-start.1 = ((bf16[2,32,24,1024]{3,2,0,1:T(8,128)(2,1)}), bf16[2,32,24,1024]{3,2,0,1:T(8,128)(2,1)S(1)}, u32[]{:S(2)}, u32[]{:S(2)}) async-start(bf16[2,32,24,1024]{3,2,0,1:T(8,128)(2,1)} %copy.49), calls=%async_computation.1 | async-start | bytes 6291456 | tf_op jit(solution)/shard_map/all_to_all | solution.py:49
  69.0 1.4 copy.48
  70.4 1.7 bitcast_convert_fusion
  72.1 3.1 %copy.52 = f32[2,768,384]{1,2,0:T(8,128)} copy(f32[2,768,384]{2,1,0:T(8,128)} %bitcast_convert_fusion) | data formatting | bytes 4718592 | tf_op jit(solution)/shard_map/convert_element_type | solution.py:24
  75.2 32.3 %all-to-all-done.1 = bf16[2,32,24,1024]{3,2,0,1:T(8,128)(2,1)S(1)} async-done(((bf16[2,32,24,1024]{3,2,0,1:T(8,128)(2,1)}), bf16[2,32,24,1024]{3,2,0,1:T(8,128)(2,1)S(1)}, u32[]{:S(2)}, u32[]{:S(2)}) %all-to-all-start.1) | async-done | bytes 3145760 | tf_op jit(solution)/shard_map/all_to_all | solution.py:49
  107.4 2.1 copy.50
  109.5 5.9 %fusion.21 = f32[2,768,768]{1,2,0:T(8,128)S(1)} fusion(bf16[2,768,1024]{2,1,0:T(8,128)(2,1)} %bitcast.40, bf16[1024,2,768]{2,0,1:T(8,128)(2,1)} %all-gather.2.cloned.1.call-done), kind=kOutput, calls=%fused_computation.48 | convolution fusion | flops 2415919104 | bytes 11010048 | tf_op jit(solution)/shard_map/jrd,dje->jre/dot_general | solution.py:58
  115.5 1.5 fusion.2
  117.3 3.5 %convolution_convert_fusion = bf16[2,768,1024]{2,1,0:T(8,128)(2,1)S(1)} fusion(bf16[1024,2,768]{2,0,1:T(8,128)(2,1)S(1)} %copy-done.7, bf16[2,768,384]{1,2,0:T(8,128)(2,1)S(1)} %get-tuple-element.10, bf16[2,768,384]{1,2,0:T(8,128)(2,1)S(1)} %get-tuple-element.9), kind=kOutput, calls=%fused_computation.11 | convolution fusion | flops 2422210560 | bytes 8650752 | tf_op jit(solution)/shard_map/jre,dje->jrd/dot_general | solution.py:60
  120.9 2.1 copy.55
  123.0 6.6 %all-to-all-start.2 = ((bf16[2,32,24,1024]{3,2,0,1:T(8,128)(2,1)}), bf16[2,32,24,1024]{3,2,0,1:T(8,128)(2,1)}, u32[]{:S(2)}, u32[]{:S(2)}) async-start(bf16[2,32,24,1024]{3,2,0,1:T(8,128)(2,1)} %copy.55), calls=%async_computation.2 | async-start | bytes 6291456 | tf_op jit(solution)/shard_map/all_to_all | solution.py:71
  129.6 5.6 %convert_bitcast_fusion = bf16[1024,2,768]{0,2,1:T(8,128)(2,1)} fusion(bf16[2,768,1024]{2,1,0:T(8,128)(2,1)S(1)} %bitcast.41, bf16[2,768,384]{1,2,0:T(8,128)(2,1)} %copy-done.4, bf16[2,768,384]{1,2,0:T(8,128)(2,1)} %copy-done.3), kind=kOutput, calls=%fused_computation.3 | convolution fusion | flops 2422210560 | bytes 8650752 | tf_op jit(solution)/shard_map/jrd,jre->dje/dot_general | solution.py:64
  135.3 8.7 %copy.57 = bf16[1024,2,768]{2,1,0:T(2,128)(2,1)} copy(bf16[1024,2,768]{0,2,1:T(8,128)(2,1)} %convert_bitcast_fusion) | data formatting | bytes 6291456 | tf_op jit(solution)/shard_map/convert_element_type | solution.py:64
  144.1 0.6 copy-done.6
  144.9 1.3 dynamic-slice
  147.0 118.4 %psum.7 = f32[64]{0:T(128)S(1)} all-reduce(f32[64]{0:T(128)S(1)} %fusion.15), channel_id=1, replica_groups=mesh['dp'=16,'expert'=32] {'dp','expert'}, use_global_device_ids=true, to_apply=%region_8.9 | all-reduce | flops 64 | bytes 512 | tf_op jit(solution)/shard_map/psum | solution.py:53
  265.3 0.6 dynamic-slice_multiply_fusion
  265.9 2.3 copy.56
  268.2 5.4 %gather_fusion = bf16[1024,1024]{1,0:T(8,128)(2,1)} fusion(bf16[1536,1024]{1,0:T(8,128)(2,1)S(1)} %bitcast.37, s32[1024]{0:T(1024)S(1)} %broadcast_clamp_fusion), kind=kCustom, calls=%fused_computation | custom fusion | bytes 4198400 | tf_op jit(solution)/shard_map/gather | solution.py:78
  273.6 3.7 %bitcast_reduce_fusion = bf16[128,1024]{1,0:T(8,128)(2,1)} fusion(bf16[1024,1024]{1,0:T(8,128)(2,1)} %gather_fusion), kind=kLoop, calls=%fused_computation.12 | loop fusion | flops 917504 | bytes 2359296 | tf_op jit(solution)/shard_map/reduce_sum | solution.py:79
  277.3 19.5 %all-reduce.3.cloned.1.call-done = bf16[1024,2,768]{2,1,0:T(2,128)(2,1)} async-done(((bf16[1024,2,768]{2,1,0:T(2,128)(2,1)}), bf16[1024,2,768]{2,1,0:T(2,128)(2,1)}) %all-reduce.3.cloned.1.call-update) | async-done | bytes 3145744
  296.9 1.7 constant_dynamic-slice_fusion
  (38 shorter events, 1.8 us)
Async XLA Ops:
  7.2 39.4 %copy-start = (bf16[128,1024]{1,0:T(8,128)(2,1)S(1)}, bf16[128,1024]{1,0:T(8,128)(2,1)}, u32[]{:S(2)}) copy-start(bf16[128,1024]{1,0:T(8,128)(2,1)} %param.5) | copy-start | bytes 786436
  7.2 22.4 %copy-start.5 = (bf16[128,8,384]{2,1,0:T(8,128)(2,1)S(1)}, bf16[128,8,384]{2,1,0:T(8,128)(2,1)}, u32[]{:S(2)}) copy-start(bf16[128,8,384]{2,1,0:T(8,128)(2,1)} %param.8) | copy-start | bytes 2359300
  7.2 102.3 %all-gather.2.cloned.1.call-start = ((), (), s32[]{:S(2)}) async-start(), calls=%async_computation.3 | async-start | bytes 3342336 | tf_op jit(solution)/shard_map/all_gather | solution.py:57
  36.2 27.0 %all-to-all-start = ((bf16[2,32,24,384]{3,2,0,1:T(8,128)(2,1)}), bf16[2,32,24,384]{3,2,0,1:T(8,128)(2,1)}, u32[]{:S(2)}, u32[]{:S(2)}) async-start(bf16[2,32,24,384]{3,2,0,1:T(8,128)(2,1)} %copy.47), calls=%async_computation | async-start | bytes 2359296 | tf_op jit(solution)/shard_map/all_to_all | solution.py:50
  63.2 44.2 %all-to-all-start.1 = ((bf16[2,32,24,1024]{3,2,0,1:T(8,128)(2,1)}), bf16[2,32,24,1024]{3,2,0,1:T(8,128)(2,1)S(1)}, u32[]{:S(2)}, u32[]{:S(2)}) async-start(bf16[2,32,24,1024]{3,2,0,1:T(8,128)(2,1)} %copy.49), calls=%async_computation.1 | async-start | bytes 6291456 | tf_op jit(solution)/shard_map/all_to_all | solution.py:49
  109.5 5.9 %copy-start.1 = (f32[2,768,384]{1,2,0:T(8,128)S(1)}, f32[2,768,384]{1,2,0:T(8,128)}, u32[]{:S(2)}) copy-start(f32[2,768,384]{1,2,0:T(8,128)} %copy.52) | copy-start | bytes 7077892
  115.4 1.9 copy-start.7
  116.9 3.9 %copy-start.3 = (bf16[2,768,384]{1,2,0:T(8,128)(2,1)}, bf16[2,768,384]{1,2,0:T(8,128)(2,1)S(1)}, u32[]{:S(2)}) copy-start(bf16[2,768,384]{1,2,0:T(8,128)(2,1)S(1)} %get-tuple-element.9) | copy-start | bytes 3538948
  116.9 3.9 %copy-start.4 = (bf16[2,768,384]{1,2,0:T(8,128)(2,1)}, bf16[2,768,384]{1,2,0:T(8,128)(2,1)S(1)}, u32[]{:S(2)}) copy-start(bf16[2,768,384]{1,2,0:T(8,128)(2,1)S(1)} %get-tuple-element.10) | copy-start | bytes 3538948
  123.0 6.6 %copy-start.2 = (bf16[2,32,24,1024]{3,2,1,0:T(8,128)(2,1)S(1)}, bf16[2,32,24,1024]{3,2,1,0:T(8,128)(2,1)}, u32[]{:S(2)}) copy-start(bf16[2,32,24,1024]{3,2,1,0:T(8,128)(2,1)} %copy.50) | copy-start | bytes 9437188
  123.0 142.9 %all-to-all-start.2 = ((bf16[2,32,24,1024]{3,2,0,1:T(8,128)(2,1)}), bf16[2,32,24,1024]{3,2,0,1:T(8,128)(2,1)}, u32[]{:S(2)}, u32[]{:S(2)}) async-start(bf16[2,32,24,1024]{3,2,0,1:T(8,128)(2,1)} %copy.55), calls=%async_computation.2 | async-start | bytes 6291456 | tf_op jit(solution)/shard_map/all_to_all | solution.py:71
  129.6 167.3 %all-reduce.3.cloned.1.call-start = ((), (), s32[]{:S(2)}) async-start(), calls=%async_computation.4 | async-start | bytes 6291456
  144.0 0.7 copy-start.6
Sparse Core Ops, SparseCore 0:
  10.7 80.4 all-gather.1
  144.2 152.6 all-reduce.2
where the time goes:
time: 307 us; the launch traced here: 305 us
  blocking collectives  118 us (38%)
  waiting for transfers between devices  60.1 us (20%)
  local copies, waits for them, and re-layouts  42.9 us (14%)
  other arithmetic  31.5 us (10%)
  starting transfers between devices  22.7 us (7%)
  matrix products  15.1 us (5%)
  between operations  14.9 us (5%)
    psum x1, blocking collectives, body(): everyone = lax.psum(own_sums, ('dp', 'expert'))  118 us
    all_to_all x1, waiting for transfers between devices, body(): lax.all_to_all(send_rows, 'expert', split_axis=1, concat_axis=1, tiled=True)  32.3 us
    another operation x4, other arithmetic  19.6 us
    unnamed x3, waiting for transfers between devices  19.6 us
    all_to_all x1, starting transfers between devices, body(): lax.all_to_all(send_cot, 'expert', split_axis=1, concat_axis=1, tiled=True)  10.3 us
    convert_element_type x1, local copies, waits for them, and re-layouts, body(): jnp.einsum('jrd,jre->dje', rows_in, grad_pre, preferred_element_type=jnp....  8.74 us
    all_to_all x1, waiting for transfers between devices, body(): lax.all_to_all(send_cot, 'expert', split_axis=1, concat_axis=1, tiled=True)  8.22 us
    unnamed x21, local copies, waits for them, and re-layouts  7.37 us
  transfers between devices with their start and end apart: 5, of which 3 were waited for; matrix products, arithmetic and copies ran while one was open for 24% of the time, Pallas kernels for 0%

commit v1 on v0

v1 whole, which is shorter than its diff:
```python
import functools

import jax
import jax.numpy as jnp
from jax import lax
from jax.experimental import pallas as pl
from jax.experimental.pallas import tpu as pltpu
from jax.sharding import PartitionSpec as P

F32 = jnp.float32
BF16 = jnp.bfloat16
VMEM_LIMIT = 48 * 1024 * 1024


def iota(shape, dim):
    return lax.broadcasted_iota(jnp.int32, shape, dim)


def dot(a, b, contract=((1,), (0,))):
    return lax.dot_general(a, b, (contract, ((), ())), preferred_element_type=F32)


def plan(routes_row, tok_count, topk, per_device, devices, cap):
    experts, count = per_device * devices, tok_count * topk
    row = iota((experts, 1), 0)
    expert = (row % devices) * per_device + row // devices
    table = routes_row == expert
    spread = (iota((tok_count, count), 1) // topk == iota((tok_count, count), 0)).astype(BF16)
    tok_table = dot(table.astype(BF16), spread, ((1,), (1,)))
    before = (iota((tok_count, tok_count), 0) < iota((tok_count, tok_count), 1)).astype(BF16)
    earlier = dot(tok_table.astype(BF16), before)
    tok_slot = jnp.where(tok_table > 0.5, earlier, -1.0).astype(jnp.int32)
    route_earlier = dot(earlier.astype(BF16), spread)
    slots = jnp.where(table, (row * cap).astype(F32) + route_earlier, 0.0)
    slot = jnp.sum(slots, axis=0, keepdims=True).astype(jnp.int32)
    return table, slot, tok_slot


def token_kernel(per_device, devices, cap, routes_ref, gates_ref, tokens_ref, rows_ref, picks_ref, slot_ref, sums_ref):
    tok_count, model = tokens_ref.shape
    topk = routes_ref.shape[1] // tok_count
    experts = per_device * devices
    table, slot, tok_slot = plan(routes_ref[...], tok_count, topk, per_device, devices, cap)
    slot_ref[...] = slot
    mark = gates_ref[...].astype(BF16).astype(F32)
    sums_ref[...] = jnp.sum(jnp.where(table, mark, 0.0), axis=1, keepdims=True)
    hits = tok_slot[:, None, :] == iota((experts, cap, tok_count), 1)
    picks = hits.astype(F32).reshape(experts * cap, tok_count).astype(BF16)
    size = devices * cap
    tokens = tokens_ref[...]
    for j in range(per_device):
        mine = picks[j * size : (j + 1) * size]
        picks_ref[:, j * tok_count : (j + 1) * tok_count] = mine
        rows_ref[:, j * model : (j + 1) * model] = dot(mine, tokens).astype(BF16)


def cot_kernel(per_device, slot_ref, gates_ref, cot_ref, out_ref):
    size = out_ref.shape[0]
    count, width = cot_ref.shape
    step = 128
    slot, gates = slot_ref[...], gates_ref[...]
    for j in range(per_device):
        for i in range(size // step):
            hit = slot == iota((step, 1), 0) + (j * size + i * step)
            gate = jnp.sum(jnp.where(hit, gates, 0.0), axis=1, keepdims=True)
            rows = dot(hit.astype(F32).astype(BF16), cot_ref[...])
            out_ref[i * step : (i + 1) * step, j * width : (j + 1) * width] = (rows * gate).astype(BF16)


def grad_kernel(rows_ref, cot_ref, w_ref, gp_ref, gw_ref):
    size, model = rows_ref.shape
    width = cot_ref.shape[1]
    step = 256
    for i in range(size // step):
        part = pl.ds(i * step, step)
        pre = dot(rows_ref[part, :], w_ref[...])
        gate, upper = pre[:, :width], pre[:, width:]
        sigma = jax.nn.sigmoid(gate)
        scaled = cot_ref[part, :].astype(F32)
        common = scaled * sigma
        gp_ref[part, :width] = (common * upper * (1.0 + gate * (1.0 - sigma))).astype(BF16)
        gp_ref[part, width:] = (common * gate).astype(BF16)
    for i in range(model // step):
        part = pl.ds(i * step, step)
        gw_ref[part, :] = dot(rows_ref[:, part], gp_ref[...], ((0,), (0,))).astype(BF16)


def route_kernel(gp_ref, w_ref, out_ref):
    size = gp_ref.shape[0]
    step = 256
    for i in range(size // step):
        part = pl.ds(i * step, step)
        out_ref[part, :] = dot(gp_ref[part, :], w_ref[...], ((1,), (1,))).astype(BF16)


def sum_kernel(per_device, picks_ref, back_ref, out_ref):
    tok_count, model = out_ref.shape
    total = jnp.zeros((tok_count, model), F32)
    for j in range(per_device):
        picks = picks_ref[:, j * tok_count : (j + 1) * tok_count]
        total += dot(picks, back_ref[:, j * model : (j + 1) * model], ((0,), (0,)))
    out_ref[...] = total.astype(BF16)


def call(kernel, outs, *args, cost):
    whole = pl.BlockSpec(memory_space=pltpu.VMEM)
    return pl.pallas_call(
        kernel,
        out_shape=[jax.ShapeDtypeStruct(s, t) for s, t in outs],
        in_specs=[whole] * len(args),
        out_specs=[whole] * len(outs),
        compiler_params=pltpu.CompilerParams(vmem_limit_bytes=VMEM_LIMIT),
        cost_estimate=cost,
    )(*args)


def estimate(flops, moved):
    return pl.CostEstimate(flops=flops, bytes_accessed=moved, transcendentals=0)


def body(tokens, routes, route_gates, route_cotangent, gate_up):
    tok_count, topk = routes.shape
    width = route_cotangent.shape[2]
    model = tokens.shape[1]
    channels, per_device, hidden = gate_up.shape
    devices = lax.axis_size("expert")
    data_ways = lax.axis_size("dp")
    cap = 3 * tok_count * topk // (2 * per_device * devices)
    size, count = devices * cap, tok_count * topk

    lift = 2.0**18
    weights = gate_up.reshape(channels, per_device * hidden)
    sent = (weights.astype(F32) * lift).astype(jnp.float16)

    routes_row = routes.reshape(1, count)
    gates_row = route_gates.reshape(1, count)
    rows, picks, slot, sums = call(
        functools.partial(token_kernel, per_device, devices, cap),
        [((size, per_device * model), BF16), ((size, per_device * tok_count), BF16), ((1, count), jnp.int32), ((per_device * devices, 1), F32)],
        routes_row,
        gates_row,
        tokens,
        cost=estimate(2 * size * per_device * tok_count * model, 2 * size * per_device * model),
    )
    got_rows = lax.all_to_all(rows, "expert", split_axis=0, concat_axis=0, tiled=True)
    (cots,) = call(
        functools.partial(cot_kernel, per_device),
        [((size, per_device * width), BF16)],
        slot,
        gates_row,
        route_cotangent.reshape(count, width),
        cost=estimate(2 * size * per_device * count * width, 2 * size * per_device * width),
    )
    got_cots = lax.all_to_all(cots, "expert", split_axis=0, concat_axis=0, tiled=True)
    everyone = lax.psum(sums.reshape(-1), ("dp", "expert"))
    gathered = lax.all_gather(sent, "dp", axis=0, tiled=True)
    full = (gathered.astype(F32) * (1.0 / lift)).astype(BF16)

    cut = [
        pl.BlockSpec((size, model), lambda j: (0, j)),
        pl.BlockSpec((size, width), lambda j: (0, j)),
        pl.BlockSpec((model, hidden), lambda j: (0, j)),
        pl.BlockSpec((size, hidden), lambda j: (0, j)),
    ]
    params = pltpu.CompilerParams(vmem_limit_bytes=VMEM_LIMIT, dimension_semantics=("arbitrary",))
    work = 2 * per_device * size * model * hidden
    grad_pre, part = pl.pallas_call(
        grad_kernel,
        grid=(per_device,),
        in_specs=[cut[0], cut[1], cut[2]],
        out_specs=[cut[3], cut[2]],
        out_shape=[
            jax.ShapeDtypeStruct((size, per_device * hidden), BF16),
            jax.ShapeDtypeStruct((model, per_device * hidden), BF16),
        ],
        compiler_params=params,
        cost_estimate=estimate(2 * work, 12 * size * model),
    )(got_rows, got_cots, full)
    mine = lax.psum_scatter(part, "dp", scatter_dimension=0, tiled=True)
    back = pl.pallas_call(
        route_kernel,
        grid=(per_device,),
        in_specs=[cut[3], cut[2]],
        out_specs=cut[0],
        out_shape=jax.ShapeDtypeStruct((size, per_device * model), BF16),
        compiler_params=params,
        cost_estimate=estimate(work, 12 * size * model),
    )(grad_pre, full)
    returned = lax.all_to_all(back, "expert", split_axis=0, concat_axis=0, tiled=True)
    (grad_tokens,) = call(
        functools.partial(sum_kernel, per_device),
        [((tok_count, model), BF16)],
        picks,
        returned,
        cost=estimate(2 * size * per_device * tok_count * model, 2 * size * per_device * model),
    )
    sums_here = lax.dynamic_index_in_dim(everyone.reshape(per_device, devices), lax.axis_index("expert"), 1, keepdims=False)
    load = sums_here * (per_device / (tok_count * topk * data_ways))
    return (grad_tokens, mine.reshape(channels, per_device, hidden), load)


def solution(mesh):
    in_specs = (
        P(("dp", "expert"), None),
        P(("dp", "expert"), None),
        P(("dp", "expert"), None),
        P(("dp", "expert"), None, None),
        P("dp", "expert", None),
    )
    out_specs = (P(("dp", "expert"), None), P("dp", "expert", None), P("expert"))
    return jax.shard_map(body, mesh=mesh, in_specs=in_specs, out_specs=out_specs, check_vma=False)
```

time: 307 us -> 278 us (0.906)
  blocking collectives: 118 us -> 210 us
  waiting for transfers between devices: 60.1 us -> 0.02 us
  local copies, waits for them, and re-layouts: 42.9 us -> 10.4 us
  other arithmetic: 31.5 us -> 4.05 us
  Pallas kernels: 0 us -> 20.3 us
  matrix products: 15.1 us -> 0 us
  starting transfers between devices: 22.7 us -> 16 us
    all_gather x0 -> x1, blocking collectives: none -> 55.5 us  [body(): gathered = lax.all_gather(sent, 'dp', axis=0, tiled=True)]
    all_to_all x3 -> x2, waiting for transfers between devices: 40.5 us -> 0.01 us  [the longest x1 0.01 us: body(): lax.all_to_all(rows, 'expert', split_axis=0, concat_axis=0, tiled=True)]
    all_to_all x0 -> x1, blocking collectives: none -> 25.8 us  [body(): lax.all_to_all(cots, 'expert', split_axis=0, concat_axis=0, tiled=True)]
    pallas_call x0 -> x5, Pallas kernels: none -> 20.3 us  [the longest x1 9.3 us: body(): pl.pallas_call(grad_kernel, grid=(per_device,), in_specs=[cut[0], cut[1],...]
    another operation x4 -> x0, other arithmetic: 19.6 us -> none
    unnamed x3 -> x1, waiting for transfers between devices: 19.6 us -> 0.02 us
    dot_general x3 -> x0, matrix products: 15.1 us -> none  [the longest x1 5.91 us: body(): jnp.einsum('jrd,dje->jre', rows_in, gathered, preferred_element_type=jnp....]
    convert_element_type x4 -> x0, local copies, waits for them, and re-layouts: 12 us -> none  [the longest x1 8.74 us: body(): jnp.einsum('jrd,jre->dje', rows_in, grad_pre, preferred_element_type=jnp....]
  transfers between devices with their start and end apart: 5 -> 3, of which waited for: 3 -> 0; matrix products, arithmetic and copies ran while one was open for 24% -> 2% of each run, Pallas kernels for 0% -> 2%
where the time goes in v1:
time: 278 us; the launch traced here: 275 us
  blocking collectives  210 us (76%)
  Pallas kernels  20.3 us (7%)
  starting transfers between devices  16 us (6%)
  between operations  14.1 us (5%)
  local copies, waits for them, and re-layouts  10.4 us (4%)
  other arithmetic  4.05 us (1%)
    psum x1, blocking collectives, body(): everyone = lax.psum(sums.reshape(-1), ('dp', 'expert'))  129 us
    all_gather x1, blocking collectives, body(): gathered = lax.all_gather(sent, 'dp', axis=0, tiled=True)  55.5 us
    all_to_all x1, blocking collectives, body(): lax.all_to_all(cots, 'expert', split_axis=0, concat_axis=0, tiled=True)  25.8 us
    pallas_call x1, Pallas kernels, body(): pl.pallas_call(grad_kernel, grid=(per_device,), in_specs=[cut[0], cut[1],...  9.3 us
    all_to_all x1, starting transfers between devices, body(): lax.all_to_all(back, 'expert', split_axis=0, concat_axis=0, tiled=True)  9.07 us
    unnamed x17, local copies, waits for them, and re-layouts  8.46 us
    all_to_all x1, starting transfers between devices, body(): lax.all_to_all(rows, 'expert', split_axis=0, concat_axis=0, tiled=True)  6.88 us
    pallas_call x3, Pallas kernels, call(): pl.pallas_call(kernel, out_shape=[jax.ShapeDtypeStruct(s, t) for s, t in...  6.43 us
  transfers between devices with their start and end apart: 3, of which 0 were waited for; matrix products, arithmetic and copies ran while one was open for 2% of the time, Pallas kernels for 2%

profile of v1, /device:TPU:6, one launch (start us, length us, event | category | flops | bytes accessed | tf_op | source)
XLA Modules:
  0.0 274.9 jit_solution(746571098564250967)
XLA Ops:
  7.2 0.8 copy.10
  8.0 0.1 reshape.37.routes_ref
  8.1 0.8 copy.11
  8.8 0.1 reshape.38.gates_ref
  8.9 0.9 copy-done.3
  9.9 3.1 %shard_map.76 = (bf16[768,2048]{1,0:T(8,128)(2,1)}, bf16[768,256]{1,0:T(8,128)(2,1)S(1)}, s32[1,1024]{1,0:T(1,128)S(1)}, f32[64,1]{1,0:T(8,128)S(1)}) custom-call(s32[1,1024]{1,0:T(1,128)S(1)} %reshape.37.routes_ref, f32[1,1024]{1,0:T(1,128)S(1)} %reshape.38.gates_ref, bf16[128,1024]{1,0:T(8,128)(2,1)S(1)} %copy-done.3), custom_call_target="tpu_custom_call" | custom-call | flops 402653184 | bytes 3145728 | tf_op jit(solution)/shard_map/pallas_call | solution.py:107
  13.0 1.1 copy-done.2
  14.1 2.0 shard_map.77
  16.2 25.8 %all_to_all.33 = bf16[32,24,768]{2,1,0:T(8,128)(2,1)S(1)} all-to-all(bf16[32,24,768]{2,1,0:T(8,128)(2,1)S(1)} %bitcast.12), channel_id=1, replica_groups=mesh['dp'=16,'expert'=32] {'expert'}, dimensions={0} | all-to-all | bytes 2359296 | tf_op jit(solution)/shard_map/all_to_all | solution.py:154
  41.9 0.0 copy-done.1
  41.9 6.9 %all-to-all-start = ((bf16[32,24,2048]{2,1,0:T(8,128)(2,1)}), bf16[32,24,2048]{2,1,0:T(8,128)(2,1)}, u32[]{:S(2)}, u32[]{:S(2)}) async-start(bf16[32,24,2048]{2,1,0:T(8,128)(2,1)} %bitcast), calls=%async_computation | async-start | bytes 6291456 | tf_op jit(solution)/shard_map/all_to_all | solution.py:145
  48.8 0.0 reduce-scatter.2.cloned.1.call-start
  48.9 0.0 copy-done.6
  48.9 0.2 multiply_convert_fusion.1
  49.1 0.1 copy.12
  49.1 55.5 %all-gather.1 = f16[1024,1536]{1,0:T(8,128)(2,1)S(1)} all-gather(f16[64,1536]{1,0:T(8,128)(2,1)S(1)} %bitcast.14), channel_id=1, replica_groups=mesh['dp'=16,'expert'=32] {'dp'}, dimensions={0}, use_global_device_ids=true | all-gather | bytes 3342336 | tf_op jit(solution)/shard_map/all_gather | solution.py:156
  104.6 2.3 multiply_convert_fusion.w_ref
  106.9 0.0 all-to-all-done
  106.9 9.3 %shard_map.78 = (bf16[768,1536]{1,0:T(8,128)(2,1)S(1)}, bf16[1024,1536]{1,0:T(8,128)(2,1)}) custom-call(bf16[768,2048]{1,0:T(8,128)(2,1)} %bitcast.1.rows_ref, bf16[768,768]{1,0:T(8,128)(2,1)S(1)} %bitcast.11, bf16[1024,1536]{1,0:T(8,128)(2,1)} %multiply_convert_fusion.w_ref), custom_call_target="tpu_custom_call" | custom-call | flops 4831838208 | bytes 9437184 | tf_op jit(solution)/shard_map/pallas_call | solution.py:167
  116.2 1.4 copy-done.4
  117.7 0.0 reduce-scatter.2.cloned.1.call-update
  117.7 1.6 copy-done.5
  119.3 4.5 %shard_map.79 = bf16[768,2048]{1,0:T(8,128)(2,1)S(1)} custom-call(bf16[768,1536]{1,0:T(8,128)(2,1)S(1)} %copy-done.5, bf16[1024,1536]{1,0:T(8,128)(2,1)} %multiply_convert_fusion.w_ref), custom_call_target="tpu_custom_call" | custom-call | flops 2415919104 | bytes 9437184 | tf_op jit(solution)/shard_map/pallas_call | solution.py:180
  123.9 1.7 copy-done
  125.5 9.1 %all-to-all-start.2 = ((bf16[32,24,2048]{2,1,0:T(8,128)(2,1)}), bf16[32,24,2048]{2,1,0:T(8,128)(2,1)S(1)}, u32[]{:S(2)}, u32[]{:S(2)}) async-start(bf16[32,24,2048]{2,1,0:T(8,128)(2,1)} %bitcast.10), calls=%async_computation.2 | async-start | bytes 6291456 | tf_op jit(solution)/shard_map/all_to_all | solution.py:189
  134.6 0.9 reduce
  135.5 0.1 reshape.42
  135.6 128.9 %psum.7 = f32[2,32]{1,0:T(2,128)S(1)} all-reduce(f32[2,32]{1,0:T(2,128)S(1)} %reshape.42), channel_id=1, replica_groups=mesh['dp'=16,'expert'=32] {'dp','expert'}, use_global_device_ids=true, to_apply=%region_1.0 | all-reduce | flops 64 | bytes 512 | tf_op jit(solution)/shard_map/psum | solution.py:155
  264.4 0.7 multiply_reduce_fusion
  265.1 0.0 all-to-all-done.2
  265.1 1.3 shard_map.80
  266.4 1.7 reshape.40
  (8 shorter events, 0.0 us)
Async XLA Ops:
  8.9 0.9 copy-start.3
  13.0 29.0 %copy-start.1 = (f32[64,1]{1,0:T(8,128)}, f32[64,1]{1,0:T(8,128)S(1)}, u32[]{:S(2)}) copy-start(f32[64,1]{1,0:T(8,128)S(1)} %get-tuple-element.14) | copy-start | bytes 772
  13.0 1.1 copy-start.2
  41.9 6.9 %copy-start.6 = (bf16[64,2,768]{2,1,0:T(2,128)(2,1)S(1)}, bf16[64,2,768]{2,1,0:T(2,128)(2,1)}, u32[]{:S(2)}) copy-start(bf16[64,2,768]{2,1,0:T(2,128)(2,1)} %param.9) | copy-start | bytes 589828
  41.9 65.0 %all-to-all-start = ((bf16[32,24,2048]{2,1,0:T(8,128)(2,1)}), bf16[32,24,2048]{2,1,0:T(8,128)(2,1)}, u32[]{:S(2)}, u32[]{:S(2)}) async-start(bf16[32,24,2048]{2,1,0:T(8,128)(2,1)} %bitcast), calls=%async_computation | async-start | bytes 6291456 | tf_op jit(solution)/shard_map/all_to_all | solution.py:145
  48.8 217.6 %reduce-scatter.2.cloned.1.call-start = ((), (), s32[]{:S(2)}) async-start(), calls=%async_computation.4 | async-start | bytes 3342336 | tf_op jit(solution)/shard_map/reduce_scatter | solution.py:179
  116.2 1.4 copy-start.4
  117.7 1.7 copy-start.5
  123.9 1.7 copy-start
  125.5 139.6 %all-to-all-start.2 = ((bf16[32,24,2048]{2,1,0:T(8,128)(2,1)}), bf16[32,24,2048]{2,1,0:T(8,128)(2,1)S(1)}, u32[]{:S(2)}, u32[]{:S(2)}) async-start(bf16[32,24,2048]{2,1,0:T(8,128)(2,1)} %bitcast.10), calls=%async_computation.2 | async-start | bytes 6291456 | tf_op jit(solution)/shard_map/all_to_all | solution.py:189
Sparse Core Ops, SparseCore 0:
  117.8 73.8 reduce-scatter.1

commit v2 on v0

v2 whole, which is shorter than its diff:
```python
import functools

import jax
import jax.numpy as jnp
from jax import lax
from jax.experimental import pallas as pl
from jax.experimental.pallas import tpu as pltpu
from jax.sharding import PartitionSpec as P

F32 = jnp.float32
BF16 = jnp.bfloat16
VMEM_LIMIT = 48 * 1024 * 1024


def iota(shape, dim):
    return lax.broadcasted_iota(jnp.int32, shape, dim)


def dot(a, b, contract=((1,), (0,))):
    return lax.dot_general(a, b, (contract, ((), ())), preferred_element_type=F32)


def split3(x):
    high = x.astype(BF16)
    rest = x - high.astype(F32)
    middle = rest.astype(BF16)
    return high, middle, (rest - middle.astype(F32)).astype(BF16)


def pack_kernel(per_device, devices, cap, routes_ref, gates_ref, tokens_hbm, cot_hbm, out_ref, picks_ref, sums_ref, tokens_ref, cot_ref, sems):
    topk, tok_count = routes_ref.shape
    model, width = tokens_ref.shape[1], cot_ref.shape[1]
    count, experts = tok_count * topk, per_device * devices
    size = devices * cap
    copies = [
        pltpu.make_async_copy(tokens_hbm, tokens_ref, sems.at[0]),
        pltpu.make_async_copy(cot_hbm, cot_ref, sems.at[1]),
    ]
    for copy in copies:
        copy.start()

    spread = (iota((tok_count, count), 1) // topk == iota((tok_count, count), 0)).astype(F32).astype(BF16)
    own = iota((topk, count), 1) % topk == iota((topk, count), 0)
    parts = [routes_ref[...].astype(F32).astype(BF16), *split3(gates_ref[...])]
    wide = [jnp.sum(jnp.where(own, dot(part, spread), 0.0), axis=0, keepdims=True) for part in parts]
    routes, gates = wide[0].astype(jnp.int32), (wide[1] + wide[2]) + wide[3]

    row = iota((experts, 1), 0)
    table = routes == (row % devices) * per_device + row // devices
    tok_table = dot(table.astype(F32).astype(BF16), spread, ((1,), (1,)))
    before = (iota((tok_count, tok_count), 0) < iota((tok_count, tok_count), 1)).astype(F32).astype(BF16)
    earlier = dot(tok_table.astype(BF16), before)
    tok_slot = jnp.where(tok_table > 0.5, earlier, -1.0).astype(jnp.int32)
    slots = jnp.where(table, (row * cap).astype(F32) + dot(earlier.astype(BF16), spread), 0.0)
    slot = jnp.sum(slots, axis=0, keepdims=True).astype(jnp.int32)

    mark = gates.astype(BF16).astype(F32)
    sums = jnp.sum(jnp.where(table, mark, 0.0), axis=1, keepdims=True)
    for j in range(per_device):
        sums_ref[:, j * 128 : (j + 1) * 128] = jnp.broadcast_to(sums[j * devices : (j + 1) * devices], (devices, 128))

    hits = tok_slot[:, None, :] == iota((experts, cap, tok_count), 1)
    picks_ref[...] = hits.astype(F32).reshape(experts * cap, tok_count).astype(BF16)
    step = 256
    copies[0].wait()
    for j in range(per_device):
        for i in range(0, size, step):
            rows = dot(picks_ref[j * size + i : j * size + i + step, :], tokens_ref[...])
            out_ref[i : i + step, j * model : (j + 1) * model] = rows.astype(BF16)
    copies[1].wait()
    for j in range(per_device):
        for i in range(0, size, step):
            hit = slot == iota((step, 1), 0) + (j * size + i)
            gate = jnp.sum(jnp.where(hit, gates, 0.0), axis=1, keepdims=True)
            rows = dot(hit.astype(F32).astype(BF16), cot_ref[...])
            at = per_device * model + j * width
            out_ref[i : i + step, at : at + width] = (rows * gate).astype(BF16)


def grad_kernel(per_device, got_hbm, w_hbm, gp_ref, gw_hbm, got_ref, w_ref, gw_ref, sems):
    size, hidden, model = gp_ref.shape[0], gp_ref.shape[1] // per_device, w_ref.shape[0]
    width = hidden // 2
    step = 256
    tiles = size // step
    rows = [pl.ds(i * step, step) for i in range(tiles)]
    columns = [pl.ds(j * hidden, hidden) for j in range(per_device)]
    w_in = [
        pltpu.make_async_copy(w_hbm.at[:, columns[j]], w_ref.at[:, columns[j]], sems.at[j]) for j in range(per_device)
    ]
    got_in = [
        pltpu.make_async_copy(got_hbm.at[rows[i], :], got_ref.at[rows[i], :], sems.at[per_device + i])
        for i in range(tiles)
    ]
    for copy in (w_in[0], *got_in, *w_in[1:]):
        copy.start()
    outs = []
    for j in range(per_device):
        w_in[j].wait()
        at = j * hidden
        for i in range(tiles):
            if j == 0:
                got_in[i].wait()
            pre = dot(got_ref[rows[i], j * model : (j + 1) * model], w_ref[:, columns[j]])
            gate, upper = pre[:, :width], pre[:, width:]
            sigma = jax.nn.sigmoid(gate)
            first = per_device * model + j * width
            common = got_ref[rows[i], first : first + width].astype(F32) * sigma
            gp_ref[rows[i], at : at + width] = (common * upper * (1.0 + gate * (1.0 - sigma))).astype(BF16)
            gp_ref[rows[i], at + width : at + hidden] = (common * gate).astype(BF16)
        for i in range(0, model, step):
            part = got_ref[:, j * model + i : j * model + i + step]
            gw_ref[i : i + step, columns[j]] = dot(part, gp_ref[:, columns[j]], ((0,), (0,))).astype(BF16)
        copy = pltpu.make_async_copy(gw_ref.at[:, columns[j]], gw_hbm.at[:, columns[j]], sems.at[per_device + tiles + j])
        copy.start()
        outs.append(copy)
    for copy in outs:
        copy.wait()


def route_kernel(gp_ref, w_ref, out_ref):
    step = 256
    for i in range(0, gp_ref.shape[0], step):
        out_ref[i : i + step, :] = dot(gp_ref[i : i + step, :], w_ref[...], ((1,), (1,))).astype(BF16)


def sum_kernel(per_device, picks_ref, back_ref, out_ref):
    tok_count, model = out_ref.shape
    size = back_ref.shape[0]
    total = jnp.zeros((tok_count, model), F32)
    for j in range(per_device):
        total += dot(picks_ref[j * size : (j + 1) * size, :], back_ref[:, j * model : (j + 1) * model], ((0,), (0,)))
    out_ref[...] = total.astype(BF16)


def call(kernel, outs, args, in_specs=None, out_specs=None, grid=(), scratch=(), flops=0, moved=0):
    whole = pl.BlockSpec(memory_space=pltpu.VMEM)
    return pl.pallas_call(
        kernel,
        grid=grid,
        out_shape=[jax.ShapeDtypeStruct(s, t) for s, t in outs],
        in_specs=in_specs or [whole] * len(args),
        out_specs=out_specs or [whole] * len(outs),
        scratch_shapes=scratch,
        compiler_params=pltpu.CompilerParams(vmem_limit_bytes=VMEM_LIMIT),
        cost_estimate=pl.CostEstimate(flops=flops, bytes_accessed=moved, transcendentals=0),
    )(*args)


def body(tokens, routes, route_gates, route_cotangent, gate_up):
    tok_count, topk = routes.shape
    width = route_cotangent.shape[2]
    model = tokens.shape[1]
    channels, per_device, hidden = gate_up.shape
    devices = lax.axis_size("expert")
    data_ways = lax.axis_size("dp")
    experts = per_device * devices
    cap = 3 * tok_count * topk // (2 * experts)
    size, count = devices * cap, tok_count * topk
    lanes = per_device * (model + width)
    vmem, anywhere = pl.BlockSpec(memory_space=pltpu.VMEM), pl.BlockSpec(memory_space=pl.ANY)

    lift = 2.0**18
    sent = (gate_up.astype(F32) * lift).astype(jnp.float16).reshape(channels, per_device * hidden)

    packed, picks, sums = call(
        functools.partial(pack_kernel, per_device, devices, cap),
        [((size, lanes), BF16), ((per_device * size, tok_count), BF16), ((devices, per_device * 128), F32)],
        [routes.T, route_gates.T, tokens, route_cotangent.reshape(count, width)],
        in_specs=[vmem, vmem, anywhere, anywhere],
        scratch=[pltpu.VMEM((tok_count, model), BF16), pltpu.VMEM((count, width), BF16), pltpu.SemaphoreType.DMA((2,))],
        flops=2 * per_device * size * (tok_count * model + count * width),
        moved=2 * size * lanes,
    )
    got = lax.all_to_all(packed, "expert", split_axis=0, concat_axis=0, tiled=True)
    gathered = lax.all_gather(sent, "dp", axis=0, tiled=True)
    full = (gathered.astype(F32) * (1.0 / lift)).astype(BF16)

    work = 2 * per_device * size * model * hidden
    grad_pre, part = call(
        functools.partial(grad_kernel, per_device),
        [((size, per_device * hidden), BF16), ((model, per_device * hidden), BF16)],
        [got, full],
        in_specs=[anywhere, anywhere],
        out_specs=[vmem, anywhere],
        scratch=[
            pltpu.VMEM((size, lanes), BF16),
            pltpu.VMEM((model, per_device * hidden), BF16),
            pltpu.VMEM((model, per_device * hidden), BF16),
            pltpu.SemaphoreType.DMA((2 * per_device + size // 256,)),
        ],
        flops=2 * work,
        moved=12 * size * model,
    )
    mine = lax.psum_scatter(part, "dp", scatter_dimension=0, tiled=True)
    (back,) = call(
        route_kernel,
        [((size, per_device * model), BF16)],
        [grad_pre, full],
        in_specs=[pl.BlockSpec((size, hidden), lambda j: (0, j)), pl.BlockSpec((model, hidden), lambda j: (0, j))],
        out_specs=[pl.BlockSpec((size, model), lambda j: (0, j))],
        grid=(per_device,),
        flops=work,
        moved=12 * size * model,
    )
    returned = lax.all_to_all(back, "expert", split_axis=0, concat_axis=0, tiled=True)
    (grad_tokens,) = call(
        functools.partial(sum_kernel, per_device),
        [((tok_count, model), BF16)],
        [picks, returned],
        flops=2 * per_device * size * tok_count * model,
        moved=4 * size * model,
    )

    here = jnp.sum(lax.all_to_all(sums, "expert", split_axis=0, concat_axis=0, tiled=True), axis=0, keepdims=True)
    heard = lax.all_to_all(jnp.tile(here, (data_ways, 1)), "dp", split_axis=0, concat_axis=0, tiled=True)
    totals = jnp.sum(heard, axis=0).reshape(per_device, 128)[:, 0]
    load = totals * (per_device / (tok_count * topk * data_ways))
    return (grad_tokens, mine.reshape(channels, per_device, hidden), load)


def solution(mesh):
    in_specs = (
        P(("dp", "expert"), None),
        P(("dp", "expert"), None),
        P(("dp", "expert"), None),
        P(("dp", "expert"), None, None),
        P("dp", "expert", None),
    )
    out_specs = (P(("dp", "expert"), None), P("dp", "expert", None), P("expert"))
    return jax.shard_map(body, mesh=mesh, in_specs=in_specs, out_specs=out_specs, check_vma=False)
```

time: 307 us -> 186 us (0.61)
  blocking collectives: 118 us -> 67 us
  local copies, waits for them, and re-layouts: 42.9 us -> 9.49 us
  other arithmetic: 31.5 us -> 4.47 us
  Pallas kernels: 0 us -> 18.9 us
  waiting for transfers between devices: 60.1 us -> 43.2 us
  matrix products: 15.1 us -> 0 us
    psum x1 -> x0, blocking collectives: 118 us -> none  [body(): everyone = lax.psum(own_sums, ('dp', 'expert'))]
    all_gather x0 -> x1, blocking collectives: none -> 53.7 us  [body(): gathered = lax.all_gather(sent, 'dp', axis=0, tiled=True)]
    another operation x4 -> x0, other arithmetic: 19.6 us -> none
    unnamed x3 -> x1, waiting for transfers between devices: 19.6 us -> 0.02 us
    pallas_call x0 -> x4, Pallas kernels: none -> 18.9 us  [call(): pl.pallas_call(kernel, grid=grid, out_shape=[jax.ShapeDtypeStruct(s, t) f...]
    dot_general x3 -> x0, matrix products: 15.1 us -> none  [the longest x1 5.91 us: body(): jnp.einsum('jrd,dje->jre', rows_in, gathered, preferred_element_type=jnp....]
    all_to_all x0 -> x1, blocking collectives: none -> 13.2 us  [body(): lax.all_to_all(sums, 'expert', split_axis=0, concat_axis=0, tiled=True)]
    convert_element_type x4 -> x0, local copies, waits for them, and re-layouts: 12 us -> none  [the longest x1 8.74 us: body(): jnp.einsum('jrd,jre->dje', rows_in, grad_pre, preferred_element_type=jnp....]
  transfers between devices with their start and end apart: 5 -> 4, of which waited for: 3 -> 2; matrix products, arithmetic and copies ran while one was open for 24% -> 3% of each run, Pallas kernels for 0% -> 3%
where the time goes in v2:
time: 186 us; the launch traced here: 183 us
  blocking collectives  67 us (36%)
  waiting for transfers between devices  43.2 us (23%)
  starting transfers between devices  25.6 us (14%)
  Pallas kernels  18.9 us (10%)
  between operations  14.1 us (8%)
  local copies, waits for them, and re-layouts  9.49 us (5%)
  other arithmetic  4.47 us (2%)
    all_gather x1, blocking collectives, body(): gathered = lax.all_gather(sent, 'dp', axis=0, tiled=True)  53.7 us
    all_to_all x1, waiting for transfers between devices, body(): lax.all_to_all(back, 'expert', split_axis=0, concat_axis=0, tiled=True)  36.6 us
    pallas_call x4, Pallas kernels, call(): pl.pallas_call(kernel, grid=grid, out_shape=[jax.ShapeDtypeStruct(s, t) f...  18.9 us
    all_to_all x1, blocking collectives, body(): lax.all_to_all(sums, 'expert', split_axis=0, concat_axis=0, tiled=True)  13.2 us
    all_to_all x1, starting transfers between devices, body(): lax.all_to_all(packed, 'expert', split_axis=0, concat_axis=0, tiled=True)  10.6 us
    all_to_all x1, starting transfers between devices, body(): lax.all_to_all(jnp.tile(here, (data_ways, 1)), 'dp', split_axis=0, concat...  9.14 us
    unnamed x15, local copies, waits for them, and re-layouts  7.19 us
    all_to_all x1, waiting for transfers between devices, body(): lax.all_to_all(jnp.tile(here, (data_ways, 1)), 'dp', split_axis=0, concat...  6.66 us
  transfers between devices with their start and end apart: 4, of which 2 were waited for; matrix products, arithmetic and copies ran while one was open for 3% of the time, Pallas kernels for 3%

profile of v2, /device:TPU:6, one launch (start us, length us, event | category | flops | bytes accessed | tf_op | source)
XLA Modules:
  0.0 182.8 jit_solution(6298939015461038076)
XLA Ops:
  7.2 0.0 copy-start.2
  7.2 1.1 copy-done.2
  8.3 0.9 copy-done.3
  9.3 0.7 copy-done.4
  9.9 0.7 copy-done.5
  10.6 3.6 %shard_map.76 = (bf16[768,2816]{1,0:T(8,128)(2,1)S(1)}, bf16[1536,128]{1,0:T(8,128)(2,1)S(1)}, f32[32,256]{1,0:T(8,128)S(1)}) custom-call(s32[8,128]{1,0:T(8,128)S(1)} %bitcast.16, f32[8,128]{1,0:T(8,128)S(1)} %bitcast.17, bf16[128,1024]{1,0:T(8,128)(2,1)S(1)} %copy-done.3, bf16[1024,384]{1,0:T(8,128)(2,1)S(1)} %bitcast.15), custom_call_target="tpu_custom_call" | custom-call | flops 1610612736 | bytes 4325376 | tf_op jit(solution)/shard_map/pallas_call | solution.py:137
  14.3 0.0 copy-start
  14.3 2.0 %copy-done = bf16[768,2816]{1,0:T(8,128)(2,1)} copy-done((bf16[768,2816]{1,0:T(8,128)(2,1)}, bf16[768,2816]{1,0:T(8,128)(2,1)S(1)}, u32[]{:S(2)}) %copy-start) | copy-done | bytes 4325400
  16.3 10.6 %all-to-all-start = ((bf16[32,24,2816]{2,1,0:T(8,128)(2,1)}), bf16[32,24,2816]{2,1,0:T(8,128)(2,1)}, u32[]{:S(2)}, u32[]{:S(2)}) async-start(bf16[32,24,2816]{2,1,0:T(8,128)(2,1)} %bitcast.12), calls=%async_computation | async-start | bytes 8650752 | tf_op jit(solution)/shard_map/all_to_all | solution.py:174
  26.9 0.0 reduce-scatter.2.cloned.1.call-start
  26.9 0.0 copy-done.6
  27.0 0.2 multiply_convert_fusion.1
  27.2 0.1 copy.13
  27.2 53.7 %all-gather.1 = f16[1024,1536]{1,0:T(8,128)(2,1)S(1)} all-gather(f16[64,1536]{1,0:T(8,128)(2,1)S(1)} %bitcast.18), channel_id=1, replica_groups=mesh['dp'=16,'expert'=32] {'dp'}, dimensions={0}, use_global_device_ids=true | all-gather | bytes 3342336 | tf_op jit(solution)/shard_map/all_gather | solution.py:175
  81.0 2.3 %multiply_convert_fusion.w_hbm.w_ref = bf16[1024,1536]{1,0:T(8,128)(2,1)} fusion(f16[1024,1536]{1,0:T(8,128)(2,1)S(1)} %all-gather.1), kind=kLoop, calls=%fused_computation | loop fusion | flops 4718592 | bytes 6291456 | tf_op jit(solution)/shard_map/convert_element_type | solution.py:176
  83.3 0.0 all-to-all-done
  83.3 9.4 %shard_map.77 = (bf16[768,1536]{1,0:T(8,128)(2,1)S(1)}, bf16[1024,1536]{1,0:T(8,128)(2,1)}) custom-call(bf16[768,2816]{1,0:T(8,128)(2,1)} %bitcast.4.got_hbm, bf16[1024,1536]{1,0:T(8,128)(2,1)} %multiply_convert_fusion.w_hbm.w_ref), custom_call_target="tpu_custom_call" | custom-call | flops 4831838208 | bytes 9437184 | tf_op jit(solution)/shard_map/pallas_call | solution.py:137
  92.7 0.0 reduce-scatter.2.cloned.1.call-update
  92.8 13.2 %all_to_all.37 = f32[32,1,256]{2,1,0:T(1,128)S(1)} all-to-all(f32[32,1,256]{2,1,0:T(1,128)S(1)} %copy.10), channel_id=1, replica_groups=mesh['dp'=16,'expert'=32] {'expert'}, dimensions={0} | all-to-all | bytes 65536 | tf_op jit(solution)/shard_map/all_to_all | solution.py:214
  106.0 0.1 reduce_sum.18
  106.0 0.6 tile.2
  106.7 9.1 %all-to-all-start.3 = ((f32[16,1,256]{2,1,0:T(1,128)}), f32[16,1,256]{2,1,0:T(1,128)S(1)}, u32[]{:S(2)}, u32[]{:S(2)}) async-start(f32[16,1,256]{2,1,0:T(1,128)} %tile.2), calls=%async_computation.4 | async-start | bytes 32768 | tf_op jit(solution)/shard_map/all_to_all | solution.py:215
  115.8 4.5 %shard_map.78 = bf16[768,2048]{1,0:T(8,128)(2,1)S(1)} custom-call(bf16[768,1536]{1,0:T(8,128)(2,1)S(1)} %get-tuple-element.10.gp_ref, bf16[1024,1536]{1,0:T(8,128)(2,1)} %multiply_convert_fusion.w_hbm.w_ref), custom_call_target="tpu_custom_call" | custom-call | flops 2415919104 | bytes 9437184 | tf_op jit(solution)/shard_map/pallas_call | solution.py:137
  120.4 0.0 copy-start.1
  120.4 1.6 copy-done.1
  122.0 6.7 %all-to-all-done.3 = f32[16,1,256]{2,1,0:T(1,128)S(1)} async-done(((f32[16,1,256]{2,1,0:T(1,128)}), f32[16,1,256]{2,1,0:T(1,128)S(1)}, u32[]{:S(2)}, u32[]{:S(2)}) %all-to-all-start.3) | async-done | bytes 16416 | tf_op jit(solution)/shard_map/all_to_all | solution.py:215
  128.7 5.9 %all-to-all-start.1 = ((bf16[32,24,2048]{2,1,0:T(8,128)(2,1)}), bf16[32,24,2048]{2,1,0:T(8,128)(2,1)S(1)}, u32[]{:S(2)}, u32[]{:S(2)}) async-start(bf16[32,24,2048]{2,1,0:T(8,128)(2,1)} %bitcast.13), calls=%async_computation.1 | async-start | bytes 6291456 | tf_op jit(solution)/shard_map/all_to_all | solution.py:205
  134.6 0.6 reduce_sum.19
  135.1 1.3 multiply_reduce_fusion
  136.5 36.6 %all-to-all-done.1 = bf16[32,24,2048]{2,1,0:T(8,128)(2,1)S(1)} async-done(((bf16[32,24,2048]{2,1,0:T(8,128)(2,1)}), bf16[32,24,2048]{2,1,0:T(8,128)(2,1)S(1)}, u32[]{:S(2)}, u32[]{:S(2)}) %all-to-all-start.1) | async-done | bytes 3145760 | tf_op jit(solution)/shard_map/all_to_all | solution.py:205
  173.0 1.3 shard_map.79
  174.3 1.7 reshape.36
  (6 shorter events, 0.0 us)
Async XLA Ops:
  7.2 1.1 copy-start.2
  8.3 0.9 copy-start.3
  9.2 0.7 copy-start.4
  9.9 0.7 copy-start.5
  14.3 2.0 %copy-start = (bf16[768,2816]{1,0:T(8,128)(2,1)}, bf16[768,2816]{1,0:T(8,128)(2,1)S(1)}, u32[]{:S(2)}) copy-start(bf16[768,2816]{1,0:T(8,128)(2,1)S(1)} %get-tuple-element.9) | copy-start | bytes 12976132
  16.3 10.6 %copy-start.6 = (bf16[64,2,768]{2,1,0:T(2,128)(2,1)S(1)}, bf16[64,2,768]{2,1,0:T(2,128)(2,1)}, u32[]{:S(2)}) copy-start(bf16[64,2,768]{2,1,0:T(2,128)(2,1)} %param.9) | copy-start | bytes 589828
  16.3 67.0 %all-to-all-start = ((bf16[32,24,2816]{2,1,0:T(8,128)(2,1)}), bf16[32,24,2816]{2,1,0:T(8,128)(2,1)}, u32[]{:S(2)}, u32[]{:S(2)}) async-start(bf16[32,24,2816]{2,1,0:T(8,128)(2,1)} %bitcast.12), calls=%async_computation | async-start | bytes 8650752 | tf_op jit(solution)/shard_map/all_to_all | solution.py:174
  26.9 147.4 %reduce-scatter.2.cloned.1.call-start = ((), (), s32[]{:S(2)}) async-start(), calls=%async_computation.5 | async-start | bytes 3342336 | tf_op jit(solution)/shard_map/reduce_scatter | solution.py:194
  106.7 22.0 %all-to-all-start.3 = ((f32[16,1,256]{2,1,0:T(1,128)}), f32[16,1,256]{2,1,0:T(1,128)S(1)}, u32[]{:S(2)}, u32[]{:S(2)}) async-start(f32[16,1,256]{2,1,0:T(1,128)} %tile.2), calls=%async_computation.4 | async-start | bytes 32768 | tf_op jit(solution)/shard_map/all_to_all | solution.py:215
  120.4 1.7 copy-start.1
  128.7 44.3 %all-to-all-start.1 = ((bf16[32,24,2048]{2,1,0:T(8,128)(2,1)}), bf16[32,24,2048]{2,1,0:T(8,128)(2,1)S(1)}, u32[]{:S(2)}, u32[]{:S(2)}) async-start(bf16[32,24,2048]{2,1,0:T(8,128)(2,1)} %bitcast.13), calls=%async_computation.1 | async-start | bytes 6291456 | tf_op jit(solution)/shard_map/all_to_all | solution.py:205
Sparse Core Ops, SparseCore 0:
  92.8 75.6 reduce-scatter.1

commit v3 on v2

--- a/solution.py
+++ b/solution.py
@@ -9,7 +9,7 @@
 
 F32 = jnp.float32
 BF16 = jnp.bfloat16
-VMEM_LIMIT = 48 * 1024 * 1024
+VMEM_LIMIT = 60 * 1024 * 1024
 
 
 def iota(shape, dim):
@@ -27,20 +27,22 @@
     return high, middle, (rest - middle.astype(F32)).astype(BF16)
 
 
-def pack_kernel(per_device, devices, cap, routes_ref, gates_ref, tokens_hbm, cot_hbm, out_ref, picks_ref, sums_ref, tokens_ref, cot_ref, sems):
+def pack_kernel(
+    per_device, devices, cap, routes_hbm, gates_hbm, tokens_hbm, cot_hbm, out_hbm, picks_ref, sums_ref, routes_ref, gates_ref, tokens_ref, cot_ref, out_ref, sems
+):
     topk, tok_count = routes_ref.shape
     model, width = tokens_ref.shape[1], cot_ref.shape[1]
     count, experts = tok_count * topk, per_device * devices
     size = devices * cap
-    copies = [
-        pltpu.make_async_copy(tokens_hbm, tokens_ref, sems.at[0]),
-        pltpu.make_async_copy(cot_hbm, cot_ref, sems.at[1]),
-    ]
+    pairs = [(routes_hbm, routes_ref), (gates_hbm, gates_ref), (tokens_hbm, tokens_ref), (cot_hbm, cot_ref)]
+    copies = [pltpu.make_async_copy(source, target, sems.at[i]) for i, (source, target) in enumerate(pairs)]
     for copy in copies:
         copy.start()
 
     spread = (iota((tok_count, count), 1) // topk == iota((tok_count, count), 0)).astype(F32).astype(BF16)
     own = iota((topk, count), 1) % topk == iota((topk, count), 0)
+    copies[0].wait()
+    copies[1].wait()
     parts = [routes_ref[...].astype(F32).astype(BF16), *split3(gates_ref[...])]
     wide = [jnp.sum(jnp.where(own, dot(part, spread), 0.0), axis=0, keepdims=True) for part in parts]
     routes, gates = wide[0].astype(jnp.int32), (wide[1] + wide[2]) + wide[3]
@@ -62,25 +64,30 @@
     hits = tok_slot[:, None, :] == iota((experts, cap, tok_count), 1)
     picks_ref[...] = hits.astype(F32).reshape(experts * cap, tok_count).astype(BF16)
     step = 256
-    copies[0].wait()
-    for j in range(per_device):
-        for i in range(0, size, step):
+    copies[2].wait()
+    copies[3].wait()
+    outs = []
+    for i in range(0, size, step):
+        for j in range(per_device):
             rows = dot(picks_ref[j * size + i : j * size + i + step, :], tokens_ref[...])
             out_ref[i : i + step, j * model : (j + 1) * model] = rows.astype(BF16)
-    copies[1].wait()
-    for j in range(per_device):
-        for i in range(0, size, step):
+        for j in range(per_device):
             hit = slot == iota((step, 1), 0) + (j * size + i)
             gate = jnp.sum(jnp.where(hit, gates, 0.0), axis=1, keepdims=True)
             rows = dot(hit.astype(F32).astype(BF16), cot_ref[...])
             at = per_device * model + j * width
             out_ref[i : i + step, at : at + width] = (rows * gate).astype(BF16)
-
-
-def grad_kernel(per_device, got_hbm, w_hbm, gp_ref, gw_hbm, got_ref, w_ref, gw_ref, sems):
+        part = pl.ds(i, step)
+        outs.append(pltpu.make_async_copy(out_ref.at[part, :], out_hbm.at[part, :], sems.at[len(pairs) + len(outs)]))
+        outs[-1].start()
+    for copy in outs:
+        copy.wait()
+
+
+def grad_kernel(per_device, got_hbm, w_hbm, gp_hbm, gw_hbm, got_ref, w_ref, gp_ref, gw_ref, sems):
     size, hidden, model = gp_ref.shape[0], gp_ref.shape[1] // per_device, w_ref.shape[0]
     width = hidden // 2
-    step = 256
+    step, half = 256, 128
     tiles = size // step
     rows = [pl.ds(i * step, step) for i in range(tiles)]
     columns = [pl.ds(j * hidden, hidden) for j in range(per_device)]
@@ -97,22 +104,24 @@
     for j in range(per_device):
         w_in[j].wait()
         at = j * hidden
-        for i in range(tiles):
-            if j == 0:
-                got_in[i].wait()
-            pre = dot(got_ref[rows[i], j * model : (j + 1) * model], w_ref[:, columns[j]])
+        for i in range(0, size, half):
+            if j == 0 and i % step == 0:
+                got_in[i // step].wait()
+            here = pl.ds(i, half)
+            pre = dot(got_ref[here, j * model : (j + 1) * model], w_ref[:, columns[j]])
             gate, upper = pre[:, :width], pre[:, width:]
             sigma = jax.nn.sigmoid(gate)
             first = per_device * model + j * width
-            common = got_ref[rows[i], first : first + width].astype(F32) * sigma
-            gp_ref[rows[i], at : at + width] = (common * upper * (1.0 + gate * (1.0 - sigma))).astype(BF16)
-            gp_ref[rows[i], at + width : at + hidden] = (common * gate).astype(BF16)
+            common = got_ref[here, first : first + width].astype(F32) * sigma
+            gp_ref[here, at : at + width] = (common * upper * (1.0 + gate * (1.0 - sigma))).astype(BF16)
+            gp_ref[here, at + width : at + hidden] = (common * gate).astype(BF16)
         for i in range(0, model, step):
             part = got_ref[:, j * model + i : j * model + i + step]
             gw_ref[i : i + step, columns[j]] = dot(part, gp_ref[:, columns[j]], ((0,), (0,))).astype(BF16)
-        copy = pltpu.make_async_copy(gw_ref.at[:, columns[j]], gw_hbm.at[:, columns[j]], sems.at[per_device + tiles + j])
-        copy.start()
-        outs.append(copy)
+        for source, target in ((gp_ref, gp_hbm), (gw_ref, gw_hbm)):
+            at = per_device + tiles + len(outs)
+            outs.append(pltpu.make_async_copy(source.at[:, columns[j]], target.at[:, columns[j]], sems.at[at]))
+            outs[-1].start()
     for copy in outs:
         copy.wait()
 
@@ -157,7 +166,7 @@
     cap = 3 * tok_count * topk // (2 * experts)
     size, count = devices * cap, tok_count * topk
     lanes = per_device * (model + width)
-    vmem, anywhere = pl.BlockSpec(memory_space=pltpu.VMEM), pl.BlockSpec(memory_space=pl.ANY)
+    vmem, hbm = pl.BlockSpec(memory_space=pltpu.VMEM), pl.BlockSpec(memory_space=pltpu.HBM)
 
     lift = 2.0**18
     sent = (gate_up.astype(F32) * lift).astype(jnp.float16).reshape(channels, per_device * hidden)
@@ -166,11 +175,20 @@
         functools.partial(pack_kernel, per_device, devices, cap),
         [((size, lanes), BF16), ((per_device * size, tok_count), BF16), ((devices, per_device * 128), F32)],
         [routes.T, route_gates.T, tokens, route_cotangent.reshape(count, width)],
-        in_specs=[vmem, vmem, anywhere, anywhere],
-        scratch=[pltpu.VMEM((tok_count, model), BF16), pltpu.VMEM((count, width), BF16), pltpu.SemaphoreType.DMA((2,))],
+        in_specs=[hbm] * 4,
+        out_specs=[hbm, vmem, vmem],
+        scratch=[
+            pltpu.VMEM((topk, tok_count), jnp.int32),
+            pltpu.VMEM((topk, tok_count), F32),
+            pltpu.VMEM((tok_count, model), BF16),
+            pltpu.VMEM((count, width), BF16),
+            pltpu.VMEM((size, lanes), BF16),
+            pltpu.SemaphoreType.DMA((4 + size // 256,)),
+        ],
         flops=2 * per_device * size * (tok_count * model + count * width),
         moved=2 * size * lanes,
     )
+    sent, packed = lax.optimization_barrier((sent, packed))
     got = lax.all_to_all(packed, "expert", split_axis=0, concat_axis=0, tiled=True)
     gathered = lax.all_gather(sent, "dp", axis=0, tiled=True)
     full = (gathered.astype(F32) * (1.0 / lift)).astype(BF16)
@@ -180,13 +198,14 @@
         functools.partial(grad_kernel, per_device),
         [((size, per_device * hidden), BF16), ((model, per_device * hidden), BF16)],
         [got, full],
-        in_specs=[anywhere, anywhere],
-        out_specs=[vmem, anywhere],
+        in_specs=[hbm, hbm],
+        out_specs=[hbm, hbm],
         scratch=[
             pltpu.VMEM((size, lanes), BF16),
             pltpu.VMEM((model, per_device * hidden), BF16),
+            pltpu.VMEM((size, per_device * hidden), BF16),
             pltpu.VMEM((model, per_device * hidden), BF16),
-            pltpu.SemaphoreType.DMA((2 * per_device + size // 256,)),
+            pltpu.SemaphoreType.DMA((3 * per_device + size // 256,)),
         ],
         flops=2 * work,
         moved=12 * size * model,
@@ -211,8 +230,10 @@
         moved=4 * size * model,
     )
 
-    here = jnp.sum(lax.all_to_all(sums, "expert", split_axis=0, concat_axis=0, tiled=True), axis=0, keepdims=True)
-    heard = lax.all_to_all(jnp.tile(here, (data_ways, 1)), "dp", split_axis=0, concat_axis=0, tiled=True)
+    sums, _ = lax.optimization_barrier((sums, back))
+    column = lax.psum(sums, "dp")
+    column, _ = lax.optimization_barrier((column, returned))
+    heard = lax.all_to_all(column, "expert", split_axis=0, concat_axis=0, tiled=True)
     totals = jnp.sum(heard, axis=0).reshape(per_device, 128)[:, 0]
     load = totals * (per_device / (tok_count * topk * data_ways))
     return (grad_tokens, mine.reshape(channels, per_device, hidden), load)

time: 186 us -> 186 us (level)
  blocking collectives: 67 us -> 110 us
  waiting for transfers between devices: 43.2 us -> 2.21 us
  local copies, waits for them, and re-layouts: 9.49 us -> 2.42 us
  Pallas kernels: 18.9 us -> 24 us
    psum x0 -> x1, blocking collectives: none -> 56.3 us  [body(): column = lax.psum(sums, 'dp')]
    all_to_all x1, waiting for transfers between devices: 36.6 us -> 0.01 us  [body(): lax.all_to_all(back, 'expert', split_axis=0, concat_axis=0, tiled=True)]
    all_to_all x1 -> x0, blocking collectives: 13.2 us -> none  [body(): lax.all_to_all(sums, 'expert', split_axis=0, concat_axis=0, tiled=True)]
    unnamed x15 -> x5, local copies, waits for them, and re-layouts: 7.19 us -> 0.06 us
    pallas_call x4, Pallas kernels: 18.9 us -> 24 us  [call(): pl.pallas_call(kernel, grid=grid, out_shape=[jax.ShapeDtypeStruct(s, t) f...]
    all_to_all x1, waiting for transfers between devices: 6.66 us -> 2.19 us  [body(): lax.all_to_all(column, 'expert', split_axis=0, concat_axis=0, tiled=True)]
    all_to_all x1, starting transfers between devices: 5.88 us -> 8.13 us  [body(): lax.all_to_all(back, 'expert', split_axis=0, concat_axis=0, tiled=True)]
  transfers between devices with their start and end apart: 4 -> 4, of which waited for: 2 -> 1; matrix products, arithmetic and copies ran while one was open for 3% -> 2% of each run, Pallas kernels for 3% -> 5%
where the time goes in v3:
time: 186 us; the launch traced here: 183 us
  blocking collectives  110 us (59%)
  starting transfers between devices  25.9 us (14%)
  Pallas kernels  24 us (13%)
  between operations  14.1 us (8%)
  other arithmetic  4.14 us (2%)
  local copies, waits for them, and re-layouts  2.42 us (1%)
  waiting for transfers between devices  2.21 us (1%)
    psum x1, blocking collectives, body(): column = lax.psum(sums, 'dp')  56.3 us
    all_gather x1, blocking collectives, body(): gathered = lax.all_gather(sent, 'dp', axis=0, tiled=True)  53.7 us
    pallas_call x4, Pallas kernels, call(): pl.pallas_call(kernel, grid=grid, out_shape=[jax.ShapeDtypeStruct(s, t) f...  24 us
    all_to_all x1, starting transfers between devices, body(): lax.all_to_all(packed, 'expert', split_axis=0, concat_axis=0, tiled=True)  10.5 us
    all_to_all x1, starting transfers between devices, body(): lax.all_to_all(back, 'expert', split_axis=0, concat_axis=0, tiled=True)  8.13 us
    all_to_all x1, starting transfers between devices, body(): lax.all_to_all(column, 'expert', split_axis=0, concat_axis=0, tiled=True)  7.29 us
  transfers between devices with their start and end apart: 4, of which 1 were waited for; matrix products, arithmetic and copies ran while one was open for 2% of the time, Pallas kernels for 5%

profile of v3, /device:TPU:6, one launch (start us, length us, event | category | flops | bytes accessed | tf_op | source)
XLA Modules:
  0.0 182.9 jit_solution(3333117848507230089)
XLA Ops:
  7.2 1.1 multiply_convert_fusion.1
  8.3 0.1 copy.9
  8.4 6.0 %shard_map.76 = (bf16[768,2816]{1,0:T(8,128)(2,1)}, bf16[1536,128]{1,0:T(8,128)(2,1)}, f32[32,256]{1,0:T(8,128)}) custom-call(s32[8,128]{1,0:T(8,128)} %bitcast.19, f32[8,128]{1,0:T(8,128)} %bitcast.20, bf16[128,1024]{1,0:T(8,128)(2,1)} %tokens_hbm.1, bf16[1024,384]{1,0:T(8,128)(2,1)} %bitcast.18), custom_call_target="tpu_custom_call" | custom-call | flops 1610612736 | bytes 4325376 | tf_op jit(solution)/shard_map/pallas_call | solution.py:146
  14.4 10.5 %all-to-all-start = ((bf16[32,24,2816]{2,1,0:T(8,128)(2,1)}), bf16[32,24,2816]{2,1,0:T(8,128)(2,1)}, u32[]{:S(2)}, u32[]{:S(2)}) async-start(bf16[32,24,2816]{2,1,0:T(8,128)(2,1)} %bitcast.12), calls=%async_computation | async-start | bytes 8650752 | tf_op jit(solution)/shard_map/all_to_all | solution.py:192
  24.8 0.0 reduce-scatter.2.cloned.1.call-start
  24.9 53.7 %all-gather.1 = f16[1024,1536]{1,0:T(8,128)(2,1)S(1)} all-gather(f16[64,1536]{1,0:T(8,128)(2,1)S(1)} %bitcast.14), channel_id=1, replica_groups=mesh['dp'=16,'expert'=32] {'dp'}, dimensions={0}, use_global_device_ids=true | all-gather | bytes 3342336 | tf_op jit(solution)/shard_map/all_gather | solution.py:193
  78.6 2.3 %multiply_convert_fusion.w_hbm.w_ref = bf16[1024,1536]{1,0:T(8,128)(2,1)} fusion(f16[1024,1536]{1,0:T(8,128)(2,1)S(1)} %all-gather.1), kind=kLoop, calls=%fused_computation | loop fusion | flops 4718592 | bytes 6291456 | tf_op jit(solution)/shard_map/convert_element_type | solution.py:194
  80.9 0.0 all-to-all-done
  80.9 8.9 %shard_map.77 = (bf16[768,1536]{1,0:T(8,128)(2,1)}, bf16[1024,1536]{1,0:T(8,128)(2,1)}) custom-call(bf16[768,2816]{1,0:T(8,128)(2,1)} %bitcast.4.got_hbm, bf16[1024,1536]{1,0:T(8,128)(2,1)} %multiply_convert_fusion.w_hbm.w_ref), custom_call_target="tpu_custom_call" | custom-call | flops 4831838208 | bytes 9437184 | tf_op jit(solution)/shard_map/pallas_call | solution.py:146
  89.8 0.0 reduce-scatter.2.cloned.1.call-update
  89.8 5.8 %shard_map.78 = bf16[768,2048]{1,0:T(8,128)(2,1)} custom-call(bf16[768,1536]{1,0:T(8,128)(2,1)} %get-tuple-element.16.gp_ref, bf16[1024,1536]{1,0:T(8,128)(2,1)} %multiply_convert_fusion.w_hbm.w_ref), custom_call_target="tpu_custom_call" | custom-call | flops 2415919104 | bytes 9437184 | tf_op jit(solution)/shard_map/pallas_call | solution.py:146
  95.7 0.0 copy-start.1
  95.7 8.1 %all-to-all-start.1 = ((bf16[32,24,2048]{2,1,0:T(8,128)(2,1)}), bf16[32,24,2048]{2,1,0:T(8,128)(2,1)S(1)}, u32[]{:S(2)}, u32[]{:S(2)}) async-start(bf16[32,24,2048]{2,1,0:T(8,128)(2,1)} %bitcast.13), calls=%async_computation.1 | async-start | bytes 6291456 | tf_op jit(solution)/shard_map/all_to_all | solution.py:224
  103.8 0.0 copy-done.1
  103.8 56.3 %psum.7 = f32[32,256]{1,0:T(8,128)S(1)} all-reduce(f32[32,256]{1,0:T(8,128)S(1)} %copy-done.1), channel_id=1, replica_groups=mesh['dp'=16,'expert'=32] {'dp'}, use_global_device_ids=true, to_apply=%region_1.0 | all-reduce | flops 8192 | bytes 65536 | tf_op jit(solution)/shard_map/psum | solution.py:234
  160.1 0.0 all-to-all-done.1
  160.1 0.0 copy-start
  160.1 0.7 copy.8
  160.8 7.3 %all-to-all-start.2 = ((f32[32,1,256]{2,1,0:T(1,128)}), f32[32,1,256]{2,1,0:T(1,128)S(1)}, u32[]{:S(2)}, u32[]{:S(2)}) async-start(f32[32,1,256]{2,1,0:T(1,128)} %copy.8), calls=%async_computation.3 | async-start | bytes 65536 | tf_op jit(solution)/shard_map/all_to_all | solution.py:236
  168.1 0.0 copy-done
  168.2 3.3 %shard_map.79 = bf16[128,1024]{1,0:T(8,128)(2,1)} custom-call(bf16[1536,128]{1,0:T(8,128)(2,1)} %get-tuple-element.12.picks_ref, bf16[768,2048]{1,0:T(8,128)(2,1)} %bitcast.11), custom_call_target="tpu_custom_call" | custom-call | flops 402653184 | bytes 3145728 | tf_op jit(solution)/shard_map/pallas_call | solution.py:146
  171.5 2.2 %all-to-all-done.2 = f32[32,1,256]{2,1,0:T(1,128)S(1)} async-done(((f32[32,1,256]{2,1,0:T(1,128)}), f32[32,1,256]{2,1,0:T(1,128)S(1)}, u32[]{:S(2)}, u32[]{:S(2)}) %all-to-all-start.2) | async-done | bytes 32800 | tf_op jit(solution)/shard_map/all_to_all | solution.py:236
  173.7 0.1 reduce_sum.9
  173.7 0.6 multiply_reduce_fusion
  174.4 0.0 reduce-scatter.2.cloned.1.call-done
  174.4 1.7 reshape.28
Async XLA Ops:
  14.4 66.6 %all-to-all-start = ((bf16[32,24,2816]{2,1,0:T(8,128)(2,1)}), bf16[32,24,2816]{2,1,0:T(8,128)(2,1)}, u32[]{:S(2)}, u32[]{:S(2)}) async-start(bf16[32,24,2816]{2,1,0:T(8,128)(2,1)} %bitcast.12), calls=%async_computation | async-start | bytes 8650752 | tf_op jit(solution)/shard_map/all_to_all | solution.py:192
  24.8 149.5 %reduce-scatter.2.cloned.1.call-start = ((), (), s32[]{:S(2)}) async-start(), calls=%async_computation.4 | async-start | bytes 3342336 | tf_op jit(solution)/shard_map/reduce_scatter | solution.py:213
  95.7 8.1 %copy-start.1 = (f32[32,256]{1,0:T(8,128)S(1)}, f32[32,256]{1,0:T(8,128)}, u32[]{:S(2)}) copy-start(f32[32,256]{1,0:T(8,128)} %get-tuple-element.19) | copy-start | bytes 98308
  95.7 64.5 %all-to-all-start.1 = ((bf16[32,24,2048]{2,1,0:T(8,128)(2,1)}), bf16[32,24,2048]{2,1,0:T(8,128)(2,1)S(1)}, u32[]{:S(2)}, u32[]{:S(2)}) async-start(bf16[32,24,2048]{2,1,0:T(8,128)(2,1)} %bitcast.13), calls=%async_computation.1 | async-start | bytes 6291456 | tf_op jit(solution)/shard_map/all_to_all | solution.py:224
  160.1 8.0 %copy-start = (bf16[32,24,2048]{2,1,0:T(8,128)(2,1)}, bf16[32,24,2048]{2,1,0:T(8,128)(2,1)S(1)}, u32[]{:S(2)}) copy-start(bf16[32,24,2048]{2,1,0:T(8,128)(2,1)S(1)} %all-to-all-done.1) | copy-start | bytes 9437188
  160.8 12.8 %all-to-all-start.2 = ((f32[32,1,256]{2,1,0:T(1,128)}), f32[32,1,256]{2,1,0:T(1,128)S(1)}, u32[]{:S(2)}, u32[]{:S(2)}) async-start(f32[32,1,256]{2,1,0:T(1,128)} %copy.8), calls=%async_computation.3 | async-start | bytes 65536 | tf_op jit(solution)/shard_map/all_to_all | solution.py:236
Sparse Core Ops, SparseCore 0:
  90.0 75.7 reduce-scatter.1

commit v4 on v3

--- a/solution.py
+++ b/solution.py
@@ -28,7 +28,7 @@
 
 
 def pack_kernel(
-    per_device, devices, cap, routes_hbm, gates_hbm, tokens_hbm, cot_hbm, out_hbm, picks_ref, sums_ref, routes_ref, gates_ref, tokens_ref, cot_ref, out_ref, sems
+    per_device, devices, cap, routes_hbm, gates_hbm, tokens_hbm, cot_hbm, out_hbm, picks_ref, routes_ref, gates_ref, tokens_ref, cot_ref, scaled_ref, out_ref, sems
 ):
     topk, tok_count = routes_ref.shape
     model, width = tokens_ref.shape[1], cot_ref.shape[1]
@@ -40,32 +40,41 @@
         copy.start()
 
     spread = (iota((tok_count, count), 1) // topk == iota((tok_count, count), 0)).astype(F32).astype(BF16)
-    own = iota((topk, count), 1) % topk == iota((topk, count), 0)
+    before = (iota((tok_count, tok_count), 0) < iota((tok_count, tok_count), 1)).astype(F32).astype(BF16)
     copies[0].wait()
     copies[1].wait()
-    parts = [routes_ref[...].astype(F32).astype(BF16), *split3(gates_ref[...])]
-    wide = [jnp.sum(jnp.where(own, dot(part, spread), 0.0), axis=0, keepdims=True) for part in parts]
-    routes, gates = wide[0].astype(jnp.int32), (wide[1] + wide[2]) + wide[3]
+    wide = dot(routes_ref[...].astype(F32).astype(BF16), spread)
+    own = iota((topk, count), 1) % topk == iota((topk, count), 0)
+    routes = jnp.sum(jnp.where(own, wide, 0.0), axis=0, keepdims=True).astype(jnp.int32)
+    own = iota((count, topk), 0) % topk == iota((count, topk), 1)
+    tall = sum(dot(spread, part, ((0,), (1,))) for part in split3(gates_ref[...]))
+    gates = jnp.sum(jnp.where(own, tall, 0.0), axis=1, keepdims=True)
 
     row = iota((experts, 1), 0)
     table = routes == (row % devices) * per_device + row // devices
-    tok_table = dot(table.astype(F32).astype(BF16), spread, ((1,), (1,)))
-    before = (iota((tok_count, tok_count), 0) < iota((tok_count, tok_count), 1)).astype(F32).astype(BF16)
+    flags = table.astype(F32).astype(BF16)
+    tok_table = dot(flags, spread, ((1,), (1,)))
     earlier = dot(tok_table.astype(BF16), before)
     tok_slot = jnp.where(tok_table > 0.5, earlier, -1.0).astype(jnp.int32)
     slots = jnp.where(table, (row * cap).astype(F32) + dot(earlier.astype(BF16), spread), 0.0)
     slot = jnp.sum(slots, axis=0, keepdims=True).astype(jnp.int32)
-
-    mark = gates.astype(BF16).astype(F32)
-    sums = jnp.sum(jnp.where(table, mark, 0.0), axis=1, keepdims=True)
-    for j in range(per_device):
-        sums_ref[:, j * 128 : (j + 1) * 128] = jnp.broadcast_to(sums[j * devices : (j + 1) * devices], (devices, 128))
-
     hits = tok_slot[:, None, :] == iota((experts, cap, tok_count), 1)
     picks_ref[...] = hits.astype(F32).reshape(experts * cap, tok_count).astype(BF16)
+
+    mark = jnp.broadcast_to(gates, (count, 128)).astype(BF16)
+    sums = dot(flags, mark)
+    lane = iota((devices, 128), 1)
+    notes = jnp.zeros((devices, 128), F32)
+    for j in range(per_device):
+        for p, part in enumerate(split3(sums[j * devices : (j + 1) * devices])):
+            notes = jnp.where(lane == 3 * j + p, part.astype(F32), notes)
+    notes = jnp.where(iota((devices, cap, 128), 1) == 0, notes[:, None, :], 0.0).reshape(size, 128).astype(BF16)
+
     step = 256
     copies[2].wait()
     copies[3].wait()
+    scaled_ref[...] = (cot_ref[...].astype(F32) * gates).astype(BF16)
+    first, last = per_device * model, per_device * (model + width)
     outs = []
     for i in range(0, size, step):
         for j in range(per_device):
@@ -73,10 +82,9 @@
             out_ref[i : i + step, j * model : (j + 1) * model] = rows.astype(BF16)
         for j in range(per_device):
             hit = slot == iota((step, 1), 0) + (j * size + i)
-            gate = jnp.sum(jnp.where(hit, gates, 0.0), axis=1, keepdims=True)
-            rows = dot(hit.astype(F32).astype(BF16), cot_ref[...])
-            at = per_device * model + j * width
-            out_ref[i : i + step, at : at + width] = (rows * gate).astype(BF16)
+            rows = dot(hit.astype(F32).astype(BF16), scaled_ref[...])
+            out_ref[i : i + step, first + j * width : first + (j + 1) * width] = rows.astype(BF16)
+        out_ref[i : i + step, last:] = notes[i : i + step]
         part = pl.ds(i, step)
         outs.append(pltpu.make_async_copy(out_ref.at[part, :], out_hbm.at[part, :], sems.at[len(pairs) + len(outs)]))
         outs[-1].start()
@@ -165,22 +173,23 @@
     experts = per_device * devices
     cap = 3 * tok_count * topk // (2 * experts)
     size, count = devices * cap, tok_count * topk
-    lanes = per_device * (model + width)
+    lanes = per_device * (model + width) + 128
     vmem, hbm = pl.BlockSpec(memory_space=pltpu.VMEM), pl.BlockSpec(memory_space=pltpu.HBM)
 
     lift = 2.0**18
     sent = (gate_up.astype(F32) * lift).astype(jnp.float16).reshape(channels, per_device * hidden)
 
-    packed, picks, sums = call(
+    packed, picks = call(
         functools.partial(pack_kernel, per_device, devices, cap),
-        [((size, lanes), BF16), ((per_device * size, tok_count), BF16), ((devices, per_device * 128), F32)],
+        [((size, lanes), BF16), ((per_device * size, tok_count), BF16)],
         [routes.T, route_gates.T, tokens, route_cotangent.reshape(count, width)],
         in_specs=[hbm] * 4,
-        out_specs=[hbm, vmem, vmem],
+        out_specs=[hbm, vmem],
         scratch=[
             pltpu.VMEM((topk, tok_count), jnp.int32),
             pltpu.VMEM((topk, tok_count), F32),
             pltpu.VMEM((tok_count, model), BF16),
+            pltpu.VMEM((count, width), BF16),
             pltpu.VMEM((count, width), BF16),
             pltpu.VMEM((size, lanes), BF16),
             pltpu.SemaphoreType.DMA((4 + size // 256,)),
@@ -188,7 +197,6 @@
         flops=2 * per_device * size * (tok_count * model + count * width),
         moved=2 * size * lanes,
     )
-    sent, packed = lax.optimization_barrier((sent, packed))
     got = lax.all_to_all(packed, "expert", split_axis=0, concat_axis=0, tiled=True)
     gathered = lax.all_gather(sent, "dp", axis=0, tiled=True)
     full = (gathered.astype(F32) * (1.0 / lift)).astype(BF16)
@@ -230,11 +238,9 @@
         moved=4 * size * model,
     )
 
-    sums, _ = lax.optimization_barrier((sums, back))
-    column = lax.psum(sums, "dp")
-    column, _ = lax.optimization_barrier((column, returned))
-    heard = lax.all_to_all(column, "expert", split_axis=0, concat_axis=0, tiled=True)
-    totals = jnp.sum(heard, axis=0).reshape(per_device, 128)[:, 0]
+    notes, _ = lax.optimization_barrier((got[:, lanes - 128 :], back))
+    plane = jnp.sum(notes.astype(F32), axis=0, keepdims=True)
+    totals = lax.psum(plane, "dp")[0, : 3 * per_device].reshape(per_device, 3).sum(axis=1)
     load = totals * (per_device / (tok_count * topk * data_ways))
     return (grad_tokens, mine.reshape(channels, per_device, hidden), load)
 

time: 186 us -> 176 us (0.946); the launches traced: 183 us -> 176 us
  blocking collectives: 110 us -> 87.1 us
  waiting for transfers between devices: 2.21 us -> 24.2 us
  starting transfers between devices: 25.9 us -> 18 us
  local copies, waits for them, and re-layouts: 2.42 us -> 4.45 us
    psum x1, blocking collectives: 56.3 us -> 33.4 us  [body(): lax.psum(plane, 'dp')[0, :3 * per_device].reshape(per_device, 3).sum(axis=1)]
    reduce_scatter x1, waiting for transfers between devices: 0.01 us -> 20.8 us  [body(): mine = lax.psum_scatter(part, 'dp', scatter_dimension=0, tiled=True)]
    all_to_all x1 -> x0, starting transfers between devices: 7.29 us -> none  [body(): lax.all_to_all(column, 'expert', split_axis=0, concat_axis=0, tiled=True)]
    all_to_all x1, waiting for transfers between devices: 0.01 us -> 3.37 us  [body(): lax.all_to_all(back, 'expert', split_axis=0, concat_axis=0, tiled=True)]
    all_to_all x1 -> x0, waiting for transfers between devices: 2.19 us -> none  [body(): lax.all_to_all(column, 'expert', split_axis=0, concat_axis=0, tiled=True)]
  transfers between devices with their start and end apart: 4 -> 3, of which waited for: 1 -> 2; matrix products, arithmetic and copies ran while one was open for 2% -> 3% of each run, Pallas kernels for 5% -> 5%
where the time goes in v4:
time: 176 us
  blocking collectives  87.1 us (49%)
  Pallas kernels  24.4 us (14%)
  waiting for transfers between devices  24.2 us (14%)
  starting transfers between devices  18 us (10%)
  between operations  14.1 us (8%)
  local copies, waits for them, and re-layouts  4.45 us (3%)
  other arithmetic  3.32 us (2%)
    all_gather x1, blocking collectives, body(): gathered = lax.all_gather(sent, 'dp', axis=0, tiled=True)  53.7 us
    psum x1, blocking collectives, body(): lax.psum(plane, 'dp')[0, :3 * per_device].reshape(per_device, 3).sum(axis=1)  33.4 us
    pallas_call x4, Pallas kernels, call(): pl.pallas_call(kernel, grid=grid, out_shape=[jax.ShapeDtypeStruct(s, t) f...  24.4 us
    reduce_scatter x1, waiting for transfers between devices, body(): mine = lax.psum_scatter(part, 'dp', scatter_dimension=0, tiled=True)  20.8 us
    all_to_all x1, starting transfers between devices, body(): lax.all_to_all(packed, 'expert', split_axis=0, concat_axis=0, tiled=True)  10.6 us
    all_to_all x1, starting transfers between devices, body(): lax.all_to_all(back, 'expert', split_axis=0, concat_axis=0, tiled=True)  7.4 us
  transfers between devices with their start and end apart: 3, of which 2 were waited for; matrix products, arithmetic and copies ran while one was open for 3% of the time, Pallas kernels for 5%

profile of v4, /device:TPU:6, one launch (start us, length us, event | category | flops | bytes accessed | tf_op | source)
XLA Modules:
  0.0 175.6 jit_solution(7444362024811455408)
XLA Ops:
  7.2 6.3 %shard_map.76 = (bf16[768,2944]{1,0:T(8,128)(2,1)}, bf16[1536,128]{1,0:T(8,128)(2,1)}) custom-call(s32[8,128]{1,0:T(8,128)} %bitcast.17, f32[8,128]{1,0:T(8,128)} %bitcast.18, bf16[128,1024]{1,0:T(8,128)(2,1)} %tokens_hbm.1, bf16[1024,384]{1,0:T(8,128)(2,1)} %bitcast.16), custom_call_target="tpu_custom_call" | custom-call | flops 1610612736 | bytes 4521984 | tf_op jit(solution)/shard_map/pallas_call | solution.py:154
  13.5 0.0 copy-start.1
  13.5 10.6 %all-to-all-start = ((bf16[32,24,2944]{2,1,0:T(8,128)(2,1)}), bf16[32,24,2944]{2,1,0:T(8,128)(2,1)}, u32[]{:S(2)}, u32[]{:S(2)}) async-start(bf16[32,24,2944]{2,1,0:T(8,128)(2,1)} %bitcast.11), calls=%async_computation | async-start | bytes 9043968 | tf_op jit(solution)/shard_map/all_to_all | solution.py:200
  24.1 0.0 reduce-scatter.2.cloned.1.call-start
  24.2 0.0 copy-done.1
  24.2 0.2 multiply_convert_fusion.1
  24.4 0.1 copy.8
  24.4 53.7 %all-gather.1 = f16[1024,1536]{1,0:T(8,128)(2,1)S(1)} all-gather(f16[64,1536]{1,0:T(8,128)(2,1)S(1)} %bitcast.13), channel_id=1, replica_groups=mesh['dp'=16,'expert'=32] {'dp'}, dimensions={0}, use_global_device_ids=true | all-gather | bytes 3342336 | tf_op jit(solution)/shard_map/all_gather | solution.py:201
  78.2 2.4 %multiply_convert_fusion.w_hbm.w_ref = bf16[1024,1536]{1,0:T(8,128)(2,1)} fusion(f16[1024,1536]{1,0:T(8,128)(2,1)S(1)} %all-gather.1), kind=kLoop, calls=%fused_computation | loop fusion | flops 4718592 | bytes 6291456 | tf_op jit(solution)/shard_map/convert_element_type | solution.py:202
  80.6 0.0 all-to-all-done
  80.6 8.8 %shard_map.77 = (bf16[768,1536]{1,0:T(8,128)(2,1)}, bf16[1024,1536]{1,0:T(8,128)(2,1)}) custom-call(bf16[768,2944]{1,0:T(8,128)(2,1)} %bitcast.4.got_hbm, bf16[1024,1536]{1,0:T(8,128)(2,1)} %multiply_convert_fusion.w_hbm.w_ref), custom_call_target="tpu_custom_call" | custom-call | flops 4831838208 | bytes 9437184 | tf_op jit(solution)/shard_map/pallas_call | solution.py:154
  89.4 0.0 reduce-scatter.2.cloned.1.call-update
  89.4 5.8 %shard_map.78 = bf16[768,2048]{1,0:T(8,128)(2,1)} custom-call(bf16[768,1536]{1,0:T(8,128)(2,1)} %get-tuple-element.10.gp_ref, bf16[1024,1536]{1,0:T(8,128)(2,1)} %multiply_convert_fusion.w_hbm.w_ref), custom_call_target="tpu_custom_call" | custom-call | flops 2415919104 | bytes 9437184 | tf_op jit(solution)/shard_map/pallas_call | solution.py:154
  95.3 7.4 %all-to-all-start.1 = ((bf16[32,24,2048]{2,1,0:T(8,128)(2,1)}), bf16[32,24,2048]{2,1,0:T(8,128)(2,1)S(1)}, u32[]{:S(2)}, u32[]{:S(2)}) async-start(bf16[32,24,2048]{2,1,0:T(8,128)(2,1)} %bitcast.12), calls=%async_computation.1 | async-start | bytes 6291456 | tf_op jit(solution)/shard_map/all_to_all | solution.py:232
  102.7 0.9 slice.8
  103.6 0.1 convert_reduce_fusion
  103.7 33.4 %psum.7 = f32[1,128]{1,0:T(1,128)S(1)} all-reduce(f32[1,128]{1,0:T(1,128)S(1)} %bitcast.15), channel_id=1, replica_groups=mesh['dp'=16,'expert'=32] {'dp'}, use_global_device_ids=true, to_apply=%region_2.0 | all-reduce | flops 128 | bytes 1024 | tf_op jit(solution)/shard_map/psum | solution.py:243
  137.1 0.1 reshape_squeeze.3
  137.2 0.1 reduce_sum.19
  137.3 0.5 broadcast_multiply_fusion
  137.8 3.4 %all-to-all-done.1 = bf16[32,24,2048]{2,1,0:T(8,128)(2,1)S(1)} async-done(((bf16[32,24,2048]{2,1,0:T(8,128)(2,1)}), bf16[32,24,2048]{2,1,0:T(8,128)(2,1)S(1)}, u32[]{:S(2)}, u32[]{:S(2)}) %all-to-all-start.1) | async-done | bytes 3145760 | tf_op jit(solution)/shard_map/all_to_all | solution.py:232
  141.2 0.0 copy-start
  141.2 1.7 copy-done
  142.9 3.4 %shard_map.79 = bf16[128,1024]{1,0:T(8,128)(2,1)} custom-call(bf16[1536,128]{1,0:T(8,128)(2,1)} %get-tuple-element.8.picks_ref, bf16[768,2048]{1,0:T(8,128)(2,1)} %bitcast.10), custom_call_target="tpu_custom_call" | custom-call | flops 402653184 | bytes 3145728 | tf_op jit(solution)/shard_map/pallas_call | solution.py:154
  146.3 20.8 %reduce-scatter.2.cloned.1.call-done = bf16[64,1536]{1,0:T(8,128)(2,1)} async-done(((bf16[1024,1536]{1,0:T(8,128)(2,1)}), bf16[64,1536]{1,0:T(8,128)(2,1)}) %reduce-scatter.2.cloned.1.call-update) | async-done | bytes 196624 | tf_op jit(solution)/shard_map/reduce_scatter | solution.py:221
  167.1 1.7 reshape.21
  (1 shorter events, 0.0 us)
Async XLA Ops:
  13.5 10.7 %copy-start.1 = (bf16[64,2,768]{2,1,0:T(2,128)(2,1)S(1)}, bf16[64,2,768]{2,1,0:T(2,128)(2,1)}, u32[]{:S(2)}) copy-start(bf16[64,2,768]{2,1,0:T(2,128)(2,1)} %param.9) | copy-start | bytes 589828
  13.5 67.1 %all-to-all-start = ((bf16[32,24,2944]{2,1,0:T(8,128)(2,1)}), bf16[32,24,2944]{2,1,0:T(8,128)(2,1)}, u32[]{:S(2)}, u32[]{:S(2)}) async-start(bf16[32,24,2944]{2,1,0:T(8,128)(2,1)} %bitcast.11), calls=%async_computation | async-start | bytes 9043968 | tf_op jit(solution)/shard_map/all_to_all | solution.py:200
  24.1 143.0 %reduce-scatter.2.cloned.1.call-start = ((), (), s32[]{:S(2)}) async-start(), calls=%async_computation.3 | async-start | bytes 3342336 | tf_op jit(solution)/shard_map/reduce_scatter | solution.py:221
  95.3 45.9 %all-to-all-start.1 = ((bf16[32,24,2048]{2,1,0:T(8,128)(2,1)}), bf16[32,24,2048]{2,1,0:T(8,128)(2,1)S(1)}, u32[]{:S(2)}, u32[]{:S(2)}) async-start(bf16[32,24,2048]{2,1,0:T(8,128)(2,1)} %bitcast.12), calls=%async_computation.1 | async-start | bytes 6291456 | tf_op jit(solution)/shard_map/all_to_all | solution.py:232
  141.2 1.7 copy-start
Sparse Core Ops, SparseCore 0:
  89.5 77.4 reduce-scatter.1

commit v5 on v4

--- a/solution.py
+++ b/solution.py
@@ -27,20 +27,35 @@
     return high, middle, (rest - middle.astype(F32)).astype(BF16)
 
 
+def slots_of(routes, per_device, devices):
+    topk, tok_count = routes.shape
+    row = iota((per_device * devices, 1), 0)
+    expert = (row % devices) * per_device + row // devices
+    hit = jnp.zeros((per_device * devices, tok_count), F32)
+    for k in range(topk):
+        hit = jnp.where(routes[k : k + 1, :] == expert, 1.0, hit)
+    before = (iota((tok_count, tok_count), 0) < iota((tok_count, tok_count), 1)).astype(F32).astype(BF16)
+    return expert, dot(hit.astype(BF16), before), hit > 0.5
+
+
+def picks_of(tok_slot, cap):
+    experts, tok_count = tok_slot.shape
+    hits = tok_slot[:, None, :] == iota((experts, cap, tok_count), 1)
+    return hits.astype(F32).reshape(experts * cap, tok_count).astype(BF16)
+
+
 def pack_kernel(
-    per_device, devices, cap, routes_hbm, gates_hbm, tokens_hbm, cot_hbm, out_hbm, picks_ref, routes_ref, gates_ref, tokens_ref, cot_ref, scaled_ref, out_ref, sems
+    per_device, devices, cap, routes_hbm, gates_hbm, tokens_hbm, cot_hbm, out_hbm, routes_ref, gates_ref, tokens_ref, cot_ref, scaled_ref, out_ref, sems
 ):
     topk, tok_count = routes_ref.shape
     model, width = tokens_ref.shape[1], cot_ref.shape[1]
-    count, experts = tok_count * topk, per_device * devices
-    size = devices * cap
+    count, size = tok_count * topk, devices * cap
     pairs = [(routes_hbm, routes_ref), (gates_hbm, gates_ref), (tokens_hbm, tokens_ref), (cot_hbm, cot_ref)]
     copies = [pltpu.make_async_copy(source, target, sems.at[i]) for i, (source, target) in enumerate(pairs)]
     for copy in copies:
         copy.start()
 
     spread = (iota((tok_count, count), 1) // topk == iota((tok_count, count), 0)).astype(F32).astype(BF16)
-    before = (iota((tok_count, tok_count), 0) < iota((tok_count, tok_count), 1)).astype(F32).astype(BF16)
     copies[0].wait()
     copies[1].wait()
     wide = dot(routes_ref[...].astype(F32).astype(BF16), spread)
@@ -50,46 +65,45 @@
     tall = sum(dot(spread, part, ((0,), (1,))) for part in split3(gates_ref[...]))
     gates = jnp.sum(jnp.where(own, tall, 0.0), axis=1, keepdims=True)
 
-    row = iota((experts, 1), 0)
-    table = routes == (row % devices) * per_device + row // devices
-    flags = table.astype(F32).astype(BF16)
-    tok_table = dot(flags, spread, ((1,), (1,)))
-    earlier = dot(tok_table.astype(BF16), before)
-    tok_slot = jnp.where(tok_table > 0.5, earlier, -1.0).astype(jnp.int32)
-    slots = jnp.where(table, (row * cap).astype(F32) + dot(earlier.astype(BF16), spread), 0.0)
+    expert, earlier, named = slots_of(routes_ref[...], per_device, devices)
+    tok_slot = jnp.where(named, earlier, -1.0).astype(jnp.int32)
+    row = iota((per_device * devices, 1), 0)
+    slots = jnp.where(routes == expert, (row * cap).astype(F32) + dot(earlier.astype(BF16), spread), 0.0)
     slot = jnp.sum(slots, axis=0, keepdims=True).astype(jnp.int32)
-    hits = tok_slot[:, None, :] == iota((experts, cap, tok_count), 1)
-    picks_ref[...] = hits.astype(F32).reshape(experts * cap, tok_count).astype(BF16)
-
-    mark = jnp.broadcast_to(gates, (count, 128)).astype(BF16)
-    sums = dot(flags, mark)
-    lane = iota((devices, 128), 1)
-    notes = jnp.zeros((devices, 128), F32)
-    for j in range(per_device):
-        for p, part in enumerate(split3(sums[j * devices : (j + 1) * devices])):
-            notes = jnp.where(lane == 3 * j + p, part.astype(F32), notes)
-    notes = jnp.where(iota((devices, cap, 128), 1) == 0, notes[:, None, :], 0.0).reshape(size, 128).astype(BF16)
+    picks = picks_of(tok_slot, cap)
 
     step = 256
     copies[2].wait()
     copies[3].wait()
     scaled_ref[...] = (cot_ref[...].astype(F32) * gates).astype(BF16)
-    first, last = per_device * model, per_device * (model + width)
+    first = per_device * model
     outs = []
     for i in range(0, size, step):
         for j in range(per_device):
-            rows = dot(picks_ref[j * size + i : j * size + i + step, :], tokens_ref[...])
+            rows = dot(picks[j * size + i : j * size + i + step], tokens_ref[...])
             out_ref[i : i + step, j * model : (j + 1) * model] = rows.astype(BF16)
         for j in range(per_device):
             hit = slot == iota((step, 1), 0) + (j * size + i)
             rows = dot(hit.astype(F32).astype(BF16), scaled_ref[...])
             out_ref[i : i + step, first + j * width : first + (j + 1) * width] = rows.astype(BF16)
-        out_ref[i : i + step, last:] = notes[i : i + step]
         part = pl.ds(i, step)
         outs.append(pltpu.make_async_copy(out_ref.at[part, :], out_hbm.at[part, :], sems.at[len(pairs) + len(outs)]))
         outs[-1].start()
     for copy in outs:
         copy.wait()
+
+
+def tally_kernel(per_device, devices, cap, routes_ref, gates_ref, picks_ref, sums_ref):
+    topk, tok_count = routes_ref.shape
+    expert, earlier, named = slots_of(routes_ref[...], per_device, devices)
+    picks_ref[...] = picks_of(jnp.where(named, earlier, -1.0).astype(jnp.int32), cap)
+    mark = gates_ref[...].astype(BF16).astype(F32)
+    sums = jnp.zeros((per_device * devices, 1), F32)
+    for k in range(topk):
+        chosen = jnp.where(routes_ref[k : k + 1, :] == expert, mark[k : k + 1, :], 0.0)
+        sums += jnp.sum(chosen, axis=1, keepdims=True)
+    row, lane = iota((per_device * devices, 128), 0), iota((per_device * devices, 128), 1)
+    sums_ref[...] = jnp.sum(jnp.where(row == lane, sums, 0.0), axis=0, keepdims=True)
 
 
 def grad_kernel(per_device, got_hbm, w_hbm, gp_hbm, gw_hbm, got_ref, w_ref, gp_ref, gw_ref, sems):
@@ -173,18 +187,18 @@
     experts = per_device * devices
     cap = 3 * tok_count * topk // (2 * experts)
     size, count = devices * cap, tok_count * topk
-    lanes = per_device * (model + width) + 128
+    lanes = per_device * (model + width)
     vmem, hbm = pl.BlockSpec(memory_space=pltpu.VMEM), pl.BlockSpec(memory_space=pltpu.HBM)
 
     lift = 2.0**18
     sent = (gate_up.astype(F32) * lift).astype(jnp.float16).reshape(channels, per_device * hidden)
 
-    packed, picks = call(
+    (packed,) = call(
         functools.partial(pack_kernel, per_device, devices, cap),
-        [((size, lanes), BF16), ((per_device * size, tok_count), BF16)],
+        [((size, lanes), BF16)],
         [routes.T, route_gates.T, tokens, route_cotangent.reshape(count, width)],
         in_specs=[hbm] * 4,
-        out_specs=[hbm, vmem],
+        out_specs=[hbm],
         scratch=[
             pltpu.VMEM((topk, tok_count), jnp.int32),
             pltpu.VMEM((topk, tok_count), F32),
@@ -229,6 +243,13 @@
         flops=work,
         moved=12 * size * model,
     )
+    later, _ = lax.optimization_barrier(((routes.T, route_gates.T), back))
+    picks, sums = call(
+        functools.partial(tally_kernel, per_device, devices, cap),
+        [((per_device * size, tok_count), BF16), ((1, 128), F32)],
+        later,
+        moved=2 * per_device * size * tok_count,
+    )
     returned = lax.all_to_all(back, "expert", split_axis=0, concat_axis=0, tiled=True)
     (grad_tokens,) = call(
         functools.partial(sum_kernel, per_device),
@@ -238,9 +259,11 @@
         moved=4 * size * model,
     )
 
-    notes, _ = lax.optimization_barrier((got[:, lanes - 128 :], back))
-    plane = jnp.sum(notes.astype(F32), axis=0, keepdims=True)
-    totals = lax.psum(plane, "dp")[0, : 3 * per_device].reshape(per_device, 3).sum(axis=1)
+    column = lax.psum(sums, "dp")[0, :experts].reshape(per_device, devices).T
+    column = jnp.broadcast_to(column[:, :, None], (devices, per_device, 128)).reshape(devices, per_device * 128)
+    column, _ = lax.optimization_barrier((column, returned))
+    heard = lax.all_to_all(column, "expert", split_axis=0, concat_axis=0, tiled=True)
+    totals = jnp.sum(heard, axis=0).reshape(per_device, 128)[:, 0]
     load = totals * (per_device / (tok_count * topk * data_ways))
     return (grad_tokens, mine.reshape(channels, per_device, hidden), load)
 

time: 176 us -> 173 us (0.983)
  starting transfers between devices: 18 us -> 25 us
  waiting for transfers between devices: 24.2 us -> 17.8 us
  blocking collectives: 87.1 us -> 84.1 us
  local copies, waits for them, and re-layouts: 4.45 us -> 2.69 us
    reduce_scatter x1, waiting for transfers between devices: 20.8 us -> 9.5 us  [body(): mine = lax.psum_scatter(part, 'dp', scatter_dimension=0, tiled=True)]
    all_to_all x0 -> x1, starting transfers between devices: none -> 6.21 us  [body(): lax.all_to_all(column, 'expert', split_axis=0, concat_axis=0, tiled=True)]
    psum x1, blocking collectives: 33.4 us -> 30.3 us  [body(): column = lax.psum(sums, 'dp')[0, :experts].reshape(per_device, devices).T]
    all_to_all x1, waiting for transfers between devices: 3.37 us -> 6.18 us  [body(): lax.all_to_all(back, 'expert', split_axis=0, concat_axis=0, tiled=True)]
    all_to_all x0 -> x1, waiting for transfers between devices: none -> 2.15 us  [body(): lax.all_to_all(column, 'expert', split_axis=0, concat_axis=0, tiled=True)]
    pallas_call x4 -> x5, Pallas kernels: 24.4 us -> 25.2 us  [call(): pl.pallas_call(kernel, grid=grid, out_shape=[jax.ShapeDtypeStruct(s, t) f...]
  transfers between devices with their start and end apart: 3 -> 4, of which waited for: 2 -> 3; matrix products, arithmetic and copies ran while one was open for 3% -> 2% of each run, Pallas kernels for 5% -> 6%
where the time goes in v5:
time: 173 us; the launch traced here: 172 us
  blocking collectives  84.1 us (49%)
  Pallas kernels  25.2 us (15%)
  starting transfers between devices  25 us (14%)
  waiting for transfers between devices  17.8 us (10%)
  between operations  14.1 us (8%)
  other arithmetic  3.21 us (2%)
  local copies, waits for them, and re-layouts  2.69 us (2%)
    all_gather x1, blocking collectives, body(): gathered = lax.all_gather(sent, 'dp', axis=0, tiled=True)  53.8 us
    psum x1, blocking collectives, body(): column = lax.psum(sums, 'dp')[0, :experts].reshape(per_device, devices).T  30.3 us
    pallas_call x5, Pallas kernels, call(): pl.pallas_call(kernel, grid=grid, out_shape=[jax.ShapeDtypeStruct(s, t) f...  25.2 us
    all_to_all x1, starting transfers between devices, body(): lax.all_to_all(packed, 'expert', split_axis=0, concat_axis=0, tiled=True)  10.6 us
    reduce_scatter x1, waiting for transfers between devices, body(): mine = lax.psum_scatter(part, 'dp', scatter_dimension=0, tiled=True)  9.5 us
    all_to_all x1, starting transfers between devices, body(): lax.all_to_all(back, 'expert', split_axis=0, concat_axis=0, tiled=True)  8.13 us
    all_to_all x1, starting transfers between devices, body(): lax.all_to_all(column, 'expert', split_axis=0, concat_axis=0, tiled=True)  6.21 us
    all_to_all x1, waiting for transfers between devices, body(): lax.all_to_all(back, 'expert', split_axis=0, concat_axis=0, tiled=True)  6.18 us
  transfers between devices with their start and end apart: 4, of which 3 were waited for; matrix products, arithmetic and copies ran while one was open for 2% of the time, Pallas kernels for 6%

profile of v5, /device:TPU:6, one launch (start us, length us, event | category | flops | bytes accessed | tf_op | source)
XLA Modules:
  0.0 172.2 jit_solution(15971131401593850196)
XLA Ops:
  7.2 5.5 %shard_map.76 = bf16[768,2816]{1,0:T(8,128)(2,1)} custom-call(s32[8,128]{1,0:T(8,128)} %bitcast.22, f32[8,128]{1,0:T(8,128)} %bitcast.24, bf16[128,1024]{1,0:T(8,128)(2,1)} %tokens_hbm.1, bf16[1024,384]{1,0:T(8,128)(2,1)} %bitcast.28), custom_call_target="tpu_custom_call" | custom-call | flops 1610612736 | bytes 4325376 | tf_op jit(solution)/shard_map/pallas_call | solution.py:168
  12.6 0.0 copy-start.1
  12.7 10.6 %all-to-all-start = ((bf16[32,24,2816]{2,1,0:T(8,128)(2,1)}), bf16[32,24,2816]{2,1,0:T(8,128)(2,1)}, u32[]{:S(2)}, u32[]{:S(2)}) async-start(bf16[32,24,2816]{2,1,0:T(8,128)(2,1)} %bitcast.16), calls=%async_computation | async-start | bytes 8650752 | tf_op jit(solution)/shard_map/all_to_all | solution.py:214
  23.2 0.0 reduce-scatter.2.cloned.1.call-start
  23.3 0.0 copy-done.1
  23.3 0.2 multiply_convert_fusion.1
  23.5 0.1 copy.12
  23.6 53.8 %all-gather.1 = f16[1024,1536]{1,0:T(8,128)(2,1)S(1)} all-gather(f16[64,1536]{1,0:T(8,128)(2,1)S(1)} %bitcast.18), channel_id=1, replica_groups=mesh['dp'=16,'expert'=32] {'dp'}, dimensions={0}, use_global_device_ids=true | all-gather | bytes 3342336 | tf_op jit(solution)/shard_map/all_gather | solution.py:215
  77.4 2.3 %multiply_convert_fusion.w_hbm.w_ref = bf16[1024,1536]{1,0:T(8,128)(2,1)} fusion(f16[1024,1536]{1,0:T(8,128)(2,1)S(1)} %all-gather.1), kind=kLoop, calls=%fused_computation | loop fusion | flops 4718592 | bytes 6291456 | tf_op jit(solution)/shard_map/convert_element_type | solution.py:216
  79.7 0.0 all-to-all-done
  79.7 8.8 %shard_map.77 = (bf16[768,1536]{1,0:T(8,128)(2,1)}, bf16[1024,1536]{1,0:T(8,128)(2,1)}) custom-call(bf16[768,2816]{1,0:T(8,128)(2,1)} %bitcast.4.got_hbm, bf16[1024,1536]{1,0:T(8,128)(2,1)} %multiply_convert_fusion.w_hbm.w_ref), custom_call_target="tpu_custom_call" | custom-call | flops 4831838208 | bytes 9437184 | tf_op jit(solution)/shard_map/pallas_call | solution.py:168
  88.5 0.0 reduce-scatter.2.cloned.1.call-update
  88.5 5.8 %shard_map.78 = bf16[768,2048]{1,0:T(8,128)(2,1)} custom-call(bf16[768,1536]{1,0:T(8,128)(2,1)} %get-tuple-element.10.gp_ref, bf16[1024,1536]{1,0:T(8,128)(2,1)} %multiply_convert_fusion.w_hbm.w_ref), custom_call_target="tpu_custom_call" | custom-call | flops 2415919104 | bytes 9437184 | tf_op jit(solution)/shard_map/pallas_call | solution.py:168
  94.4 8.1 %all-to-all-start.1 = ((bf16[32,24,2048]{2,1,0:T(8,128)(2,1)}), bf16[32,24,2048]{2,1,0:T(8,128)(2,1)S(1)}, u32[]{:S(2)}, u32[]{:S(2)}) async-start(bf16[32,24,2048]{2,1,0:T(8,128)(2,1)} %bitcast.17), calls=%async_computation.1 | async-start | bytes 6291456 | tf_op jit(solution)/shard_map/all_to_all | solution.py:253
  102.5 1.7 shard_map.79
  104.2 30.3 %psum.7 = f32[1,128]{1,0:T(1,128)S(1)} all-reduce(f32[1,128]{1,0:T(1,128)} %get-tuple-element.15), channel_id=1, replica_groups=mesh['dp'=16,'expert'=32] {'dp'}, use_global_device_ids=true, to_apply=%region_1.0 | all-reduce | flops 128 | bytes 1024 | tf_op jit(solution)/shard_map/psum | solution.py:262
  134.6 0.1 reshape_squeeze.3
  134.7 0.1 copy.11
  134.8 0.1 broadcast_in_dim.2
  134.9 6.2 %all-to-all-done.1 = bf16[32,24,2048]{2,1,0:T(8,128)(2,1)S(1)} async-done(((bf16[32,24,2048]{2,1,0:T(8,128)(2,1)}), bf16[32,24,2048]{2,1,0:T(8,128)(2,1)S(1)}, u32[]{:S(2)}, u32[]{:S(2)}) %all-to-all-start.1) | async-done | bytes 3145760 | tf_op jit(solution)/shard_map/all_to_all | solution.py:253
  141.0 0.0 copy-start
  141.0 0.7 all_to_all.26
  141.7 6.2 %all-to-all-start.2 = ((f32[32,1,256]{2,1,0:T(1,128)}), f32[32,1,256]{2,1,0:T(1,128)S(1)}, u32[]{:S(2)}, u32[]{:S(2)}) async-start(f32[32,1,256]{2,1,0:T(1,128)} %all_to_all.26), calls=%async_computation.3 | async-start | bytes 65536 | tf_op jit(solution)/shard_map/all_to_all | solution.py:265
  148.0 0.0 copy-done
  148.0 3.4 %shard_map.80 = bf16[128,1024]{1,0:T(8,128)(2,1)} custom-call(bf16[1536,128]{1,0:T(8,128)(2,1)} %get-tuple-element.13.picks_ref, bf16[768,2048]{1,0:T(8,128)(2,1)} %bitcast.15), custom_call_target="tpu_custom_call" | custom-call | flops 402653184 | bytes 3145728 | tf_op jit(solution)/shard_map/pallas_call | solution.py:168
  151.3 2.1 %all-to-all-done.2 = f32[32,1,256]{2,1,0:T(1,128)S(1)} async-done(((f32[32,1,256]{2,1,0:T(1,128)}), f32[32,1,256]{2,1,0:T(1,128)S(1)}, u32[]{:S(2)}, u32[]{:S(2)}) %all-to-all-start.2) | async-done | bytes 32800 | tf_op jit(solution)/shard_map/all_to_all | solution.py:265
  153.5 0.1 reduce_sum.9
  153.5 0.6 multiply_reduce_fusion
  154.2 9.5 %reduce-scatter.2.cloned.1.call-done = bf16[64,1536]{1,0:T(8,128)(2,1)} async-done(((bf16[1024,1536]{1,0:T(8,128)(2,1)}), bf16[64,1536]{1,0:T(8,128)(2,1)}) %reduce-scatter.2.cloned.1.call-update) | async-done | bytes 196624 | tf_op jit(solution)/shard_map/reduce_scatter | solution.py:235
  163.7 1.7 reshape.32
  (2 shorter events, 0.0 us)
Async XLA Ops:
  12.6 10.7 %copy-start.1 = (bf16[64,2,768]{2,1,0:T(2,128)(2,1)S(1)}, bf16[64,2,768]{2,1,0:T(2,128)(2,1)}, u32[]{:S(2)}) copy-start(bf16[64,2,768]{2,1,0:T(2,128)(2,1)} %param.9) | copy-start | bytes 589828
  12.7 67.0 %all-to-all-start = ((bf16[32,24,2816]{2,1,0:T(8,128)(2,1)}), bf16[32,24,2816]{2,1,0:T(8,128)(2,1)}, u32[]{:S(2)}, u32[]{:S(2)}) async-start(bf16[32,24,2816]{2,1,0:T(8,128)(2,1)} %bitcast.16), calls=%async_computation | async-start | bytes 8650752 | tf_op jit(solution)/shard_map/all_to_all | solution.py:214
  23.2 140.4 %reduce-scatter.2.cloned.1.call-start = ((), (), s32[]{:S(2)}) async-start(), calls=%async_computation.4 | async-start | bytes 3342336 | tf_op jit(solution)/shard_map/reduce_scatter | solution.py:235
  94.4 46.7 %all-to-all-start.1 = ((bf16[32,24,2048]{2,1,0:T(8,128)(2,1)}), bf16[32,24,2048]{2,1,0:T(8,128)(2,1)S(1)}, u32[]{:S(2)}, u32[]{:S(2)}) async-start(bf16[32,24,2048]{2,1,0:T(8,128)(2,1)} %bitcast.17), calls=%async_computation.1 | async-start | bytes 6291456 | tf_op jit(solution)/shard_map/all_to_all | solution.py:253
  141.0 6.9 %copy-start = (bf16[32,24,2048]{2,1,0:T(8,128)(2,1)}, bf16[32,24,2048]{2,1,0:T(8,128)(2,1)S(1)}, u32[]{:S(2)}) copy-start(bf16[32,24,2048]{2,1,0:T(8,128)(2,1)S(1)} %all-to-all-done.1) | copy-start | bytes 9437188
  141.7 11.8 %all-to-all-start.2 = ((f32[32,1,256]{2,1,0:T(1,128)}), f32[32,1,256]{2,1,0:T(1,128)S(1)}, u32[]{:S(2)}, u32[]{:S(2)}) async-start(f32[32,1,256]{2,1,0:T(1,128)} %all_to_all.26), calls=%async_computation.3 | async-start | bytes 65536 | tf_op jit(solution)/shard_map/all_to_all | solution.py:265
Sparse Core Ops, SparseCore 0:
  88.7 74.9 reduce-scatter.1

commit v6 on v5

--- a/solution.py
+++ b/solution.py
@@ -10,6 +10,7 @@
 F32 = jnp.float32
 BF16 = jnp.bfloat16
 VMEM_LIMIT = 60 * 1024 * 1024
+ROOM = 32 * 1024 * 1024
 
 
 def iota(shape, dim):
@@ -78,17 +79,22 @@
     scaled_ref[...] = (cot_ref[...].astype(F32) * gates).astype(BF16)
     first = per_device * model
     outs = []
+
+    def send(i, at, lanes):
+        here = (pl.ds(i, step), pl.ds(at, lanes))
+        outs.append(pltpu.make_async_copy(out_ref.at[here], out_hbm.at[here], sems.at[len(pairs) + len(outs)]))
+        outs[-1].start()
+
     for i in range(0, size, step):
         for j in range(per_device):
             rows = dot(picks[j * size + i : j * size + i + step], tokens_ref[...])
             out_ref[i : i + step, j * model : (j + 1) * model] = rows.astype(BF16)
+        send(i, 0, first)
         for j in range(per_device):
             hit = slot == iota((step, 1), 0) + (j * size + i)
             rows = dot(hit.astype(F32).astype(BF16), scaled_ref[...])
             out_ref[i : i + step, first + j * width : first + (j + 1) * width] = rows.astype(BF16)
-        part = pl.ds(i, step)
-        outs.append(pltpu.make_async_copy(out_ref.at[part, :], out_hbm.at[part, :], sems.at[len(pairs) + len(outs)]))
-        outs[-1].start()
+        send(i, first, per_device * width)
     for copy in outs:
         copy.wait()
 
@@ -106,52 +112,81 @@
     sums_ref[...] = jnp.sum(jnp.where(row == lane, sums, 0.0), axis=0, keepdims=True)
 
 
-def grad_kernel(per_device, got_hbm, w_hbm, gp_hbm, gw_hbm, got_ref, w_ref, gp_ref, gw_ref, sems):
-    size, hidden, model = gp_ref.shape[0], gp_ref.shape[1] // per_device, w_ref.shape[0]
-    width = hidden // 2
-    step, half = 256, 128
-    tiles = size // step
-    rows = [pl.ds(i * step, step) for i in range(tiles)]
-    columns = [pl.ds(j * hidden, hidden) for j in range(per_device)]
-    w_in = [
-        pltpu.make_async_copy(w_hbm.at[:, columns[j]], w_ref.at[:, columns[j]], sems.at[j]) for j in range(per_device)
+def starter(sems):
+    copies = []
+
+    def start(source, target):
+        copies.append(pltpu.make_async_copy(source, target, sems.at[len(copies)]))
+        copies[-1].start()
+        return copies[-1]
+
+    return start
+
+
+def fetch_rows(start, got_hbm, got_ref, per_device, model, width, step):
+    return [
+        [
+            start(got_hbm.at[pl.ds(i, step), pl.ds(at, count)], got_ref.at[pl.ds(i, step), pl.ds(at, count)])
+            for at, count in ((j * model, model), (per_device * model + j * width, width))
+        ]
+        for j in range(per_device)
+        for i in range(0, got_ref.shape[0], step)
     ]
-    got_in = [
-        pltpu.make_async_copy(got_hbm.at[rows[i], :], got_ref.at[rows[i], :], sems.at[per_device + i])
-        for i in range(tiles)
-    ]
-    for copy in (w_in[0], *got_in, *w_in[1:]):
-        copy.start()
+
+
+def swiglu_grads(got_ref, w_ref, gp_ref, per_device, j, start, rows):
+    model, hidden = w_ref.shape[0], w_ref.shape[1] // per_device
+    width, here, at = hidden // 2, pl.ds(start, rows), j * hidden
+    pre = dot(got_ref[here, j * model : (j + 1) * model], w_ref[:, at : at + hidden])
+    gate, upper = pre[:, :width], pre[:, width:]
+    sigma = jax.nn.sigmoid(gate)
+    first = per_device * model + j * width
+    common = got_ref[here, first : first + width].astype(F32) * sigma
+    gp_ref[here, at : at + width] = (common * upper * (1.0 + gate * (1.0 - sigma))).astype(BF16)
+    gp_ref[here, at + width : at + hidden] = (common * gate).astype(BF16)
+
+
+def grad_kernel(per_device, got_hbm, w_ref, gw_hbm, got_ref, gp_ref, gw_ref, sems):
+    model, hidden = w_ref.shape[0], w_ref.shape[1] // per_device
+    size, step, half = got_ref.shape[0], 256, 128
+    start = starter(sems)
+    got_in = iter(fetch_rows(start, got_hbm, got_ref, per_device, model, hidden // 2, step))
     outs = []
     for j in range(per_device):
-        w_in[j].wait()
         at = j * hidden
         for i in range(0, size, half):
-            if j == 0 and i % step == 0:
-                got_in[i // step].wait()
-            here = pl.ds(i, half)
-            pre = dot(got_ref[here, j * model : (j + 1) * model], w_ref[:, columns[j]])
-            gate, upper = pre[:, :width], pre[:, width:]
-            sigma = jax.nn.sigmoid(gate)
-            first = per_device * model + j * width
-            common = got_ref[here, first : first + width].astype(F32) * sigma
-            gp_ref[here, at : at + width] = (common * upper * (1.0 + gate * (1.0 - sigma))).astype(BF16)
-            gp_ref[here, at + width : at + hidden] = (common * gate).astype(BF16)
+            if i % step == 0:
+                for copy in next(got_in):
+                    copy.wait()
+            swiglu_grads(got_ref, w_ref, gp_ref, per_device, j, i, half)
         for i in range(0, model, step):
             part = got_ref[:, j * model + i : j * model + i + step]
-            gw_ref[i : i + step, columns[j]] = dot(part, gp_ref[:, columns[j]], ((0,), (0,))).astype(BF16)
-        for source, target in ((gp_ref, gp_hbm), (gw_ref, gw_hbm)):
-            at = per_device + tiles + len(outs)
-            outs.append(pltpu.make_async_copy(source.at[:, columns[j]], target.at[:, columns[j]], sems.at[at]))
-            outs[-1].start()
+            gw_ref[i : i + step, at : at + hidden] = dot(part, gp_ref[:, at : at + hidden], ((0,), (0,))).astype(BF16)
+            here = (pl.ds(i, step), pl.ds(at, hidden))
+            outs.append(start(gw_ref.at[here], gw_hbm.at[here]))
     for copy in outs:
         copy.wait()
 
 
-def route_kernel(gp_ref, w_ref, out_ref):
-    step = 256
-    for i in range(0, gp_ref.shape[0], step):
-        out_ref[i : i + step, :] = dot(gp_ref[i : i + step, :], w_ref[...], ((1,), (1,))).astype(BF16)
+def route_kernel(per_device, got_hbm, w_ref, back_hbm, got_ref, gp_ref, back_ref, sems):
+    model, hidden = w_ref.shape[0], w_ref.shape[1] // per_device
+    size, step = got_ref.shape[0], 256
+    start = starter(sems)
+    got_in = iter(fetch_rows(start, got_hbm, got_ref, per_device, model, hidden // 2, step))
+    outs = []
+    for j in range(per_device):
+        at = j * hidden
+        for i in range(0, size, step):
+            for copy in next(got_in):
+                copy.wait()
+            for half in (0, step // 2):
+                swiglu_grads(got_ref, w_ref, gp_ref, per_device, j, i + half, step // 2)
+            here = (pl.ds(i, step), pl.ds(j * model, model))
+            rows = dot(gp_ref[i : i + step, at : at + hidden], w_ref[:, at : at + hidden], ((1,), (1,)))
+            back_ref[i : i + step, j * model : (j + 1) * model] = rows.astype(BF16)
+            outs.append(start(back_ref.at[here], back_hbm.at[here]))
+    for copy in outs:
+        copy.wait()
 
 
 def sum_kernel(per_device, picks_ref, back_ref, out_ref):
@@ -163,7 +198,7 @@
     out_ref[...] = total.astype(BF16)
 
 
-def call(kernel, outs, args, in_specs=None, out_specs=None, grid=(), scratch=(), flops=0, moved=0):
+def call(kernel, outs, args, in_specs=None, out_specs=None, grid=(), scratch=(), flops=0, moved=0, room=VMEM_LIMIT):
     whole = pl.BlockSpec(memory_space=pltpu.VMEM)
     return pl.pallas_call(
         kernel,
@@ -172,7 +207,7 @@
         in_specs=in_specs or [whole] * len(args),
         out_specs=out_specs or [whole] * len(outs),
         scratch_shapes=scratch,
-        compiler_params=pltpu.CompilerParams(vmem_limit_bytes=VMEM_LIMIT),
+        compiler_params=pltpu.CompilerParams(vmem_limit_bytes=room),
         cost_estimate=pl.CostEstimate(flops=flops, bytes_accessed=moved, transcendentals=0),
     )(*args)
 
@@ -206,7 +241,7 @@
             pltpu.VMEM((count, width), BF16),
             pltpu.VMEM((count, width), BF16),
             pltpu.VMEM((size, lanes), BF16),
-            pltpu.SemaphoreType.DMA((4 + size // 256,)),
+            pltpu.SemaphoreType.DMA((4 + 2 * (size // 256),)),
         ],
         flops=2 * per_device * size * (tok_count * model + count * width),
         moved=2 * size * lanes,
@@ -216,32 +251,34 @@
     full = (gathered.astype(F32) * (1.0 / lift)).astype(BF16)
 
     work = 2 * per_device * size * model * hidden
-    grad_pre, part = call(
+    tiles = size // 256
+    held = [pltpu.VMEM((size, lanes), BF16), pltpu.VMEM((size, per_device * hidden), BF16)]
+    (part,) = call(
         functools.partial(grad_kernel, per_device),
-        [((size, per_device * hidden), BF16), ((model, per_device * hidden), BF16)],
+        [((model, per_device * hidden), BF16)],
         [got, full],
-        in_specs=[hbm, hbm],
-        out_specs=[hbm, hbm],
+        in_specs=[hbm, vmem],
+        out_specs=[hbm],
         scratch=[
-            pltpu.VMEM((size, lanes), BF16),
+            *held,
             pltpu.VMEM((model, per_device * hidden), BF16),
-            pltpu.VMEM((size, per_device * hidden), BF16),
-            pltpu.VMEM((model, per_device * hidden), BF16),
-            pltpu.SemaphoreType.DMA((3 * per_device + size // 256,)),
+            pltpu.SemaphoreType.DMA((per_device * (2 * tiles + model // 256),)),
         ],
         flops=2 * work,
         moved=12 * size * model,
+        room=ROOM,
     )
     mine = lax.psum_scatter(part, "dp", scatter_dimension=0, tiled=True)
     (back,) = call(
-        route_kernel,
+        functools.partial(route_kernel, per_device),
         [((size, per_device * model), BF16)],
-        [grad_pre, full],
-        in_specs=[pl.BlockSpec((size, hidden), lambda j: (0, j)), pl.BlockSpec((model, hidden), lambda j: (0, j))],
-        out_specs=[pl.BlockSpec((size, model), lambda j: (0, j))],
-        grid=(per_device,),
-        flops=work,
+        [got, full],
+        in_specs=[hbm, vmem],
+        out_specs=[hbm],
+        scratch=[*held, pltpu.VMEM((size, per_device * model), BF16), pltpu.SemaphoreType.DMA((3 * per_device * tiles,))],
+        flops=2 * work,
         moved=12 * size * model,
+        room=ROOM,
     )
     later, _ = lax.optimization_barrier(((routes.T, route_gates.T), back))
     picks, sums = call(

time: 173 us -> 172 us (level)
  waiting for transfers between devices: 17.8 us -> 15.5 us
  blocking collectives: 84.1 us -> 86 us
    all_to_all x1, waiting for transfers between devices: 6.18 us -> 4.39 us  [body(): lax.all_to_all(back, 'expert', split_axis=0, concat_axis=0, tiled=True)]
    psum x1, blocking collectives: 30.3 us -> 32.1 us  [body(): column = lax.psum(sums, 'dp')[0, :experts].reshape(per_device, devices).T]
  transfers between devices with their start and end apart: 4 -> 4, of which waited for: 3 -> 3; matrix products, arithmetic and copies ran while one was open for 2% -> 1% of each run, Pallas kernels for 6% -> 8%
where the time goes in v6:
time: 172 us
  blocking collectives  86 us (50%)
  Pallas kernels  26.9 us (16%)
  starting transfers between devices  24.8 us (14%)
  waiting for transfers between devices  15.5 us (9%)
  between operations  14.1 us (8%)
  local copies, waits for them, and re-layouts  2.71 us (2%)
    all_gather x1, blocking collectives, body(): gathered = lax.all_gather(sent, 'dp', axis=0, tiled=True)  53.9 us
    psum x1, blocking collectives, body(): column = lax.psum(sums, 'dp')[0, :experts].reshape(per_device, devices).T  32.1 us
    pallas_call x5, Pallas kernels, call(): pl.pallas_call(kernel, grid=grid, out_shape=[jax.ShapeDtypeStruct(s, t) f...  26.9 us
    all_to_all x1, starting transfers between devices, body(): lax.all_to_all(packed, 'expert', split_axis=0, concat_axis=0, tiled=True)  10.6 us
    reduce_scatter x1, waiting for transfers between devices, body(): mine = lax.psum_scatter(part, 'dp', scatter_dimension=0, tiled=True)  8.87 us
    all_to_all x1, starting transfers between devices, body(): lax.all_to_all(back, 'expert', split_axis=0, concat_axis=0, tiled=True)  7.92 us
    all_to_all x1, starting transfers between devices, body(): lax.all_to_all(column, 'expert', split_axis=0, concat_axis=0, tiled=True)  6.22 us
    all_to_all x1, waiting for transfers between devices, body(): lax.all_to_all(back, 'expert', split_axis=0, concat_axis=0, tiled=True)  4.39 us
  transfers between devices with their start and end apart: 4, of which 3 were waited for; matrix products, arithmetic and copies ran while one was open for 1% of the time, Pallas kernels for 8%

profile of v6, /device:TPU:6, one launch (start us, length us, event | category | flops | bytes accessed | tf_op | source)
XLA Modules:
  0.0 171.5 jit_solution(9571265963848459860)
XLA Ops:
  7.2 5.2 %shard_map.76 = bf16[768,2816]{1,0:T(8,128)(2,1)} custom-call(s32[8,128]{1,0:T(8,128)} %bitcast.21, f32[8,128]{1,0:T(8,128)} %bitcast.23, bf16[128,1024]{1,0:T(8,128)(2,1)} %tokens_hbm.1, bf16[1024,384]{1,0:T(8,128)(2,1)} %bitcast.27), custom_call_target="tpu_custom_call" | custom-call | flops 1610612736 | bytes 4325376 | tf_op jit(solution)/shard_map/pallas_call | solution.py:203
  12.3 0.0 copy-start.1
  12.3 10.6 %all-to-all-start = ((bf16[32,24,2816]{2,1,0:T(8,128)(2,1)}), bf16[32,24,2816]{2,1,0:T(8,128)(2,1)}, u32[]{:S(2)}, u32[]{:S(2)}) async-start(bf16[32,24,2816]{2,1,0:T(8,128)(2,1)} %bitcast.16), calls=%async_computation | async-start | bytes 8650752 | tf_op jit(solution)/shard_map/all_to_all | solution.py:249
  22.9 0.0 reduce-scatter.2.cloned.1.call-start
  23.0 0.0 copy-done.1
  23.0 0.2 multiply_convert_fusion.1
  23.2 0.1 copy.12
  23.3 53.9 %all-gather.1 = f16[1024,1536]{1,0:T(8,128)(2,1)S(1)} all-gather(f16[64,1536]{1,0:T(8,128)(2,1)S(1)} %bitcast.17), channel_id=1, replica_groups=mesh['dp'=16,'expert'=32] {'dp'}, dimensions={0}, use_global_device_ids=true | all-gather | bytes 3342336 | tf_op jit(solution)/shard_map/all_gather | solution.py:250
  77.2 0.6 multiply_convert_fusion.w_ref
  77.8 0.0 all-to-all-done
  77.8 8.1 %shard_map.80 = bf16[1024,1536]{1,0:T(8,128)(2,1)} custom-call(bf16[768,2816]{1,0:T(8,128)(2,1)} %bitcast.4.got_hbm, bf16[1024,1536]{1,0:T(8,128)(2,1)S(1)} %multiply_convert_fusion.w_ref), custom_call_target="tpu_custom_call" | custom-call | flops 4831838208 | bytes 9437184 | tf_op jit(solution)/shard_map/pallas_call | solution.py:203
  85.9 0.0 reduce-scatter.2.cloned.1.call-update
  85.9 8.6 %shard_map.77 = bf16[768,2048]{1,0:T(8,128)(2,1)} custom-call(bf16[768,2816]{1,0:T(8,128)(2,1)} %bitcast.4.got_hbm, bf16[1024,1536]{1,0:T(8,128)(2,1)S(1)} %multiply_convert_fusion.w_ref), custom_call_target="tpu_custom_call" | custom-call | flops 4831838208 | bytes 9437184 | tf_op jit(solution)/shard_map/pallas_call | solution.py:203
  94.5 7.9 %all-to-all-start.1 = ((bf16[32,24,2048]{2,1,0:T(8,128)(2,1)}), bf16[32,24,2048]{2,1,0:T(8,128)(2,1)S(1)}, u32[]{:S(2)}, u32[]{:S(2)}) async-start(bf16[32,24,2048]{2,1,0:T(8,128)(2,1)} %bitcast.5), calls=%async_computation.1 | async-start | bytes 6291456 | tf_op jit(solution)/shard_map/all_to_all | solution.py:290
  102.5 1.7 shard_map.78
  104.2 32.1 %psum.7 = f32[1,128]{1,0:T(1,128)S(1)} all-reduce(f32[1,128]{1,0:T(1,128)} %get-tuple-element.11), channel_id=1, replica_groups=mesh['dp'=16,'expert'=32] {'dp'}, use_global_device_ids=true, to_apply=%region_1.0 | all-reduce | flops 128 | bytes 1024 | tf_op jit(solution)/shard_map/psum | solution.py:299
  136.3 0.1 reshape_squeeze.3
  136.4 0.1 copy.11
  136.5 0.1 broadcast_in_dim.2
  136.6 4.4 %all-to-all-done.1 = bf16[32,24,2048]{2,1,0:T(8,128)(2,1)S(1)} async-done(((bf16[32,24,2048]{2,1,0:T(8,128)(2,1)}), bf16[32,24,2048]{2,1,0:T(8,128)(2,1)S(1)}, u32[]{:S(2)}, u32[]{:S(2)}) %all-to-all-start.1) | async-done | bytes 3145760 | tf_op jit(solution)/shard_map/all_to_all | solution.py:290
  141.0 0.0 copy-start
  141.0 0.7 all_to_all.26
  141.7 6.2 %all-to-all-start.2 = ((f32[32,1,256]{2,1,0:T(1,128)}), f32[32,1,256]{2,1,0:T(1,128)S(1)}, u32[]{:S(2)}, u32[]{:S(2)}) async-start(f32[32,1,256]{2,1,0:T(1,128)} %all_to_all.26), calls=%async_computation.3 | async-start | bytes 65536 | tf_op jit(solution)/shard_map/all_to_all | solution.py:302
  147.9 0.0 copy-done
  147.9 3.4 %shard_map.79 = bf16[128,1024]{1,0:T(8,128)(2,1)} custom-call(bf16[1536,128]{1,0:T(8,128)(2,1)} %get-tuple-element.10.picks_ref, bf16[768,2048]{1,0:T(8,128)(2,1)} %bitcast.15), custom_call_target="tpu_custom_call" | custom-call | flops 402653184 | bytes 3145728 | tf_op jit(solution)/shard_map/pallas_call | solution.py:203
  151.3 2.2 %all-to-all-done.2 = f32[32,1,256]{2,1,0:T(1,128)S(1)} async-done(((f32[32,1,256]{2,1,0:T(1,128)}), f32[32,1,256]{2,1,0:T(1,128)S(1)}, u32[]{:S(2)}, u32[]{:S(2)}) %all-to-all-start.2) | async-done | bytes 32800 | tf_op jit(solution)/shard_map/all_to_all | solution.py:302
  153.4 0.1 reduce_sum.9
  153.5 0.6 multiply_reduce_fusion
  154.1 8.9 %reduce-scatter.2.cloned.1.call-done = bf16[64,1536]{1,0:T(8,128)(2,1)} async-done(((bf16[1024,1536]{1,0:T(8,128)(2,1)}), bf16[64,1536]{1,0:T(8,128)(2,1)}) %reduce-scatter.2.cloned.1.call-update) | async-done | bytes 196624 | tf_op jit(solution)/shard_map/reduce_scatter | solution.py:271
  163.0 1.7 reshape.32
  (2 shorter events, 0.0 us)
Async XLA Ops:
  12.3 10.7 %copy-start.1 = (bf16[64,2,768]{2,1,0:T(2,128)(2,1)S(1)}, bf16[64,2,768]{2,1,0:T(2,128)(2,1)}, u32[]{:S(2)}) copy-start(bf16[64,2,768]{2,1,0:T(2,128)(2,1)} %param.9) | copy-start | bytes 589828
  12.3 65.5 %all-to-all-start = ((bf16[32,24,2816]{2,1,0:T(8,128)(2,1)}), bf16[32,24,2816]{2,1,0:T(8,128)(2,1)}, u32[]{:S(2)}, u32[]{:S(2)}) async-start(bf16[32,24,2816]{2,1,0:T(8,128)(2,1)} %bitcast.16), calls=%async_computation | async-start | bytes 8650752 | tf_op jit(solution)/shard_map/all_to_all | solution.py:249
  22.9 140.1 %reduce-scatter.2.cloned.1.call-start = ((), (), s32[]{:S(2)}) async-start(), calls=%async_computation.4 | async-start | bytes 3342336 | tf_op jit(solution)/shard_map/reduce_scatter | solution.py:271
  94.5 46.5 %all-to-all-start.1 = ((bf16[32,24,2048]{2,1,0:T(8,128)(2,1)}), bf16[32,24,2048]{2,1,0:T(8,128)(2,1)S(1)}, u32[]{:S(2)}, u32[]{:S(2)}) async-start(bf16[32,24,2048]{2,1,0:T(8,128)(2,1)} %bitcast.5), calls=%async_computation.1 | async-start | bytes 6291456 | tf_op jit(solution)/shard_map/all_to_all | solution.py:290
  141.0 6.9 %copy-start = (bf16[32,24,2048]{2,1,0:T(8,128)(2,1)}, bf16[32,24,2048]{2,1,0:T(8,128)(2,1)S(1)}, u32[]{:S(2)}) copy-start(bf16[32,24,2048]{2,1,0:T(8,128)(2,1)S(1)} %all-to-all-done.1) | copy-start | bytes 9437188
  141.7 11.8 %all-to-all-start.2 = ((f32[32,1,256]{2,1,0:T(1,128)}), f32[32,1,256]{2,1,0:T(1,128)S(1)}, u32[]{:S(2)}, u32[]{:S(2)}) async-start(f32[32,1,256]{2,1,0:T(1,128)} %all_to_all.26), calls=%async_computation.3 | async-start | bytes 65536 | tf_op jit(solution)/shard_map/all_to_all | solution.py:302
Sparse Core Ops, SparseCore 0:
  86.1 76.9 reduce-scatter.1

commit v7 on v6

--- a/solution.py
+++ b/solution.py
@@ -198,6 +198,31 @@
     out_ref[...] = total.astype(BF16)
 
 
+STEPS = tuple(2.0 ** (-10 * k) for k in range(1, 11))
+NOTE_ROWS = 8
+
+
+def to_half(weights):
+    wide = weights.astype(F32)
+    top = jnp.max(jnp.abs(wide))
+    level, lift = jnp.float32(0.0), jnp.float32(2.0**15)
+    for bound in STEPS:
+        level += jnp.where(top < bound, 1.0, 0.0)
+        lift *= jnp.where(top < bound, 2.0**10, 1.0)
+    note = jnp.broadcast_to(level, (NOTE_ROWS, weights.shape[1]))
+    return jnp.concatenate([wide * lift, note], axis=0).astype(jnp.float16)
+
+
+def from_half(gathered, shards):
+    parts = gathered.reshape(shards, -1, gathered.shape[1])
+    level = parts[:, -1, 0].astype(F32)
+    drop = jnp.full((shards,), 2.0**-15, F32)
+    for k in range(len(STEPS)):
+        drop *= jnp.where(level > k + 0.5, 2.0**-10, 1.0)
+    whole = parts[:, :-NOTE_ROWS].astype(F32) * drop[:, None, None]
+    return whole.astype(BF16).reshape(-1, gathered.shape[1])
+
+
 def call(kernel, outs, args, in_specs=None, out_specs=None, grid=(), scratch=(), flops=0, moved=0, room=VMEM_LIMIT):
     whole = pl.BlockSpec(memory_space=pltpu.VMEM)
     return pl.pallas_call(
@@ -224,9 +249,6 @@
     size, count = devices * cap, tok_count * topk
     lanes = per_device * (model + width)
     vmem, hbm = pl.BlockSpec(memory_space=pltpu.VMEM), pl.BlockSpec(memory_space=pltpu.HBM)
-
-    lift = 2.0**18
-    sent = (gate_up.astype(F32) * lift).astype(jnp.float16).reshape(channels, per_device * hidden)
 
     (packed,) = call(
         functools.partial(pack_kernel, per_device, devices, cap),
@@ -247,8 +269,9 @@
         moved=2 * size * lanes,
     )
     got = lax.all_to_all(packed, "expert", split_axis=0, concat_axis=0, tiled=True)
-    gathered = lax.all_gather(sent, "dp", axis=0, tiled=True)
-    full = (gathered.astype(F32) * (1.0 / lift)).astype(BF16)
+    later, _ = lax.optimization_barrier((gate_up, packed))
+    sent = to_half(later.reshape(channels, per_device * hidden))
+    full = from_half(lax.all_gather(sent, "dp", axis=0, tiled=True), data_ways)
 
     work = 2 * per_device * size * model * hidden
     tiles = size // 256

time: 172 us -> 180 us (1.047)
  between operations: 14.1 us -> 20.7 us
    all_to_all x1, waiting for transfers between devices: 4.39 us -> 9.07 us  [body(): lax.all_to_all(back, 'expert', split_axis=0, concat_axis=0, tiled=True)]
    psum x1, blocking collectives: 32.1 us -> 27.4 us  [body(): column = lax.psum(sums, 'dp')[0, :experts].reshape(per_device, devices).T]
    reduce_scatter x1, waiting for transfers between devices: 8.87 us -> 4.36 us  [body(): mine = lax.psum_scatter(part, 'dp', scatter_dimension=0, tiled=True)]
    all_gather x1, blocking collectives: 53.9 us -> 56.9 us  [body(): full = from_half(lax.all_gather(sent, 'dp', axis=0, tiled=True), data_ways)]
  transfers between devices with their start and end apart: 4 -> 4, of which waited for: 3 -> 3; matrix products, arithmetic and copies ran while one was open for 1% -> 2% of each run, Pallas kernels for 8% -> 8%
where the time goes in v7:
time: 180 us; the launch traced here: 179 us
  blocking collectives  84.4 us (47%)
  Pallas kernels  26.9 us (15%)
  starting transfers between devices  25.5 us (14%)
  between operations  20.7 us (12%)
  waiting for transfers between devices  15.6 us (9%)
  other arithmetic  2.9 us (2%)
  local copies, waits for them, and re-layouts  2.75 us (2%)
    all_gather x1, blocking collectives, body(): full = from_half(lax.all_gather(sent, 'dp', axis=0, tiled=True), data_ways)  56.9 us
    psum x1, blocking collectives, body(): column = lax.psum(sums, 'dp')[0, :experts].reshape(per_device, devices).T  27.4 us
    pallas_call x5, Pallas kernels, call(): pl.pallas_call(kernel, grid=grid, out_shape=[jax.ShapeDtypeStruct(s, t) f...  26.9 us
    all_to_all x1, starting transfers between devices, body(): lax.all_to_all(packed, 'expert', split_axis=0, concat_axis=0, tiled=True)  10.6 us
    all_to_all x1, waiting for transfers between devices, body(): lax.all_to_all(back, 'expert', split_axis=0, concat_axis=0, tiled=True)  9.07 us
    all_to_all x1, starting transfers between devices, body(): lax.all_to_all(back, 'expert', split_axis=0, concat_axis=0, tiled=True)  8.64 us
    all_to_all x1, starting transfers between devices, body(): lax.all_to_all(column, 'expert', split_axis=0, concat_axis=0, tiled=True)  6.21 us
    reduce_scatter x1, waiting for transfers between devices, body(): mine = lax.psum_scatter(part, 'dp', scatter_dimension=0, tiled=True)  4.36 us
  transfers between devices with their start and end apart: 4, of which 3 were waited for; matrix products, arithmetic and copies ran while one was open for 2% of the time, Pallas kernels for 8%

profile of v7, /device:TPU:6, one launch (start us, length us, event | category | flops | bytes accessed | tf_op | source)
XLA Modules:
  0.0 178.8 jit_solution(10339059773579845286)
XLA Ops:
  7.2 5.2 %shard_map.76 = bf16[768,2816]{1,0:T(8,128)(2,1)} custom-call(s32[8,128]{1,0:T(8,128)} %bitcast.27, f32[8,128]{1,0:T(8,128)} %bitcast.29, bf16[128,1024]{1,0:T(8,128)(2,1)} %tokens_hbm.1, bf16[1024,384]{1,0:T(8,128)(2,1)} %bitcast.33), custom_call_target="tpu_custom_call" | custom-call | flops 1610612736 | bytes 4325376 | tf_op jit(solution)/shard_map/pallas_call | solution.py:228
  12.3 0.0 copy-start.1
  12.3 10.6 %all-to-all-start = ((bf16[32,24,2816]{2,1,0:T(8,128)(2,1)}), bf16[32,24,2816]{2,1,0:T(8,128)(2,1)}, u32[]{:S(2)}, u32[]{:S(2)}) async-start(bf16[32,24,2816]{2,1,0:T(8,128)(2,1)} %bitcast.22), calls=%async_computation | async-start | bytes 8650752 | tf_op jit(solution)/shard_map/all_to_all | solution.py:271
  22.9 0.0 reduce-scatter.2.cloned.1.call-start
  23.0 0.0 copy-done.1
  23.0 1.0 fusion
  30.5 0.2 fusion.1
  30.8 0.1 copy.13
  30.9 56.9 %all-gather.1 = f16[1152,1536]{1,0:T(8,128)(2,1)S(1)} all-gather(f16[72,1536]{1,0:T(8,128)(2,1)S(1)} %concatenate.3), channel_id=1, replica_groups=mesh['dp'=16,'expert'=32] {'dp'}, dimensions={0}, use_global_device_ids=true | all-gather | bytes 3760128 | tf_op jit(solution)/shard_map/all_gather | solution.py:274
  87.8 0.2 fusion.12
  88.0 0.8 multiply_convert_fusion
  88.8 0.0 all-to-all-done
  88.8 8.1 %shard_map.80 = bf16[1024,1536]{1,0:T(8,128)(2,1)} custom-call(bf16[768,2816]{1,0:T(8,128)(2,1)} %bitcast.4.got_hbm, bf16[1024,1536]{1,0:T(8,128)(2,1)S(1)} %bitcast.17), custom_call_target="tpu_custom_call" | custom-call | flops 4831838208 | bytes 9437184 | tf_op jit(solution)/shard_map/pallas_call | solution.py:228
  97.0 0.0 reduce-scatter.2.cloned.1.call-update
  97.0 8.6 %shard_map.77 = bf16[768,2048]{1,0:T(8,128)(2,1)} custom-call(bf16[768,2816]{1,0:T(8,128)(2,1)} %bitcast.4.got_hbm, bf16[1024,1536]{1,0:T(8,128)(2,1)S(1)} %bitcast.18), custom_call_target="tpu_custom_call" | custom-call | flops 4831838208 | bytes 9437184 | tf_op jit(solution)/shard_map/pallas_call | solution.py:228
  105.6 8.6 %all-to-all-start.1 = ((bf16[32,24,2048]{2,1,0:T(8,128)(2,1)}), bf16[32,24,2048]{2,1,0:T(8,128)(2,1)S(1)}, u32[]{:S(2)}, u32[]{:S(2)}) async-start(bf16[32,24,2048]{2,1,0:T(8,128)(2,1)} %bitcast.7), calls=%async_computation.1 | async-start | bytes 6291456 | tf_op jit(solution)/shard_map/all_to_all | solution.py:313
  114.2 1.7 shard_map.78
  116.0 27.4 %psum.7 = f32[1,128]{1,0:T(1,128)S(1)} all-reduce(f32[1,128]{1,0:T(1,128)} %get-tuple-element.13), channel_id=1, replica_groups=mesh['dp'=16,'expert'=32] {'dp'}, use_global_device_ids=true, to_apply=%region_2.3 | all-reduce | flops 128 | bytes 1024 | tf_op jit(solution)/shard_map/psum | solution.py:322
  143.4 0.1 reshape_squeeze.3
  143.5 0.1 copy.12
  143.6 0.1 broadcast_in_dim.36
  143.7 9.1 %all-to-all-done.1 = bf16[32,24,2048]{2,1,0:T(8,128)(2,1)S(1)} async-done(((bf16[32,24,2048]{2,1,0:T(8,128)(2,1)}), bf16[32,24,2048]{2,1,0:T(8,128)(2,1)S(1)}, u32[]{:S(2)}, u32[]{:S(2)}) %all-to-all-start.1) | async-done | bytes 3145760 | tf_op jit(solution)/shard_map/all_to_all | solution.py:313
  152.8 0.0 copy-start
  152.8 0.7 all_to_all.26
  153.5 6.2 %all-to-all-start.2 = ((f32[32,1,256]{2,1,0:T(1,128)}), f32[32,1,256]{2,1,0:T(1,128)S(1)}, u32[]{:S(2)}, u32[]{:S(2)}) async-start(f32[32,1,256]{2,1,0:T(1,128)} %all_to_all.26), calls=%async_computation.3 | async-start | bytes 65536 | tf_op jit(solution)/shard_map/all_to_all | solution.py:325
  159.7 0.0 copy-done
  159.7 3.3 %shard_map.79 = bf16[128,1024]{1,0:T(8,128)(2,1)} custom-call(bf16[1536,128]{1,0:T(8,128)(2,1)} %get-tuple-element.12.picks_ref, bf16[768,2048]{1,0:T(8,128)(2,1)} %bitcast.21), custom_call_target="tpu_custom_call" | custom-call | flops 402653184 | bytes 3145728 | tf_op jit(solution)/shard_map/pallas_call | solution.py:228
  163.1 2.2 %all-to-all-done.2 = f32[32,1,256]{2,1,0:T(1,128)S(1)} async-done(((f32[32,1,256]{2,1,0:T(1,128)}), f32[32,1,256]{2,1,0:T(1,128)S(1)}, u32[]{:S(2)}, u32[]{:S(2)}) %all-to-all-start.2) | async-done | bytes 32800 | tf_op jit(solution)/shard_map/all_to_all | solution.py:325
  165.2 0.1 reduce_sum.9
  165.3 0.6 multiply_reduce_fusion
  165.9 4.4 %reduce-scatter.2.cloned.1.call-done = bf16[64,1536]{1,0:T(8,128)(2,1)} async-done(((bf16[1024,1536]{1,0:T(8,128)(2,1)}), bf16[64,1536]{1,0:T(8,128)(2,1)}) %reduce-scatter.2.cloned.1.call-update) | async-done | bytes 196624 | tf_op jit(solution)/shard_map/reduce_scatter | solution.py:294
  170.3 1.7 reshape.41
  (3 shorter events, 0.1 us)
Async XLA Ops:
  12.3 10.7 %copy-start.1 = (bf16[64,2,768]{2,1,0:T(2,128)(2,1)S(1)}, bf16[64,2,768]{2,1,0:T(2,128)(2,1)}, u32[]{:S(2)}) copy-start(bf16[64,2,768]{2,1,0:T(2,128)(2,1)} %param.9) | copy-start | bytes 589828
  12.3 76.5 %all-to-all-start = ((bf16[32,24,2816]{2,1,0:T(8,128)(2,1)}), bf16[32,24,2816]{2,1,0:T(8,128)(2,1)}, u32[]{:S(2)}, u32[]{:S(2)}) async-start(bf16[32,24,2816]{2,1,0:T(8,128)(2,1)} %bitcast.22), calls=%async_computation | async-start | bytes 8650752 | tf_op jit(solution)/shard_map/all_to_all | solution.py:271
  22.9 147.3 %reduce-scatter.2.cloned.1.call-start = ((), (), s32[]{:S(2)}) async-start(), calls=%async_computation.4 | async-start | bytes 3342336 | tf_op jit(solution)/shard_map/reduce_scatter | solution.py:294
  105.6 47.2 %all-to-all-start.1 = ((bf16[32,24,2048]{2,1,0:T(8,128)(2,1)}), bf16[32,24,2048]{2,1,0:T(8,128)(2,1)S(1)}, u32[]{:S(2)}, u32[]{:S(2)}) async-start(bf16[32,24,2048]{2,1,0:T(8,128)(2,1)} %bitcast.7), calls=%async_computation.1 | async-start | bytes 6291456 | tf_op jit(solution)/shard_map/all_to_all | solution.py:313
  152.8 6.9 %copy-start = (bf16[32,24,2048]{2,1,0:T(8,128)(2,1)}, bf16[32,24,2048]{2,1,0:T(8,128)(2,1)S(1)}, u32[]{:S(2)}) copy-start(bf16[32,24,2048]{2,1,0:T(8,128)(2,1)S(1)} %all-to-all-done.1) | copy-start | bytes 9437188
  153.5 11.8 %all-to-all-start.2 = ((f32[32,1,256]{2,1,0:T(1,128)}), f32[32,1,256]{2,1,0:T(1,128)S(1)}, u32[]{:S(2)}, u32[]{:S(2)}) async-start(f32[32,1,256]{2,1,0:T(1,128)} %all_to_all.26), calls=%async_computation.3 | async-start | bytes 65536 | tf_op jit(solution)/shard_map/all_to_all | solution.py:325
Sparse Core Ops, SparseCore 0:
  97.1 73.1 reduce-scatter.1

commit v8 on v6

--- a/solution.py
+++ b/solution.py
@@ -198,6 +198,31 @@
     out_ref[...] = total.astype(BF16)
 
 
+STEPS = 10
+NOTE_LANES = 128
+
+
+def to_half(weights):
+    wide = weights.astype(F32)
+    top = jnp.max(jnp.abs(wide))
+    bounds = jnp.array([2.0 ** (-10 * k) for k in range(1, STEPS + 1)], F32)
+    lifts = jnp.array([2.0 ** (15 + 10 * k) for k in range(1, STEPS + 1)], F32)
+    lift = jnp.max(jnp.where(top < bounds, lifts, 2.0**15))
+    level = jnp.sum(jnp.where(top < bounds, 1.0, 0.0))
+    note = jnp.broadcast_to(level, (weights.shape[0], NOTE_LANES))
+    return jnp.concatenate([wide * lift, note], axis=1).astype(jnp.float16)
+
+
+def from_half(gathered, shards):
+    rows, lanes = gathered.shape[0], gathered.shape[1] - NOTE_LANES
+    parts = gathered.reshape(shards, rows // shards, lanes + NOTE_LANES)
+    level = parts[:, 0, lanes].astype(F32)[:, None]
+    steps = jnp.arange(STEPS + 1, dtype=F32)[None, :]
+    drops = jnp.array([2.0 ** (-15 - 10 * k) for k in range(STEPS + 1)], F32)[None, :]
+    drop = jnp.sum(jnp.where(level == steps, drops, 0.0), axis=1)
+    return (parts[:, :, :lanes].astype(F32) * drop[:, None, None]).astype(BF16).reshape(rows, lanes)
+
+
 def call(kernel, outs, args, in_specs=None, out_specs=None, grid=(), scratch=(), flops=0, moved=0, room=VMEM_LIMIT):
     whole = pl.BlockSpec(memory_space=pltpu.VMEM)
     return pl.pallas_call(
@@ -224,9 +249,6 @@
     size, count = devices * cap, tok_count * topk
     lanes = per_device * (model + width)
     vmem, hbm = pl.BlockSpec(memory_space=pltpu.VMEM), pl.BlockSpec(memory_space=pltpu.HBM)
-
-    lift = 2.0**18
-    sent = (gate_up.astype(F32) * lift).astype(jnp.float16).reshape(channels, per_device * hidden)
 
     (packed,) = call(
         functools.partial(pack_kernel, per_device, devices, cap),
@@ -247,8 +269,9 @@
         moved=2 * size * lanes,
     )
     got = lax.all_to_all(packed, "expert", split_axis=0, concat_axis=0, tiled=True)
-    gathered = lax.all_gather(sent, "dp", axis=0, tiled=True)
-    full = (gathered.astype(F32) * (1.0 / lift)).astype(BF16)
+    later, _ = lax.optimization_barrier((gate_up, packed))
+    sent = to_half(later.reshape(channels, per_device * hidden))
+    full = from_half(lax.all_gather(sent, "dp", axis=0, tiled=True), data_ways)
 
     work = 2 * per_device * size * model * hidden
     tiles = size // 256

time: 172 us -> 176 us (1.023)
  other arithmetic: 1.49 us -> 4.97 us
  blocking collectives: 86 us -> 83.1 us
    all_to_all x1, waiting for transfers between devices: 4.39 us -> 9.19 us  [body(): lax.all_to_all(back, 'expert', split_axis=0, concat_axis=0, tiled=True)]
    psum x1, blocking collectives: 32.1 us -> 27.3 us  [body(): column = lax.psum(sums, 'dp')[0, :experts].reshape(per_device, devices).T]
    reduce_scatter x1, waiting for transfers between devices: 8.87 us -> 5.43 us  [body(): mine = lax.psum_scatter(part, 'dp', scatter_dimension=0, tiled=True)]
    all_gather x1, blocking collectives: 53.9 us -> 55.8 us  [body(): full = from_half(lax.all_gather(sent, 'dp', axis=0, tiled=True), data_ways)]
  transfers between devices with their start and end apart: 4 -> 4, of which waited for: 3 -> 3; matrix products, arithmetic and copies ran while one was open for 1% -> 3% of each run, Pallas kernels for 8% -> 8%
where the time goes in v8:
time: 176 us; the launch traced here: 175 us
  blocking collectives  83.1 us (47%)
  Pallas kernels  26.9 us (15%)
  starting transfers between devices  25.7 us (15%)
  waiting for transfers between devices  16.8 us (10%)
  between operations  14.8 us (8%)
  other arithmetic  4.97 us (3%)
  local copies, waits for them, and re-layouts  2.77 us (2%)
    all_gather x1, blocking collectives, body(): full = from_half(lax.all_gather(sent, 'dp', axis=0, tiled=True), data_ways)  55.8 us
    psum x1, blocking collectives, body(): column = lax.psum(sums, 'dp')[0, :experts].reshape(per_device, devices).T  27.3 us
    pallas_call x5, Pallas kernels, call(): pl.pallas_call(kernel, grid=grid, out_shape=[jax.ShapeDtypeStruct(s, t) f...  26.9 us
    all_to_all x1, starting transfers between devices, body(): lax.all_to_all(packed, 'expert', split_axis=0, concat_axis=0, tiled=True)  10.6 us
    all_to_all x1, waiting for transfers between devices, body(): lax.all_to_all(back, 'expert', split_axis=0, concat_axis=0, tiled=True)  9.19 us
    all_to_all x1, starting transfers between devices, body(): lax.all_to_all(back, 'expert', split_axis=0, concat_axis=0, tiled=True)  8.87 us
    all_to_all x1, starting transfers between devices, body(): lax.all_to_all(column, 'expert', split_axis=0, concat_axis=0, tiled=True)  6.21 us
    reduce_scatter x1, waiting for transfers between devices, body(): mine = lax.psum_scatter(part, 'dp', scatter_dimension=0, tiled=True)  5.43 us
  transfers between devices with their start and end apart: 4, of which 3 were waited for; matrix products, arithmetic and copies ran while one was open for 3% of the time, Pallas kernels for 8%

profile of v8, /device:TPU:6, one launch (start us, length us, event | category | flops | bytes accessed | tf_op | source)
XLA Modules:
  0.0 175.1 jit_solution(12677652701833898880)
XLA Ops:
  7.2 5.2 %shard_map.103 = bf16[768,2816]{1,0:T(8,128)(2,1)} custom-call(s32[8,128]{1,0:T(8,128)} %bitcast.27, f32[8,128]{1,0:T(8,128)} %bitcast.29, bf16[128,1024]{1,0:T(8,128)(2,1)} %tokens_hbm.1, bf16[1024,384]{1,0:T(8,128)(2,1)} %bitcast.33), custom_call_target="tpu_custom_call" | custom-call | flops 1610612736 | bytes 4325376 | tf_op jit(solution)/shard_map/pallas_call | solution.py:228
  12.3 0.0 copy-start.2
  12.4 0.0 copy-start.3
  12.4 10.6 %all-to-all-start = ((bf16[32,24,2816]{2,1,0:T(8,128)(2,1)}), bf16[32,24,2816]{2,1,0:T(8,128)(2,1)}, u32[]{:S(2)}, u32[]{:S(2)}) async-start(bf16[32,24,2816]{2,1,0:T(8,128)(2,1)} %bitcast.22), calls=%async_computation | async-start | bytes 8650752 | tf_op jit(solution)/shard_map/all_to_all | solution.py:271
  23.0 0.0 copy-start.4
  23.0 0.0 reduce-scatter.2.cloned.1.call-start
  23.0 1.0 fusion
  24.1 1.2 fusion.4
  26.0 0.9 fusion.1
  26.8 0.1 copy.17
  26.9 55.8 %all-gather.1 = f16[1024,1664]{1,0:T(8,128)(2,1)S(1)} all-gather(f16[64,1664]{1,0:T(8,128)(2,1)S(1)} %concatenate.3), channel_id=1, replica_groups=mesh['dp'=16,'expert'=32] {'dp'}, dimensions={0}, use_global_device_ids=true | all-gather | bytes 3620864 | tf_op jit(solution)/shard_map/all_gather | solution.py:274
  82.7 0.2 fusion.2
  82.9 0.2 select_reduce_fusion
  83.1 0.8 multiply_convert_fusion
  83.9 8.1 %shard_map.107 = bf16[1024,1536]{1,0:T(8,128)(2,1)} custom-call(bf16[768,2816]{1,0:T(8,128)(2,1)} %bitcast.4.got_hbm, bf16[1024,1536]{1,0:T(8,128)(2,1)S(1)} %bitcast.17), custom_call_target="tpu_custom_call" | custom-call | flops 4831838208 | bytes 9437184 | tf_op jit(solution)/shard_map/pallas_call | solution.py:228
  92.0 0.0 reduce-scatter.2.cloned.1.call-update
  92.1 8.6 %shard_map.104 = bf16[768,2048]{1,0:T(8,128)(2,1)} custom-call(bf16[768,2816]{1,0:T(8,128)(2,1)} %bitcast.4.got_hbm, bf16[1024,1536]{1,0:T(8,128)(2,1)S(1)} %bitcast.18), custom_call_target="tpu_custom_call" | custom-call | flops 4831838208 | bytes 9437184 | tf_op jit(solution)/shard_map/pallas_call | solution.py:228
  100.7 8.9 %all-to-all-start.1 = ((bf16[32,24,2048]{2,1,0:T(8,128)(2,1)}), bf16[32,24,2048]{2,1,0:T(8,128)(2,1)S(1)}, u32[]{:S(2)}, u32[]{:S(2)}) async-start(bf16[32,24,2048]{2,1,0:T(8,128)(2,1)} %bitcast.7), calls=%async_computation.1 | async-start | bytes 6291456 | tf_op jit(solution)/shard_map/all_to_all | solution.py:313
  109.5 1.7 shard_map.105
  111.2 27.3 %psum.7 = f32[1,128]{1,0:T(1,128)S(1)} all-reduce(f32[1,128]{1,0:T(1,128)} %get-tuple-element.13), channel_id=1, replica_groups=mesh['dp'=16,'expert'=32] {'dp'}, use_global_device_ids=true, to_apply=%region_5.6 | all-reduce | flops 128 | bytes 1024 | tf_op jit(solution)/shard_map/psum | solution.py:322
  138.6 0.1 reshape_squeeze.3
  138.7 0.1 copy.16
  138.8 0.1 broadcast_in_dim.40
  138.9 9.2 %all-to-all-done.1 = bf16[32,24,2048]{2,1,0:T(8,128)(2,1)S(1)} async-done(((bf16[32,24,2048]{2,1,0:T(8,128)(2,1)}), bf16[32,24,2048]{2,1,0:T(8,128)(2,1)S(1)}, u32[]{:S(2)}, u32[]{:S(2)}) %all-to-all-start.1) | async-done | bytes 3145760 | tf_op jit(solution)/shard_map/all_to_all | solution.py:313
  148.1 0.7 all_to_all.26
  148.8 6.2 %all-to-all-start.2 = ((f32[32,1,256]{2,1,0:T(1,128)}), f32[32,1,256]{2,1,0:T(1,128)S(1)}, u32[]{:S(2)}, u32[]{:S(2)}) async-start(f32[32,1,256]{2,1,0:T(1,128)} %all_to_all.26), calls=%async_computation.3 | async-start | bytes 65536 | tf_op jit(solution)/shard_map/all_to_all | solution.py:325
  155.0 3.4 %shard_map.106 = bf16[128,1024]{1,0:T(8,128)(2,1)} custom-call(bf16[1536,128]{1,0:T(8,128)(2,1)} %get-tuple-element.12.picks_ref, bf16[768,2048]{1,0:T(8,128)(2,1)} %bitcast.21), custom_call_target="tpu_custom_call" | custom-call | flops 402653184 | bytes 3145728 | tf_op jit(solution)/shard_map/pallas_call | solution.py:228
  158.4 2.1 %all-to-all-done.2 = f32[32,1,256]{2,1,0:T(1,128)S(1)} async-done(((f32[32,1,256]{2,1,0:T(1,128)}), f32[32,1,256]{2,1,0:T(1,128)S(1)}, u32[]{:S(2)}, u32[]{:S(2)}) %all-to-all-start.2) | async-done | bytes 32800 | tf_op jit(solution)/shard_map/all_to_all | solution.py:325
  160.5 0.1 reduce_sum.29
  160.6 0.6 multiply_reduce_fusion
  161.2 5.4 %reduce-scatter.2.cloned.1.call-done = bf16[64,1536]{1,0:T(8,128)(2,1)} async-done(((bf16[1024,1536]{1,0:T(8,128)(2,1)}), bf16[64,1536]{1,0:T(8,128)(2,1)}) %reduce-scatter.2.cloned.1.call-update) | async-done | bytes 196624 | tf_op jit(solution)/shard_map/reduce_scatter | solution.py:294
  166.6 1.7 reshape.50
  (11 shorter events, 0.1 us)
Async XLA Ops:
  12.3 10.7 %copy-start.1 = (bf16[64,2,768]{2,1,0:T(2,128)(2,1)S(1)}, bf16[64,2,768]{2,1,0:T(2,128)(2,1)}, u32[]{:S(2)}) copy-start(bf16[64,2,768]{2,1,0:T(2,128)(2,1)} %param.12) | copy-start | bytes 589828
  12.3 11.7 %copy-start.2 = (f32[10]{0:T(128)S(1)}, f32[10]{0:T(128)}, u32[]{:S(2)}) copy-start(f32[10]{0:T(128)} %constant.17.clone) | copy-start | bytes 124
  12.4 11.7 %copy-start.3 = (f32[10]{0:T(128)S(1)}, f32[10]{0:T(128)}, u32[]{:S(2)}) copy-start(f32[10]{0:T(128)} %constant.16.clone) | copy-start | bytes 124
  12.4 71.5 %all-to-all-start = ((bf16[32,24,2816]{2,1,0:T(8,128)(2,1)}), bf16[32,24,2816]{2,1,0:T(8,128)(2,1)}, u32[]{:S(2)}, u32[]{:S(2)}) async-start(bf16[32,24,2816]{2,1,0:T(8,128)(2,1)} %bitcast.22), calls=%async_computation | async-start | bytes 8650752 | tf_op jit(solution)/shard_map/all_to_all | solution.py:271
  23.0 59.9 %copy-start.4 = (f32[11]{0:T(128)S(1)}, f32[11]{0:T(128)}, u32[]{:S(2)}) copy-start(f32[11]{0:T(128)} %constant.18.clone) | copy-start | bytes 136
  23.0 143.7 %reduce-scatter.2.cloned.1.call-start = ((), (), s32[]{:S(2)}) async-start(), calls=%async_computation.4 | async-start | bytes 3342336 | tf_op jit(solution)/shard_map/reduce_scatter | solution.py:294
  100.7 47.4 %all-to-all-start.1 = ((bf16[32,24,2048]{2,1,0:T(8,128)(2,1)}), bf16[32,24,2048]{2,1,0:T(8,128)(2,1)S(1)}, u32[]{:S(2)}, u32[]{:S(2)}) async-start(bf16[32,24,2048]{2,1,0:T(8,128)(2,1)} %bitcast.7), calls=%async_computation.1 | async-start | bytes 6291456 | tf_op jit(solution)/shard_map/all_to_all | solution.py:313
  148.1 6.9 %copy-start = (bf16[32,24,2048]{2,1,0:T(8,128)(2,1)}, bf16[32,24,2048]{2,1,0:T(8,128)(2,1)S(1)}, u32[]{:S(2)}) copy-start(bf16[32,24,2048]{2,1,0:T(8,128)(2,1)S(1)} %all-to-all-done.1) | copy-start | bytes 9437188
  148.8 11.8 %all-to-all-start.2 = ((f32[32,1,256]{2,1,0:T(1,128)}), f32[32,1,256]{2,1,0:T(1,128)S(1)}, u32[]{:S(2)}, u32[]{:S(2)}) async-start(f32[32,1,256]{2,1,0:T(1,128)} %all_to_all.26), calls=%async_computation.3 | async-start | bytes 65536 | tf_op jit(solution)/shard_map/all_to_all | solution.py:325
Sparse Core Ops, SparseCore 0:
  92.2 74.4 reduce-scatter.1

commit v9 on v8

--- a/solution.py
+++ b/solution.py
@@ -202,21 +202,22 @@
 NOTE_LANES = 128
 
 
-def to_half(weights):
-    wide = weights.astype(F32)
-    top = jnp.max(jnp.abs(wide))
-    bounds = jnp.array([2.0 ** (-10 * k) for k in range(1, STEPS + 1)], F32)
-    lifts = jnp.array([2.0 ** (15 + 10 * k) for k in range(1, STEPS + 1)], F32)
-    lift = jnp.max(jnp.where(top < bounds, lifts, 2.0**15))
-    level = jnp.sum(jnp.where(top < bounds, 1.0, 0.0))
-    note = jnp.broadcast_to(level, (weights.shape[0], NOTE_LANES))
-    return jnp.concatenate([wide * lift, note], axis=1).astype(jnp.float16)
+def lift_kernel(w_ref, out_ref):
+    lanes = w_ref.shape[1]
+    wide = w_ref[...].astype(F32)
+    top = jnp.max(jnp.max(jnp.abs(wide), axis=0, keepdims=True), axis=1, keepdims=True)
+    level, lift = jnp.zeros((1, 1), F32), jnp.full((1, 1), 2.0**15, F32)
+    for k in range(1, STEPS + 1):
+        level = jnp.where(top < 2.0 ** (-10 * k), float(k), level)
+        lift = jnp.where(top < 2.0 ** (-10 * k), 2.0 ** (15 + 10 * k), lift)
+    out_ref[:, :lanes] = (wide * lift).astype(BF16)
+    out_ref[:, lanes:] = jnp.broadcast_to(level, (w_ref.shape[0], NOTE_LANES)).astype(BF16)
 
 
 def from_half(gathered, shards):
     rows, lanes = gathered.shape[0], gathered.shape[1] - NOTE_LANES
     parts = gathered.reshape(shards, rows // shards, lanes + NOTE_LANES)
-    level = parts[:, 0, lanes].astype(F32)[:, None]
+    level = jnp.max(parts[:, :8, lanes:].astype(F32), axis=(1, 2))[:, None]
     steps = jnp.arange(STEPS + 1, dtype=F32)[None, :]
     drops = jnp.array([2.0 ** (-15 - 10 * k) for k in range(STEPS + 1)], F32)[None, :]
     drop = jnp.sum(jnp.where(level == steps, drops, 0.0), axis=1)
@@ -270,7 +271,14 @@
     )
     got = lax.all_to_all(packed, "expert", split_axis=0, concat_axis=0, tiled=True)
     later, _ = lax.optimization_barrier((gate_up, packed))
-    sent = to_half(later.reshape(channels, per_device * hidden))
+    (lifted,) = call(
+        lift_kernel,
+        [((channels, per_device * hidden + NOTE_LANES), BF16)],
+        [later.reshape(channels, per_device * hidden)],
+        moved=4 * channels * per_device * hidden,
+        room=ROOM,
+    )
+    sent = lifted.astype(jnp.float16)
     full = from_half(lax.all_gather(sent, "dp", axis=0, tiled=True), data_ways)
 
     work = 2 * per_device * size * model * hidden

time: 176 us -> 173 us (0.983)
  other arithmetic: 4.97 us -> 1.91 us
    pallas_call x5 -> x6, Pallas kernels: 26.9 us -> 27.1 us  [call(): pl.pallas_call(kernel, grid=grid, out_shape=[jax.ShapeDtypeStruct(s, t) f...]
  transfers between devices with their start and end apart: 4 -> 4, of which waited for: 3 -> 3; matrix products, arithmetic and copies ran while one was open for 3% -> 1% of each run, Pallas kernels for 8% -> 8%
where the time goes in v9:
time: 173 us; the launch traced here: 172 us
  blocking collectives  83.9 us (48%)
  Pallas kernels  27.1 us (16%)
  starting transfers between devices  26.3 us (15%)
  waiting for transfers between devices  16.1 us (9%)
  between operations  14.2 us (8%)
  local copies, waits for them, and re-layouts  2.68 us (2%)
  other arithmetic  1.91 us (1%)
    all_gather x1, blocking collectives, body(): full = from_half(lax.all_gather(sent, 'dp', axis=0, tiled=True), data_ways)  55.7 us
    psum x1, blocking collectives, body(): column = lax.psum(sums, 'dp')[0, :experts].reshape(per_device, devices).T  28.2 us
    pallas_call x6, Pallas kernels, call(): pl.pallas_call(kernel, grid=grid, out_shape=[jax.ShapeDtypeStruct(s, t) f...  27.1 us
    all_to_all x1, starting transfers between devices, body(): lax.all_to_all(packed, 'expert', split_axis=0, concat_axis=0, tiled=True)  10.6 us
    all_to_all x1, starting transfers between devices, body(): lax.all_to_all(back, 'expert', split_axis=0, concat_axis=0, tiled=True)  9.42 us
    all_to_all x1, waiting for transfers between devices, body(): lax.all_to_all(back, 'expert', split_axis=0, concat_axis=0, tiled=True)  8.32 us
    all_to_all x1, starting transfers between devices, body(): lax.all_to_all(column, 'expert', split_axis=0, concat_axis=0, tiled=True)  6.21 us
    reduce_scatter x1, waiting for transfers between devices, body(): mine = lax.psum_scatter(part, 'dp', scatter_dimension=0, tiled=True)  5.59 us
  transfers between devices with their start and end apart: 4, of which 3 were waited for; matrix products, arithmetic and copies ran while one was open for 1% of the time, Pallas kernels for 8%

profile of v9, /device:TPU:6, one launch (start us, length us, event | category | flops | bytes accessed | tf_op | source)
XLA Modules:
  0.0 172.2 jit_solution(4091063376254718667)
XLA Ops:
  7.2 5.2 %shard_map.85 = bf16[768,2816]{1,0:T(8,128)(2,1)} custom-call(s32[8,128]{1,0:T(8,128)} %bitcast.27, f32[8,128]{1,0:T(8,128)} %bitcast.29, bf16[128,1024]{1,0:T(8,128)(2,1)} %tokens_hbm.1, bf16[1024,384]{1,0:T(8,128)(2,1)} %bitcast.33), custom_call_target="tpu_custom_call" | custom-call | flops 1610612736 | bytes 4325376 | tf_op jit(solution)/shard_map/pallas_call | solution.py:229
  12.3 0.0 copy-start.1
  12.3 10.6 %all-to-all-start = ((bf16[32,24,2816]{2,1,0:T(8,128)(2,1)}), bf16[32,24,2816]{2,1,0:T(8,128)(2,1)}, u32[]{:S(2)}, u32[]{:S(2)}) async-start(bf16[32,24,2816]{2,1,0:T(8,128)(2,1)} %bitcast.23), calls=%async_computation | async-start | bytes 8650752 | tf_op jit(solution)/shard_map/all_to_all | solution.py:272
  22.9 0.0 copy-start.2
  23.0 0.0 reduce-scatter.2.cloned.1.call-start
  23.0 0.0 copy-done.1
  23.1 0.2 shard_map.86
  23.3 55.7 %all-gather.1 = f16[1024,1664]{1,0:T(8,128)(2,1)S(1)} all-gather(f16[64,1664]{1,0:T(8,128)(2,1)S(1)} %convert_element_type.12), channel_id=1, replica_groups=mesh['dp'=16,'expert'=32] {'dp'}, dimensions={0}, use_global_device_ids=true | all-gather | bytes 3620864 | tf_op jit(solution)/shard_map/all_gather | solution.py:282
  79.0 0.2 convert_reduce_fusion
  79.2 0.0 copy-done.2
  79.2 0.2 select_reduce_fusion
  79.4 0.8 multiply_convert_fusion
  80.2 0.0 all-to-all-done
  80.2 8.1 %shard_map.90 = bf16[1024,1536]{1,0:T(8,128)(2,1)} custom-call(bf16[768,2816]{1,0:T(8,128)(2,1)} %bitcast.4.got_hbm, bf16[1024,1536]{1,0:T(8,128)(2,1)S(1)} %bitcast.17), custom_call_target="tpu_custom_call" | custom-call | flops 4831838208 | bytes 9437184 | tf_op jit(solution)/shard_map/pallas_call | solution.py:229
  88.3 0.0 reduce-scatter.2.cloned.1.call-update
  88.3 8.6 %shard_map.87 = bf16[768,2048]{1,0:T(8,128)(2,1)} custom-call(bf16[768,2816]{1,0:T(8,128)(2,1)} %bitcast.4.got_hbm, bf16[1024,1536]{1,0:T(8,128)(2,1)S(1)} %bitcast.18), custom_call_target="tpu_custom_call" | custom-call | flops 4831838208 | bytes 9437184 | tf_op jit(solution)/shard_map/pallas_call | solution.py:229
  97.0 9.4 %all-to-all-start.1 = ((bf16[32,24,2048]{2,1,0:T(8,128)(2,1)}), bf16[32,24,2048]{2,1,0:T(8,128)(2,1)S(1)}, u32[]{:S(2)}, u32[]{:S(2)}) async-start(bf16[32,24,2048]{2,1,0:T(8,128)(2,1)} %bitcast.7), calls=%async_computation.1 | async-start | bytes 6291456 | tf_op jit(solution)/shard_map/all_to_all | solution.py:321
  106.4 1.7 shard_map.88
  108.1 28.2 %psum.7 = f32[1,128]{1,0:T(1,128)S(1)} all-reduce(f32[1,128]{1,0:T(1,128)} %get-tuple-element.13), channel_id=1, replica_groups=mesh['dp'=16,'expert'=32] {'dp'}, use_global_device_ids=true, to_apply=%region_3.4 | all-reduce | flops 128 | bytes 1024 | tf_op jit(solution)/shard_map/psum | solution.py:330
  136.3 0.1 reshape_squeeze.3
  136.4 0.1 copy.13
  136.5 0.1 broadcast_in_dim.24
  136.6 8.3 %all-to-all-done.1 = bf16[32,24,2048]{2,1,0:T(8,128)(2,1)S(1)} async-done(((bf16[32,24,2048]{2,1,0:T(8,128)(2,1)}), bf16[32,24,2048]{2,1,0:T(8,128)(2,1)S(1)}, u32[]{:S(2)}, u32[]{:S(2)}) %all-to-all-start.1) | async-done | bytes 3145760 | tf_op jit(solution)/shard_map/all_to_all | solution.py:321
  144.9 0.7 all_to_all.26
  145.6 6.2 %all-to-all-start.2 = ((f32[32,1,256]{2,1,0:T(1,128)}), f32[32,1,256]{2,1,0:T(1,128)S(1)}, u32[]{:S(2)}, u32[]{:S(2)}) async-start(f32[32,1,256]{2,1,0:T(1,128)} %all_to_all.26), calls=%async_computation.3 | async-start | bytes 65536 | tf_op jit(solution)/shard_map/all_to_all | solution.py:333
  151.8 0.0 copy-done
  151.9 3.4 %shard_map.89 = bf16[128,1024]{1,0:T(8,128)(2,1)} custom-call(bf16[1536,128]{1,0:T(8,128)(2,1)} %get-tuple-element.12.picks_ref, bf16[768,2048]{1,0:T(8,128)(2,1)} %bitcast.22), custom_call_target="tpu_custom_call" | custom-call | flops 402653184 | bytes 3145728 | tf_op jit(solution)/shard_map/pallas_call | solution.py:229
  155.2 2.2 %all-to-all-done.2 = f32[32,1,256]{2,1,0:T(1,128)S(1)} async-done(((f32[32,1,256]{2,1,0:T(1,128)}), f32[32,1,256]{2,1,0:T(1,128)S(1)}, u32[]{:S(2)}, u32[]{:S(2)}) %all-to-all-start.2) | async-done | bytes 32800 | tf_op jit(solution)/shard_map/all_to_all | solution.py:333
  157.4 0.1 reduce_sum.19
  157.4 0.6 multiply_reduce_fusion
  158.1 5.6 %reduce-scatter.2.cloned.1.call-done = bf16[64,1536]{1,0:T(8,128)(2,1)} async-done(((bf16[1024,1536]{1,0:T(8,128)(2,1)}), bf16[64,1536]{1,0:T(8,128)(2,1)}) %reduce-scatter.2.cloned.1.call-update) | async-done | bytes 196624 | tf_op jit(solution)/shard_map/reduce_scatter | solution.py:302
  163.7 1.7 reshape.43
  (5 shorter events, 0.1 us)
Async XLA Ops:
  12.3 10.7 %copy-start.1 = (bf16[64,2,768]{2,1,0:T(2,128)(2,1)S(1)}, bf16[64,2,768]{2,1,0:T(2,128)(2,1)}, u32[]{:S(2)}) copy-start(bf16[64,2,768]{2,1,0:T(2,128)(2,1)} %param.10) | copy-start | bytes 589828
  12.3 67.8 %all-to-all-start = ((bf16[32,24,2816]{2,1,0:T(8,128)(2,1)}), bf16[32,24,2816]{2,1,0:T(8,128)(2,1)}, u32[]{:S(2)}, u32[]{:S(2)}) async-start(bf16[32,24,2816]{2,1,0:T(8,128)(2,1)} %bitcast.23), calls=%async_computation | async-start | bytes 8650752 | tf_op jit(solution)/shard_map/all_to_all | solution.py:272
  22.9 56.2 %copy-start.2 = (f32[11]{0:T(128)S(1)}, f32[11]{0:T(128)}, u32[]{:S(2)}) copy-start(f32[11]{0:T(128)} %constant.8.clone) | copy-start | bytes 136
  23.0 140.7 %reduce-scatter.2.cloned.1.call-start = ((), (), s32[]{:S(2)}) async-start(), calls=%async_computation.4 | async-start | bytes 3342336 | tf_op jit(solution)/shard_map/reduce_scatter | solution.py:302
  97.0 48.0 %all-to-all-start.1 = ((bf16[32,24,2048]{2,1,0:T(8,128)(2,1)}), bf16[32,24,2048]{2,1,0:T(8,128)(2,1)S(1)}, u32[]{:S(2)}, u32[]{:S(2)}) async-start(bf16[32,24,2048]{2,1,0:T(8,128)(2,1)} %bitcast.7), calls=%async_computation.1 | async-start | bytes 6291456 | tf_op jit(solution)/shard_map/all_to_all | solution.py:321
  144.9 6.9 %copy-start = (bf16[32,24,2048]{2,1,0:T(8,128)(2,1)}, bf16[32,24,2048]{2,1,0:T(8,128)(2,1)S(1)}, u32[]{:S(2)}) copy-start(bf16[32,24,2048]{2,1,0:T(8,128)(2,1)S(1)} %all-to-all-done.1) | copy-start | bytes 9437188
  145.6 11.8 %all-to-all-start.2 = ((f32[32,1,256]{2,1,0:T(1,128)}), f32[32,1,256]{2,1,0:T(1,128)S(1)}, u32[]{:S(2)}, u32[]{:S(2)}) async-start(f32[32,1,256]{2,1,0:T(1,128)} %all_to_all.26), calls=%async_computation.3 | async-start | bytes 65536 | tf_op jit(solution)/shard_map/all_to_all | solution.py:333
Sparse Core Ops, SparseCore 0:
  88.5 75.1 reduce-scatter.1

commit v10 on v9

--- a/solution.py
+++ b/solution.py
@@ -74,9 +74,6 @@
     picks = picks_of(tok_slot, cap)
 
     step = 256
-    copies[2].wait()
-    copies[3].wait()
-    scaled_ref[...] = (cot_ref[...].astype(F32) * gates).astype(BF16)
     first = per_device * model
     outs = []
 
@@ -85,11 +82,15 @@
         outs.append(pltpu.make_async_copy(out_ref.at[here], out_hbm.at[here], sems.at[len(pairs) + len(outs)]))
         outs[-1].start()
 
+    copies[2].wait()
     for i in range(0, size, step):
         for j in range(per_device):
             rows = dot(picks[j * size + i : j * size + i + step], tokens_ref[...])
             out_ref[i : i + step, j * model : (j + 1) * model] = rows.astype(BF16)
         send(i, 0, first)
+    copies[3].wait()
+    scaled_ref[...] = (cot_ref[...].astype(F32) * gates).astype(BF16)
+    for i in range(0, size, step):
         for j in range(per_device):
             hit = slot == iota((step, 1), 0) + (j * size + i)
             rows = dot(hit.astype(F32).astype(BF16), scaled_ref[...])
@@ -153,12 +154,13 @@
     got_in = iter(fetch_rows(start, got_hbm, got_ref, per_device, model, hidden // 2, step))
     outs = []
     for j in range(per_device):
-        at = j * hidden
         for i in range(0, size, half):
             if i % step == 0:
                 for copy in next(got_in):
                     copy.wait()
             swiglu_grads(got_ref, w_ref, gp_ref, per_device, j, i, half)
+    for j in range(per_device):
+        at = j * hidden
         for i in range(0, model, step):
             part = got_ref[:, j * model + i : j * model + i + step]
             gw_ref[i : i + step, at : at + hidden] = dot(part, gp_ref[:, at : at + hidden], ((0,), (0,))).astype(BF16)

time: 173 us -> 173 us (level)
  no operation moved by 1% of the time
where the time goes in v10:
time: 173 us; the launch traced here: 172 us
  blocking collectives  84 us (49%)
  Pallas kernels  27.2 us (16%)
  starting transfers between devices  26.2 us (15%)
  waiting for transfers between devices  15.7 us (9%)
  between operations  14.2 us (8%)
  local copies, waits for them, and re-layouts  2.68 us (2%)
  other arithmetic  1.91 us (1%)
    all_gather x1, blocking collectives, body(): full = from_half(lax.all_gather(sent, 'dp', axis=0, tiled=True), data_ways)  55.8 us
    psum x1, blocking collectives, body(): column = lax.psum(sums, 'dp')[0, :experts].reshape(per_device, devices).T  28.2 us
    pallas_call x6, Pallas kernels, call(): pl.pallas_call(kernel, grid=grid, out_shape=[jax.ShapeDtypeStruct(s, t) f...  27.2 us
    all_to_all x1, starting transfers between devices, body(): lax.all_to_all(packed, 'expert', split_axis=0, concat_axis=0, tiled=True)  10.6 us
    all_to_all x1, starting transfers between devices, body(): lax.all_to_all(back, 'expert', split_axis=0, concat_axis=0, tiled=True)  9.39 us
    all_to_all x1, waiting for transfers between devices, body(): lax.all_to_all(back, 'expert', split_axis=0, concat_axis=0, tiled=True)  8.33 us
    all_to_all x1, starting transfers between devices, body(): lax.all_to_all(column, 'expert', split_axis=0, concat_axis=0, tiled=True)  6.21 us
    reduce_scatter x1, waiting for transfers between devices, body(): mine = lax.psum_scatter(part, 'dp', scatter_dimension=0, tiled=True)  5.22 us
  transfers between devices with their start and end apart: 4, of which 3 were waited for; matrix products, arithmetic and copies ran while one was open for 1% of the time, Pallas kernels for 8%

profile of v10, /device:TPU:6, one launch (start us, length us, event | category | flops | bytes accessed | tf_op | source)
XLA Modules:
  0.0 171.9 jit_solution(1641288272257895947)
XLA Ops:
  7.2 5.3 %shard_map.85 = bf16[768,2816]{1,0:T(8,128)(2,1)} custom-call(s32[8,128]{1,0:T(8,128)} %bitcast.27, f32[8,128]{1,0:T(8,128)} %bitcast.29, bf16[128,1024]{1,0:T(8,128)(2,1)} %tokens_hbm.1, bf16[1024,384]{1,0:T(8,128)(2,1)} %bitcast.33), custom_call_target="tpu_custom_call" | custom-call | flops 1610612736 | bytes 4325376 | tf_op jit(solution)/shard_map/pallas_call | solution.py:231
  12.4 0.0 copy-start.1
  12.4 10.6 %all-to-all-start = ((bf16[32,24,2816]{2,1,0:T(8,128)(2,1)}), bf16[32,24,2816]{2,1,0:T(8,128)(2,1)}, u32[]{:S(2)}, u32[]{:S(2)}) async-start(bf16[32,24,2816]{2,1,0:T(8,128)(2,1)} %bitcast.23), calls=%async_computation | async-start | bytes 8650752 | tf_op jit(solution)/shard_map/all_to_all | solution.py:274
  23.0 0.0 copy-start.2
  23.0 0.0 reduce-scatter.2.cloned.1.call-start
  23.1 0.0 copy-done.1
  23.1 0.2 shard_map.86
  23.3 55.8 %all-gather.1 = f16[1024,1664]{1,0:T(8,128)(2,1)S(1)} all-gather(f16[64,1664]{1,0:T(8,128)(2,1)S(1)} %convert_element_type.12), channel_id=1, replica_groups=mesh['dp'=16,'expert'=32] {'dp'}, dimensions={0}, use_global_device_ids=true | all-gather | bytes 3620864 | tf_op jit(solution)/shard_map/all_gather | solution.py:284
  79.1 0.2 convert_reduce_fusion
  79.3 0.0 copy-done.2
  79.3 0.2 select_reduce_fusion
  79.5 0.8 multiply_convert_fusion
  80.3 0.0 all-to-all-done
  80.3 8.1 %shard_map.90 = bf16[1024,1536]{1,0:T(8,128)(2,1)} custom-call(bf16[768,2816]{1,0:T(8,128)(2,1)} %bitcast.4.got_hbm, bf16[1024,1536]{1,0:T(8,128)(2,1)S(1)} %bitcast.17), custom_call_target="tpu_custom_call" | custom-call | flops 4831838208 | bytes 9437184 | tf_op jit(solution)/shard_map/pallas_call | solution.py:231
  88.4 0.0 reduce-scatter.2.cloned.1.call-update
  88.4 8.6 %shard_map.87 = bf16[768,2048]{1,0:T(8,128)(2,1)} custom-call(bf16[768,2816]{1,0:T(8,128)(2,1)} %bitcast.4.got_hbm, bf16[1024,1536]{1,0:T(8,128)(2,1)S(1)} %bitcast.18), custom_call_target="tpu_custom_call" | custom-call | flops 4831838208 | bytes 9437184 | tf_op jit(solution)/shard_map/pallas_call | solution.py:231
  97.1 9.4 %all-to-all-start.1 = ((bf16[32,24,2048]{2,1,0:T(8,128)(2,1)}), bf16[32,24,2048]{2,1,0:T(8,128)(2,1)S(1)}, u32[]{:S(2)}, u32[]{:S(2)}) async-start(bf16[32,24,2048]{2,1,0:T(8,128)(2,1)} %bitcast.7), calls=%async_computation.1 | async-start | bytes 6291456 | tf_op jit(solution)/shard_map/all_to_all | solution.py:323
  106.5 1.7 shard_map.88
  108.2 28.2 %psum.7 = f32[1,128]{1,0:T(1,128)S(1)} all-reduce(f32[1,128]{1,0:T(1,128)} %get-tuple-element.13), channel_id=1, replica_groups=mesh['dp'=16,'expert'=32] {'dp'}, use_global_device_ids=true, to_apply=%region_3.4 | all-reduce | flops 128 | bytes 1024 | tf_op jit(solution)/shard_map/psum | solution.py:332
  136.4 0.1 reshape_squeeze.3
  136.5 0.1 copy.13
  136.6 0.1 broadcast_in_dim.24
  136.7 8.3 %all-to-all-done.1 = bf16[32,24,2048]{2,1,0:T(8,128)(2,1)S(1)} async-done(((bf16[32,24,2048]{2,1,0:T(8,128)(2,1)}), bf16[32,24,2048]{2,1,0:T(8,128)(2,1)S(1)}, u32[]{:S(2)}, u32[]{:S(2)}) %all-to-all-start.1) | async-done | bytes 3145760 | tf_op jit(solution)/shard_map/all_to_all | solution.py:323
  145.0 0.7 all_to_all.26
  145.7 6.2 %all-to-all-start.2 = ((f32[32,1,256]{2,1,0:T(1,128)}), f32[32,1,256]{2,1,0:T(1,128)S(1)}, u32[]{:S(2)}, u32[]{:S(2)}) async-start(f32[32,1,256]{2,1,0:T(1,128)} %all_to_all.26), calls=%async_computation.3 | async-start | bytes 65536 | tf_op jit(solution)/shard_map/all_to_all | solution.py:335
  151.9 0.0 copy-done
  151.9 3.4 %shard_map.89 = bf16[128,1024]{1,0:T(8,128)(2,1)} custom-call(bf16[1536,128]{1,0:T(8,128)(2,1)} %get-tuple-element.12.picks_ref, bf16[768,2048]{1,0:T(8,128)(2,1)} %bitcast.22), custom_call_target="tpu_custom_call" | custom-call | flops 402653184 | bytes 3145728 | tf_op jit(solution)/shard_map/pallas_call | solution.py:231
  155.3 2.1 %all-to-all-done.2 = f32[32,1,256]{2,1,0:T(1,128)S(1)} async-done(((f32[32,1,256]{2,1,0:T(1,128)}), f32[32,1,256]{2,1,0:T(1,128)S(1)}, u32[]{:S(2)}, u32[]{:S(2)}) %all-to-all-start.2) | async-done | bytes 32800 | tf_op jit(solution)/shard_map/all_to_all | solution.py:335
  157.4 0.1 reduce_sum.19
  157.5 0.6 multiply_reduce_fusion
  158.1 5.2 %reduce-scatter.2.cloned.1.call-done = bf16[64,1536]{1,0:T(8,128)(2,1)} async-done(((bf16[1024,1536]{1,0:T(8,128)(2,1)}), bf16[64,1536]{1,0:T(8,128)(2,1)}) %reduce-scatter.2.cloned.1.call-update) | async-done | bytes 196624 | tf_op jit(solution)/shard_map/reduce_scatter | solution.py:304
  163.4 1.7 reshape.43
  (5 shorter events, 0.1 us)
Async XLA Ops:
  12.4 10.7 %copy-start.1 = (bf16[64,2,768]{2,1,0:T(2,128)(2,1)S(1)}, bf16[64,2,768]{2,1,0:T(2,128)(2,1)}, u32[]{:S(2)}) copy-start(bf16[64,2,768]{2,1,0:T(2,128)(2,1)} %param.10) | copy-start | bytes 589828
  12.4 67.9 %all-to-all-start = ((bf16[32,24,2816]{2,1,0:T(8,128)(2,1)}), bf16[32,24,2816]{2,1,0:T(8,128)(2,1)}, u32[]{:S(2)}, u32[]{:S(2)}) async-start(bf16[32,24,2816]{2,1,0:T(8,128)(2,1)} %bitcast.23), calls=%async_computation | async-start | bytes 8650752 | tf_op jit(solution)/shard_map/all_to_all | solution.py:274
  23.0 56.3 %copy-start.2 = (f32[11]{0:T(128)S(1)}, f32[11]{0:T(128)}, u32[]{:S(2)}) copy-start(f32[11]{0:T(128)} %constant.8.clone) | copy-start | bytes 136
  23.0 140.3 %reduce-scatter.2.cloned.1.call-start = ((), (), s32[]{:S(2)}) async-start(), calls=%async_computation.4 | async-start | bytes 3342336 | tf_op jit(solution)/shard_map/reduce_scatter | solution.py:304
  97.1 47.9 %all-to-all-start.1 = ((bf16[32,24,2048]{2,1,0:T(8,128)(2,1)}), bf16[32,24,2048]{2,1,0:T(8,128)(2,1)S(1)}, u32[]{:S(2)}, u32[]{:S(2)}) async-start(bf16[32,24,2048]{2,1,0:T(8,128)(2,1)} %bitcast.7), calls=%async_computation.1 | async-start | bytes 6291456 | tf_op jit(solution)/shard_map/all_to_all | solution.py:323
  145.0 6.9 %copy-start = (bf16[32,24,2048]{2,1,0:T(8,128)(2,1)}, bf16[32,24,2048]{2,1,0:T(8,128)(2,1)S(1)}, u32[]{:S(2)}) copy-start(bf16[32,24,2048]{2,1,0:T(8,128)(2,1)S(1)} %all-to-all-done.1) | copy-start | bytes 9437188
  145.7 11.8 %all-to-all-start.2 = ((f32[32,1,256]{2,1,0:T(1,128)}), f32[32,1,256]{2,1,0:T(1,128)S(1)}, u32[]{:S(2)}, u32[]{:S(2)}) async-start(f32[32,1,256]{2,1,0:T(1,128)} %all_to_all.26), calls=%async_computation.3 | async-start | bytes 65536 | tf_op jit(solution)/shard_map/all_to_all | solution.py:335
Sparse Core Ops, SparseCore 0:
  88.6 74.7 reduce-scatter.1

commit v11 on v9

--- a/solution.py
+++ b/solution.py
@@ -91,8 +91,9 @@
             out_ref[i : i + step, j * model : (j + 1) * model] = rows.astype(BF16)
         send(i, 0, first)
         for j in range(per_device):
-            hit = slot == iota((step, 1), 0) + (j * size + i)
-            rows = dot(hit.astype(F32).astype(BF16), scaled_ref[...])
+            near = jnp.clip(slot - (j * size + i), -1, step).astype(F32).astype(BF16)
+            hit = jnp.where(near == iota((step, 1), 0).astype(F32).astype(BF16), jnp.bfloat16(1), jnp.bfloat16(0))
+            rows = dot(hit, scaled_ref[...])
             out_ref[i : i + step, first + j * width : first + (j + 1) * width] = rows.astype(BF16)
         send(i, first, per_device * width)
     for copy in outs:

time: 173 us -> 173 us (level)
  no operation moved by 1% of the time
where the time goes in v11:
time: 173 us; the launch traced here: 172 us
  blocking collectives  83.9 us (48%)
  Pallas kernels  27 us (16%)
  starting transfers between devices  26.3 us (15%)
  waiting for transfers between devices  16 us (9%)
  between operations  14.2 us (8%)
  local copies, waits for them, and re-layouts  2.68 us (2%)
  other arithmetic  1.91 us (1%)
    all_gather x1, blocking collectives, body(): full = from_half(lax.all_gather(sent, 'dp', axis=0, tiled=True), data_ways)  55.7 us
    psum x1, blocking collectives, body(): column = lax.psum(sums, 'dp')[0, :experts].reshape(per_device, devices).T  28.2 us
    pallas_call x6, Pallas kernels, call(): pl.pallas_call(kernel, grid=grid, out_shape=[jax.ShapeDtypeStruct(s, t) f...  27 us
    all_to_all x1, starting transfers between devices, body(): lax.all_to_all(packed, 'expert', split_axis=0, concat_axis=0, tiled=True)  10.6 us
    all_to_all x1, starting transfers between devices, body(): lax.all_to_all(back, 'expert', split_axis=0, concat_axis=0, tiled=True)  9.45 us
    all_to_all x1, waiting for transfers between devices, body(): lax.all_to_all(back, 'expert', split_axis=0, concat_axis=0, tiled=True)  8.33 us
    all_to_all x1, starting transfers between devices, body(): lax.all_to_all(column, 'expert', split_axis=0, concat_axis=0, tiled=True)  6.21 us
    reduce_scatter x1, waiting for transfers between devices, body(): mine = lax.psum_scatter(part, 'dp', scatter_dimension=0, tiled=True)  5.51 us
  transfers between devices with their start and end apart: 4, of which 3 were waited for; matrix products, arithmetic and copies ran while one was open for 1% of the time, Pallas kernels for 8%

profile of v11, /device:TPU:6, one launch (start us, length us, event | category | flops | bytes accessed | tf_op | source)
XLA Modules:
  0.0 172.0 jit_solution(12667835008243174046)
XLA Ops:
  7.2 5.1 %shard_map.85 = bf16[768,2816]{1,0:T(8,128)(2,1)} custom-call(s32[8,128]{1,0:T(8,128)} %bitcast.27, f32[8,128]{1,0:T(8,128)} %bitcast.29, bf16[128,1024]{1,0:T(8,128)(2,1)} %tokens_hbm.1, bf16[1024,384]{1,0:T(8,128)(2,1)} %bitcast.33), custom_call_target="tpu_custom_call" | custom-call | flops 1610612736 | bytes 4325376 | tf_op jit(solution)/shard_map/pallas_call | solution.py:230
  12.3 0.0 copy-start.1
  12.3 10.6 %all-to-all-start = ((bf16[32,24,2816]{2,1,0:T(8,128)(2,1)}), bf16[32,24,2816]{2,1,0:T(8,128)(2,1)}, u32[]{:S(2)}, u32[]{:S(2)}) async-start(bf16[32,24,2816]{2,1,0:T(8,128)(2,1)} %bitcast.23), calls=%async_computation | async-start | bytes 8650752 | tf_op jit(solution)/shard_map/all_to_all | solution.py:273
  22.9 0.0 copy-start.2
  22.9 0.0 reduce-scatter.2.cloned.1.call-start
  22.9 0.0 copy-done.1
  23.0 0.2 shard_map.86
  23.2 55.7 %all-gather.1 = f16[1024,1664]{1,0:T(8,128)(2,1)S(1)} all-gather(f16[64,1664]{1,0:T(8,128)(2,1)S(1)} %convert_element_type.12), channel_id=1, replica_groups=mesh['dp'=16,'expert'=32] {'dp'}, dimensions={0}, use_global_device_ids=true | all-gather | bytes 3620864 | tf_op jit(solution)/shard_map/all_gather | solution.py:283
  78.9 0.2 convert_reduce_fusion
  79.1 0.0 copy-done.2
  79.1 0.2 select_reduce_fusion
  79.3 0.8 multiply_convert_fusion
  80.1 0.0 all-to-all-done
  80.1 8.1 %shard_map.90 = bf16[1024,1536]{1,0:T(8,128)(2,1)} custom-call(bf16[768,2816]{1,0:T(8,128)(2,1)} %bitcast.4.got_hbm, bf16[1024,1536]{1,0:T(8,128)(2,1)S(1)} %bitcast.17), custom_call_target="tpu_custom_call" | custom-call | flops 4831838208 | bytes 9437184 | tf_op jit(solution)/shard_map/pallas_call | solution.py:230
  88.2 0.0 reduce-scatter.2.cloned.1.call-update
  88.3 8.6 %shard_map.87 = bf16[768,2048]{1,0:T(8,128)(2,1)} custom-call(bf16[768,2816]{1,0:T(8,128)(2,1)} %bitcast.4.got_hbm, bf16[1024,1536]{1,0:T(8,128)(2,1)S(1)} %bitcast.18), custom_call_target="tpu_custom_call" | custom-call | flops 4831838208 | bytes 9437184 | tf_op jit(solution)/shard_map/pallas_call | solution.py:230
  96.9 9.5 %all-to-all-start.1 = ((bf16[32,24,2048]{2,1,0:T(8,128)(2,1)}), bf16[32,24,2048]{2,1,0:T(8,128)(2,1)S(1)}, u32[]{:S(2)}, u32[]{:S(2)}) async-start(bf16[32,24,2048]{2,1,0:T(8,128)(2,1)} %bitcast.7), calls=%async_computation.1 | async-start | bytes 6291456 | tf_op jit(solution)/shard_map/all_to_all | solution.py:322
  106.3 1.7 shard_map.88
  108.0 28.2 %psum.7 = f32[1,128]{1,0:T(1,128)S(1)} all-reduce(f32[1,128]{1,0:T(1,128)} %get-tuple-element.13), channel_id=1, replica_groups=mesh['dp'=16,'expert'=32] {'dp'}, use_global_device_ids=true, to_apply=%region_3.4 | all-reduce | flops 128 | bytes 1024 | tf_op jit(solution)/shard_map/psum | solution.py:331
  136.2 0.1 reshape_squeeze.3
  136.3 0.1 copy.13
  136.4 0.1 broadcast_in_dim.24
  136.5 8.3 %all-to-all-done.1 = bf16[32,24,2048]{2,1,0:T(8,128)(2,1)S(1)} async-done(((bf16[32,24,2048]{2,1,0:T(8,128)(2,1)}), bf16[32,24,2048]{2,1,0:T(8,128)(2,1)S(1)}, u32[]{:S(2)}, u32[]{:S(2)}) %all-to-all-start.1) | async-done | bytes 3145760 | tf_op jit(solution)/shard_map/all_to_all | solution.py:322
  144.9 0.7 all_to_all.26
  145.6 6.2 %all-to-all-start.2 = ((f32[32,1,256]{2,1,0:T(1,128)}), f32[32,1,256]{2,1,0:T(1,128)S(1)}, u32[]{:S(2)}, u32[]{:S(2)}) async-start(f32[32,1,256]{2,1,0:T(1,128)} %all_to_all.26), calls=%async_computation.3 | async-start | bytes 65536 | tf_op jit(solution)/shard_map/all_to_all | solution.py:334
  151.8 0.0 copy-done
  151.8 3.4 %shard_map.89 = bf16[128,1024]{1,0:T(8,128)(2,1)} custom-call(bf16[1536,128]{1,0:T(8,128)(2,1)} %get-tuple-element.12.picks_ref, bf16[768,2048]{1,0:T(8,128)(2,1)} %bitcast.22), custom_call_target="tpu_custom_call" | custom-call | flops 402653184 | bytes 3145728 | tf_op jit(solution)/shard_map/pallas_call | solution.py:230
  155.2 2.2 %all-to-all-done.2 = f32[32,1,256]{2,1,0:T(1,128)S(1)} async-done(((f32[32,1,256]{2,1,0:T(1,128)}), f32[32,1,256]{2,1,0:T(1,128)S(1)}, u32[]{:S(2)}, u32[]{:S(2)}) %all-to-all-start.2) | async-done | bytes 32800 | tf_op jit(solution)/shard_map/all_to_all | solution.py:334
  157.3 0.1 reduce_sum.19
  157.4 0.6 multiply_reduce_fusion
  158.0 5.5 %reduce-scatter.2.cloned.1.call-done = bf16[64,1536]{1,0:T(8,128)(2,1)} async-done(((bf16[1024,1536]{1,0:T(8,128)(2,1)}), bf16[64,1536]{1,0:T(8,128)(2,1)}) %reduce-scatter.2.cloned.1.call-update) | async-done | bytes 196624 | tf_op jit(solution)/shard_map/reduce_scatter | solution.py:303
  163.5 1.7 reshape.43
  (5 shorter events, 0.1 us)
Async XLA Ops:
  12.3 10.7 %copy-start.1 = (bf16[64,2,768]{2,1,0:T(2,128)(2,1)S(1)}, bf16[64,2,768]{2,1,0:T(2,128)(2,1)}, u32[]{:S(2)}) copy-start(bf16[64,2,768]{2,1,0:T(2,128)(2,1)} %param.10) | copy-start | bytes 589828
  12.3 67.8 %all-to-all-start = ((bf16[32,24,2816]{2,1,0:T(8,128)(2,1)}), bf16[32,24,2816]{2,1,0:T(8,128)(2,1)}, u32[]{:S(2)}, u32[]{:S(2)}) async-start(bf16[32,24,2816]{2,1,0:T(8,128)(2,1)} %bitcast.23), calls=%async_computation | async-start | bytes 8650752 | tf_op jit(solution)/shard_map/all_to_all | solution.py:273
  22.9 56.2 %copy-start.2 = (f32[11]{0:T(128)S(1)}, f32[11]{0:T(128)}, u32[]{:S(2)}) copy-start(f32[11]{0:T(128)} %constant.8.clone) | copy-start | bytes 136
  22.9 140.6 %reduce-scatter.2.cloned.1.call-start = ((), (), s32[]{:S(2)}) async-start(), calls=%async_computation.4 | async-start | bytes 3342336 | tf_op jit(solution)/shard_map/reduce_scatter | solution.py:303
  96.9 48.0 %all-to-all-start.1 = ((bf16[32,24,2048]{2,1,0:T(8,128)(2,1)}), bf16[32,24,2048]{2,1,0:T(8,128)(2,1)S(1)}, u32[]{:S(2)}, u32[]{:S(2)}) async-start(bf16[32,24,2048]{2,1,0:T(8,128)(2,1)} %bitcast.7), calls=%async_computation.1 | async-start | bytes 6291456 | tf_op jit(solution)/shard_map/all_to_all | solution.py:322
  144.9 6.9 %copy-start = (bf16[32,24,2048]{2,1,0:T(8,128)(2,1)}, bf16[32,24,2048]{2,1,0:T(8,128)(2,1)S(1)}, u32[]{:S(2)}) copy-start(bf16[32,24,2048]{2,1,0:T(8,128)(2,1)S(1)} %all-to-all-done.1) | copy-start | bytes 9437188
  145.6 11.8 %all-to-all-start.2 = ((f32[32,1,256]{2,1,0:T(1,128)}), f32[32,1,256]{2,1,0:T(1,128)S(1)}, u32[]{:S(2)}, u32[]{:S(2)}) async-start(f32[32,1,256]{2,1,0:T(1,128)} %all_to_all.26), calls=%async_computation.3 | async-start | bytes 65536 | tf_op jit(solution)/shard_map/all_to_all | solution.py:334
Sparse Core Ops, SparseCore 0:
  88.4 75.0 reduce-scatter.1
